TPU v7x, 32 devices: a whole 2x2x4 slice. The times are simulated.
32 devices in a mesh: dp: 2 (over y), fsdp: 16 (over z, x, core).
Axes of the slice: x: 2, y: 2, z: 4, core: 2. Of those that a mesh axis runs over, the one named last changes fastest.
Arguments:
- acts: bfloat16 [14336, 7168], P(('dp', 'fsdp')), may hold values from -6 to 6
- upstream: bfloat16 [14336, 512], P(('dp', 'fsdp')), may hold values from -1.25 to 1.25
- k_weight: bfloat16 [7168, 512], P('fsdp'), may hold values from -0.0625 to 0.0625
- probe: bfloat16 [7168, 512], P('fsdp'), may hold values from -5 to 5
- norm_gain: float32 [128], replicated, may hold values from 0.1 to 1.9
- momentum: float32 [7168, 512], P('fsdp', 'dp'), may hold values from -4 to 4
- curvature: float32 [7168, 512], P('fsdp', 'dp'), may hold values from 0.3 to 3
Outputs:
- new_momentum: float32 [7168, 512], P('fsdp', 'dp')
- new_curvature: float32 [7168, 512], P('fsdp', 'dp')
- update: float32 [7168, 512], P('fsdp', 'dp')
All inputs are finite; a program needn't handle non-finite values.
Results may differ from a plain program's by a relative error of at most 0.024.
Values may be sent and summed in bfloat16 or wider, within the bound.
No kernel may reach another device: no remote copies, remote signals or barrier semaphores. Data moves between devices by JAX's collectives and lax.ppermute only.
A program may use at most 128 MiB of HBM per device.

v0:
```python
import jax
import jax.numpy as jnp
from jax import lax
from jax.sharding import PartitionSpec as P


def head_terms(projected, tangent, upstream, norm_gain):
    token_count = projected.shape[0]
    head_size = norm_gain.shape[0]
    head_count = projected.shape[1] // head_size
    shaped = (token_count, head_count, head_size)
    values = projected.reshape(shaped)
    moving = tangent.reshape(shaped)
    weighted = upstream.astype(jnp.float32).reshape(shaped) * norm_gain
    inverse = lax.rsqrt(jnp.mean(values * values, axis=-1, keepdims=True) + 1e-06)
    cubed = inverse * inverse * inverse
    along = jnp.sum(weighted * values, axis=-1, keepdims=True)
    grad_vals = inverse * weighted - cubed * values * along / head_size
    inverse_dot = -cubed * jnp.sum(values * moving, axis=-1, keepdims=True) / head_size
    along_dot = jnp.sum(weighted * moving, axis=-1, keepdims=True)
    hvp_vals = (
        inverse_dot * weighted
        - (
            3.0 * inverse * inverse * inverse_dot * values * along
            + cubed * moving * along
            + cubed * values * along_dot
        )
        / head_size
    )
    return (grad_vals.reshape(token_count, -1), hvp_vals.reshape(token_count, -1))


def contract_tokens(left, right):
    return lax.dot_general(
        left, right, (((0,), (0,)), ((), ())), preferred_element_type=jnp.float32
    )


def on_device(acts, upstream, k_weight, probe, norm_gain, momentum, curvature):
    width = k_weight.shape[1]
    weight_piece = lax.all_gather(k_weight, "fsdp", axis=0, tiled=True)
    probe_piece = lax.all_gather(probe, "fsdp", axis=0, tiled=True)
    projected = jnp.dot(acts, weight_piece, preferred_element_type=jnp.float32)
    tangent = jnp.dot(acts, probe_piece, preferred_element_type=jnp.float32)
    grad_vals, hvp_vals = head_terms(projected, tangent, upstream, norm_gain)
    stacked = jnp.concatenate([grad_vals, hvp_vals], axis=1).astype(jnp.bfloat16)
    owned = lax.psum_scatter(
        contract_tokens(acts, stacked).astype(jnp.bfloat16), "fsdp", scatter_dimension=0, tiled=True
    ).astype(jnp.float32)
    grad_owned = owned[:, :width]
    hvp_owned = owned[:, width:]
    grad_share, hvp_share = (
        lax.psum_scatter(grad_owned, "dp", scatter_dimension=1, tiled=True),
        lax.psum_scatter(hvp_owned, "dp", scatter_dimension=1, tiled=True),
    )
    share_width = grad_share.shape[1]
    probe_cols = lax.dynamic_slice_in_dim(
        probe, lax.axis_index("dp") * share_width, share_width, 1
    ).astype(jnp.float32)
    new_momentum = 0.965 * momentum + 0.035 * grad_share
    new_curvature = 0.99 * curvature + 0.01 * (probe_cols * hvp_share)
    update = jnp.clip(new_momentum / jnp.maximum(0.5 * new_curvature, 0.25), -1.0, 1.0)
    return (new_momentum, new_curvature, update)


def solution(mesh):
    return jax.shard_map(
        on_device,
        mesh=mesh,
        in_specs=(
            P(("dp", "fsdp"), None),
            P(("dp", "fsdp"), None),
            P("fsdp", None),
            P("fsdp", None),
            P(),
            P("fsdp", "dp"),
            P("fsdp", "dp"),
        ),
        out_specs=(P("fsdp", "dp"), P("fsdp", "dp"), P("fsdp", "dp")),
        check_vma=False,
    )
```

profile of v0, /device:TPU:11, one launch (start us, length us, event | category | flops | bytes accessed | tf_op | source)
XLA Modules:
  0.0 411.4 jit_solution(14416804661122462800)
XLA Ops:
  7.2 0.0 all-gather.3.cloned.1.call-start
  7.2 0.7 all-gather.3.cloned.1.call-update
  7.9 0.0 all-gather.5.cloned.1.call-start
  7.9 0.7 all-gather.5.cloned.1.call-update
  8.6 0.0 reduce-scatter.10.cloned.1.call-start
  8.7 1.3 reshape.67
  10.0 0.7 broadcast_bitcast_fusion
  10.7 68.3 %all-gather.3.cloned.1.call-done = bf16[7168,512]{1,0:T(8,128)(2,1)} async-done(((bf16[448,512]{1,0:T(8,128)(2,1)}), bf16[7168,512]{1,0:T(8,128)(2,1)}) %all-gather.3.cloned.1.call-update) | async-done | bytes 7340048 | tf_op jit(solution)/shard_map/all_gather | solution.py:41
  79.0 7.7 %fusion.23 = f32[448,512]{1,0:T(8,128)S(1)} fusion(bf16[448,7168]{1,0:T(8,128)(2,1)} %param.7, bf16[7168,512]{1,0:T(8,128)(2,1)} %all-gather.3.cloned.1.call-done), kind=kOutput, calls=%fused_computation.44 | convolution fusion | flops 3288334336 | bytes 14680064 | tf_op jit(solution)/shard_map/dot_general | solution.py:43
  86.7 0.3 reshape.66
  87.0 0.0 copy-start.8
  87.0 61.0 %all-gather.5.cloned.1.call-done = bf16[7168,512]{1,0:T(8,128)(2,1)} async-done(((bf16[448,512]{1,0:T(8,128)(2,1)}), bf16[7168,512]{1,0:T(8,128)(2,1)}) %all-gather.5.cloned.1.call-update) | async-done | bytes 7340048 | tf_op jit(solution)/shard_map/all_gather | solution.py:42
  148.0 9.4 %fusion.24 = f32[448,512]{1,0:T(8,128)} fusion(bf16[448,7168]{1,0:T(8,128)(2,1)} %param.7, bf16[7168,512]{1,0:T(8,128)(2,1)} %all-gather.5.cloned.1.call-done), kind=kOutput, calls=%fused_computation.45 | convolution fusion | flops 3288334336 | bytes 14680064 | tf_op jit(solution)/shard_map/dot_general | solution.py:44
  157.3 1.5 reshape.68
  158.8 1.6 multiply_reduce_fusion.3
  160.5 1.5 fusion
  162.0 1.5 fusion.1
  163.5 1.2 copy.33
  164.6 0.1 copy.36
  164.8 0.1 copy.38
  164.9 0.8 copy.34
  165.8 0.8 copy.35
  166.6 0.8 copy.37
  167.4 0.5 mul.254
  168.0 1.7 mul.227
  169.7 1.5 mul.236
  171.2 1.5 mul.247
  172.7 0.0 slice-start.1
  172.7 2.3 fusion.10
  175.1 11.3 %convert_bitcast_fusion = bf16[7168,1024]{0,1:T(8,128)(2,1)} fusion(bf16[448,7168]{1,0:T(8,128)(2,1)S(1)} %bitcast.67, bf16[448,512]{1,0:T(8,128)(2,1)S(1)} %get-tuple-element.21, bf16[448,512]{1,0:T(8,128)(2,1)S(1)} %get-tuple-element.20), kind=kOutput, calls=%fused_computation.2 | convolution fusion | flops 6585843712 | bytes 22020096 | tf_op jit(solution)/shard_map/dot_general | solution.py:34
  186.4 19.9 %copy.44 = bf16[7168,1024]{1,0:T(8,128)(2,1)} copy(bf16[7168,1024]{0,1:T(8,128)(2,1)} %convert_bitcast_fusion) | data formatting | bytes 29360128
  206.3 0.0 reduce-scatter.10.cloned.1.call-update
  206.3 0.0 reduce-scatter.6.cloned.1.call-start
  206.4 147.8 %reduce-scatter.10.cloned.1.call-done = bf16[448,1024]{1,0:T(8,128)(2,1)} async-done(((bf16[7168,1024]{1,0:T(8,128)(2,1)}), bf16[448,1024]{1,0:T(8,128)(2,1)}) %reduce-scatter.10.cloned.1.call-update) | async-done | bytes 917520
  354.2 1.5 copy.45
  355.6 1.6 fusion.22
  357.3 0.0 reduce-scatter.6.cloned.1.call-update
  357.3 0.0 reduce-scatter.8.cloned.1.call-start
  357.3 0.5 reduce-scatter.8.cloned.1.call-update
  357.9 0.1 copy.46
  358.1 0.2 copy.32
  358.3 0.2 copy.39
  358.5 19.5 %reduce-scatter.6.cloned.1.call-done = f32[448,256]{0,1:T(8,128)} async-done(((f32[448,512]{0,1:T(8,128)}), f32[448,256]{0,1:T(8,128)}) %reduce-scatter.6.cloned.1.call-update) | async-done | bytes 458768 | tf_op jit(solution)/shard_map/reduce_scatter | solution.py:53
  378.0 22.5 %reduce-scatter.8.cloned.1.call-done = f32[448,256]{0,1:T(8,128)} async-done(((f32[448,512]{0,1:T(8,128)}), f32[448,256]{0,1:T(8,128)}) %reduce-scatter.8.cloned.1.call-update) | async-done | bytes 458768 | tf_op jit(solution)/shard_map/reduce_scatter | solution.py:54
  400.5 1.5 divide_clamp_fusion
  402.0 1.0 copy.41
  403.0 1.0 copy.42
  403.9 1.0 copy.43
  (23 shorter events, 0.1 us)
Async XLA Ops:
  7.2 71.8 %all-gather.3.cloned.1.call-start = ((), (), s32[]{:S(2)}) async-start(), calls=%async_computation.3 | async-start | bytes 7798784 | tf_op jit(solution)/shard_map/all_gather | solution.py:41
  7.9 140.1 %all-gather.5.cloned.1.call-start = ((), (), s32[]{:S(2)}) async-start(), calls=%async_computation.4 | async-start | bytes 7798784 | tf_op jit(solution)/shard_map/all_gather | solution.py:42
  8.6 345.5 %reduce-scatter.10.cloned.1.call-start = ((), (), s32[]{:S(2)}) async-start(), calls=%async_computation.7 | async-start | bytes 15597568
  86.7 61.3 %copy-start = (f32[448,512]{1,0:T(8,128)}, f32[448,512]{1,0:T(8,128)S(1)}, u32[]{:S(2)}) copy-start(f32[448,512]{1,0:T(8,128)S(1)} %fusion.23) | copy-start | bytes 2752516
  87.0 73.5 %copy-start.8 = (f32[128]{0:T(128)S(1)}, f32[128]{0:T(128)}, u32[]{:S(2)}) copy-start(f32[128]{0:T(128)} %param.11) | copy-start | bytes 1540
  158.8 13.9 %copy-start.4 = (bf16[448,512]{1,0:T(8,128)(2,1)S(1)}, bf16[448,512]{1,0:T(8,128)(2,1)}, u32[]{:S(2)}) copy-start(bf16[448,512]{1,0:T(8,128)(2,1)} %param.8) | copy-start | bytes 1376260
  162.0 10.7 %copy-start.1 = (f32[448,512]{1,0:T(8,128)S(1)}, f32[448,512]{1,0:T(8,128)}, u32[]{:S(2)}) copy-start(f32[448,512]{1,0:T(8,128)} %copy-done) | copy-start | bytes 2752516
  163.5 9.2 %copy-start.2 = (f32[448,512]{1,0:T(8,128)S(1)}, f32[448,512]{1,0:T(8,128)}, u32[]{:S(2)}) copy-start(f32[448,512]{1,0:T(8,128)} %fusion.24) | copy-start | bytes 2752516
  163.5 9.3 %copy-start.3 = (f32[448,4,128]{2,1,0:T(4,128)S(1)}, f32[448,4,128]{2,1,0:T(4,128)}, u32[]{:S(2)}) copy-start(f32[448,4,128]{2,1,0:T(4,128)} %fusion) | copy-start | bytes 2752516
  167.4 7.6 %slice-start = ((s8[6422528]{0:T(1024)(128)(4,1)}), s8[4194304]{0:T(1024)(128)(4,1)S(1)}, s32[]{:S(2)}) async-start(s8[6422528]{0:T(1024)(128)(4,1)} %bitcast.66), calls=%async_computation.8 | async-start | bytes 8388608
  172.7 2.3 slice-start.1
  206.3 151.6 %copy-start.5 = (bf16[448,512]{1,0:T(8,128)(2,1)S(1)}, bf16[448,512]{1,0:T(8,128)(2,1)}, u32[]{:S(2)}) copy-start(bf16[448,512]{1,0:T(8,128)(2,1)} %param.10) | copy-start | bytes 1376260
  206.3 151.7 %copy-start.6 = (f32[448,256]{1,0:T(8,128)S(1)}, f32[448,256]{1,0:T(8,128)}, u32[]{:S(2)}) copy-start(f32[448,256]{1,0:T(8,128)} %param.12) | copy-start | bytes 1376260
  206.3 152.0 %copy-start.7 = (f32[448,256]{1,0:T(8,128)S(1)}, f32[448,256]{1,0:T(8,128)}, u32[]{:S(2)}) copy-start(f32[448,256]{1,0:T(8,128)} %param.13) | copy-start | bytes 1376260
  206.3 171.6 %reduce-scatter.6.cloned.1.call-start = ((), (), s32[]{:S(2)}) async-start(), calls=%async_computation.5 | async-start | bytes 1572864 | tf_op jit(solution)/shard_map/reduce_scatter | solution.py:53
  357.3 43.2 %reduce-scatter.8.cloned.1.call-start = ((), (), s32[]{:S(2)}) async-start(), calls=%async_computation.6 | async-start | bytes 1572864 | tf_op jit(solution)/shard_map/reduce_scatter | solution.py:54
Sparse Core Ops, SparseCore 0:
  10.3 68.6 all-gather.2
  81.2 66.6 all-gather.4
  206.4 147.6 reduce-scatter.9
  357.4 20.5 reduce-scatter.5
  380.2 20.3 reduce-scatter.7
where the time goes:
time: 414 us; the launch traced here: 411 us
  waiting for transfers between devices  321 us (78%)
  local copies, waits for them, and re-layouts  39.3 us (9%)
  matrix products  28.4 us (7%)
  between operations  14 us (3%)
  other arithmetic  8.46 us (2%)
    unnamed x6, waiting for transfers between devices  150 us
    all_gather x1, waiting for transfers between devices, on_device(): weight_piece = lax.all_gather(k_weight, 'fsdp', axis=0, tiled=True)  68.3 us
    all_gather x1, waiting for transfers between devices, on_device(): probe_piece = lax.all_gather(probe, 'fsdp', axis=0, tiled=True)  61 us
    unnamed x30, local copies, waits for them, and re-layouts  24.8 us
    reduce_scatter x1, waiting for transfers between devices, on_device(): lax.psum_scatter(hvp_owned, 'dp', scatter_dimension=1, tiled=True)  22.5 us
    reduce_scatter x1, waiting for transfers between devices, on_device(): lax.psum_scatter(grad_owned, 'dp', scatter_dimension=1, tiled=True)  19.5 us
    dot_general x1, matrix products, contract_tokens(): lax.dot_general(left, right, (((0,), (0,)), ((), ())), preferred_element_...  11.3 us
    dot_general x1, matrix products, on_device(): tangent = jnp.dot(acts, probe_piece, preferred_element_type=jnp.float32)  9.36 us
  transfers between devices with their start and end apart: 5, of which 5 were waited for; matrix products, arithmetic and copies ran while one was open for 3% of the time, Pallas kernels for 0%

commit v1 on v0

v1 whole, which is shorter than its diff:
```python
import functools

import jax
import jax.numpy as jnp
from jax import lax
from jax.sharding import PartitionSpec as P

AXES = ("dp", "fsdp")


def contract_tokens(left, right):
    return lax.dot_general(
        left, right, (((0,), (0,)), ((), ())), preferred_element_type=jnp.float32
    )


def head_terms(values, moving, weighted):
    head_size = values.shape[-1]
    inverse = lax.rsqrt(jnp.mean(values * values, axis=-1, keepdims=True) + 1e-06)
    cubed = inverse * inverse * inverse
    along = jnp.sum(weighted * values, axis=-1, keepdims=True)
    grad_vals = inverse * weighted - cubed * values * along / head_size
    inverse_dot = -cubed * jnp.sum(values * moving, axis=-1, keepdims=True) / head_size
    along_dot = jnp.sum(weighted * moving, axis=-1, keepdims=True)
    hvp_vals = (
        inverse_dot * weighted
        - (
            3.0 * inverse * inverse * inverse_dot * values * along
            + cubed * moving * along
            + cubed * values * along_dot
        )
        / head_size
    )
    return grad_vals, hvp_vals


def step_outputs(momentum, curvature, probe_cols, grad_share, hvp_share):
    new_momentum = 0.965 * momentum + 0.035 * grad_share
    new_curvature = 0.99 * curvature + 0.01 * (probe_cols * hvp_share)
    update = jnp.clip(new_momentum / jnp.maximum(0.5 * new_curvature, 0.25), -1.0, 1.0)
    return (new_momentum, new_curvature, update)


def by_collectives(acts, upstream, k_weight, probe, norm_gain, momentum, curvature):
    width = k_weight.shape[1]
    weight_piece = lax.all_gather(k_weight, "fsdp", axis=0, tiled=True)
    probe_piece = lax.all_gather(probe, "fsdp", axis=0, tiled=True)
    projected = jnp.dot(acts, weight_piece, preferred_element_type=jnp.float32)
    tangent = jnp.dot(acts, probe_piece, preferred_element_type=jnp.float32)
    shaped = (acts.shape[0], -1, norm_gain.shape[0])
    weighted = upstream.astype(jnp.float32).reshape(shaped) * norm_gain
    pair = head_terms(projected.reshape(shaped), tangent.reshape(shaped), weighted)
    stacked = jnp.concatenate([v.reshape(acts.shape[0], -1) for v in pair], axis=1)
    owned = lax.psum_scatter(
        contract_tokens(acts, stacked.astype(jnp.bfloat16)).astype(jnp.bfloat16),
        "fsdp",
        scatter_dimension=0,
        tiled=True,
    ).astype(jnp.float32)
    grad_share, hvp_share = (
        lax.psum_scatter(owned[:, :width], "dp", scatter_dimension=1, tiled=True),
        lax.psum_scatter(owned[:, width:], "dp", scatter_dimension=1, tiled=True),
    )
    share_width = grad_share.shape[1]
    probe_cols = lax.dynamic_slice_in_dim(
        probe, lax.axis_index("dp") * share_width, share_width, 1
    ).astype(jnp.float32)
    return step_outputs(momentum, curvature, probe_cols, grad_share, hvp_share)


def pairs_of(move):
    def flat(y, z, x, c):
        return ((y * 4 + z) * 2 + x) * 2 + c

    found = []
    for y in range(2):
        for z in range(4):
            for x in range(2):
                for c in range(2):
                    target = move(y, z, x, c)
                    if target is not None:
                        found.append((flat(y, z, x, c), flat(*target)))
    return found


def send(value, move):
    return lax.ppermute(value, AXES, pairs_of(move))


def to_core(y, z, x, c):
    return (y, z, x, 1 - c)


def to_x(y, z, x, c):
    return (y, z, 1 - x, c)


def to_y(y, z, x, c):
    return (1 - y, z, x, c)


def to_first(y, z, x, c):
    return to_x(y, z, x, c) if c == 0 else to_y(y, z, x, c)


def to_second(y, z, x, c):
    return to_y(y, z, x, c) if c == 0 else to_x(y, z, x, c)


def to_z(steps):
    return lambda y, z, x, c: (y, steps[z], x, c) if z in steps else None


Z_PAIR = to_z({0: 1, 1: 0, 2: 3, 3: 2})
Z_MIDDLE = to_z({1: 2, 2: 1})
Z_OUT = to_z({1: 0, 2: 3})
Z_IN = to_z({0: 1, 3: 2})


def by_links(acts, upstream, k_weight, probe, norm_gain, momentum, curvature):
    head = norm_gain.shape[0]
    rows = k_weight.shape[0]
    place = lax.axis_index("fsdp")
    y, z, x, c = lax.axis_index("dp"), place // 4, (place // 2) % 2, place % 2
    own_first = c == 0

    def column(value, number):
        return lax.dynamic_slice_in_dim(value, number * head, head, 1)

    def weights_for(core, side):
        return [column(k_weight, 2 * side + core), column(probe, 2 * side + core)]

    leaving = jnp.concatenate(weights_for(1 - c, y) + weights_for(1 - c, 1 - y), axis=1)
    staying = jnp.concatenate(weights_for(c, y) + weights_for(c, 1 - y), axis=1)
    coming = send(leaving, to_core)
    other_acts = send(acts, to_core)
    other_up = send(
        jnp.concatenate(
            [column(upstream, 2 * y + 1 - c), column(upstream, 2 * (1 - y) + 1 - c)], axis=1
        ),
        to_core,
    )
    chip_rows = jnp.where(
        own_first,
        jnp.concatenate([staying, coming], axis=0),
        jnp.concatenate([coming, staying], axis=0),
    )
    mine, beside = chip_rows[:, : 2 * head], chip_rows[:, 2 * head :]

    one = send(mine, Z_PAIR)
    near = send(mine, Z_MIDDLE)
    two = send(near, Z_OUT) + send(one, Z_MIDDLE)
    three = near + send(two, Z_OUT)

    across = send(mine, to_x)
    units = [(mine, across, beside, send(across, to_y))]
    for held in (one, two, three):
        first = send(held, to_first)
        units.append((held, first, send(held, to_second), send(first, to_second)))

    all_acts = jnp.concatenate([acts, other_acts], axis=0)

    def block_of(slot, flip_x):
        start = ((z ^ slot) * 2 + (x ^ flip_x)) * (2 * rows)
        return lax.dynamic_slice_in_dim(all_acts, start, 2 * rows, 1)

    def dot(left, right):
        return jnp.dot(left, right, preferred_element_type=jnp.float32)

    here = there = None
    for slot in range(4):
        own, first, second, both = units[slot]
        if slot == 0:
            flip_y, flip_x = second, first
        else:
            flip_x = jnp.where(own_first, first, second)
            flip_y = jnp.where(own_first, second, first)
        near_x, far_x = block_of(slot, 0), block_of(slot, 1)
        a = dot(near_x, own) + dot(far_x, flip_x)
        b = dot(near_x, flip_y) + dot(far_x, both)
        here = a if here is None else here + a
        there = b if there is None else there + b

    def stacked(projections, side, other):
        weighted = (
            jnp.concatenate([column(upstream, 2 * side + c), other], axis=0).astype(jnp.float32)
            * norm_gain
        )
        pair = head_terms(projections[:, :head], projections[:, head:], weighted)
        return jnp.concatenate(pair, axis=1).astype(jnp.bfloat16)

    right_here = stacked(here, y, other_up[:, :head])
    right_there = stacked(there, 1 - y, other_up[:, head:])
    right_first = jnp.where(own_first, right_here, right_there)
    right_second = jnp.where(own_first, right_there, right_here)

    def partial(slot, flip_x, right):
        return contract_tokens(block_of(slot, flip_x), right).astype(jnp.bfloat16)

    def plus(*terms):
        total = terms[0].astype(jnp.float32)
        for term in terms[1:]:
            total = total + term.astype(jnp.float32)
        return total.astype(jnp.bfloat16)

    def over_plane(slot):
        far = partial(slot, 1, right_there)
        second = partial(slot, c, right_second)
        first = partial(slot, 1 - c, right_first)
        own = partial(slot, 0, right_here)
        first = plus(first, send(far, to_second))
        return own, send(second, to_second), send(first, to_first)

    three = plus(*over_plane(3))
    two = plus(*over_plane(2), send(three, Z_IN))
    three = plus(three, send(two, Z_IN))
    one = plus(*over_plane(1), send(two, Z_MIDDLE))
    owned = over_plane(0) + (send(three, Z_MIDDLE), send(one, Z_PAIR))
    owned = functools.reduce(lambda s, t: s + t.astype(jnp.float32), owned, jnp.float32(0))

    kept = lax.dynamic_slice_in_dim(owned, c * rows, rows, 0)
    given = lax.dynamic_slice_in_dim(owned, (1 - c) * rows, rows, 0)
    taken = send(given, to_core)
    left = jnp.where(own_first, kept, taken)
    right = jnp.where(own_first, taken, kept)
    grad_share = jnp.concatenate([left[:, :head], right[:, :head]], axis=1)
    hvp_share = jnp.concatenate([left[:, head:], right[:, head:]], axis=1)
    probe_cols = lax.dynamic_slice_in_dim(probe, y * 2 * head, 2 * head, 1).astype(jnp.float32)
    return step_outputs(momentum, curvature, probe_cols, grad_share, hvp_share)


def solution(mesh):
    on_links = mesh.shape["dp"] == 2 and mesh.shape["fsdp"] == 16
    return jax.shard_map(
        by_links if on_links else by_collectives,
        mesh=mesh,
        in_specs=(
            P(("dp", "fsdp"), None),
            P(("dp", "fsdp"), None),
            P("fsdp", None),
            P("fsdp", None),
            P(),
            P("fsdp", "dp"),
            P("fsdp", "dp"),
        ),
        out_specs=(P("fsdp", "dp"), P("fsdp", "dp"), P("fsdp", "dp")),
        check_vma=False,
    )
```

time: 414 us -> 202 us (0.49)
  waiting for transfers between devices: 321 us -> 81.8 us
  starting transfers between devices: 0.2 us -> 64.5 us
  local copies, waits for them, and re-layouts: 39.3 us -> 14.8 us
  between operations: 14 us -> 1.29 us
    unnamed x6 -> x0, waiting for transfers between devices: 150 us -> none
    all_gather x2 -> x0, waiting for transfers between devices: 129 us -> none  [the longest x1 68.3 us: on_device(): weight_piece = lax.all_gather(k_weight, 'fsdp', axis=0, tiled=True)]
    ppermute x0 -> x37, waiting for transfers between devices: none -> 81.8 us  [send(): return lax.ppermute(value, AXES, pairs_of(move))]
    ppermute x0 -> x37, starting transfers between devices: none -> 64.5 us  [send(): return lax.ppermute(value, AXES, pairs_of(move))]
    reduce_scatter x2 -> x0, waiting for transfers between devices: 42 us -> none  [the longest x1 22.5 us: on_device(): lax.psum_scatter(hvp_owned, 'dp', scatter_dimension=1, tiled=True)]
    unnamed x30 -> x25, local copies, waits for them, and re-layouts: 24.8 us -> 7.29 us
    mul x7 -> x0, local copies, waits for them, and re-layouts: 6.85 us -> none  [the longest x2 3.21 us: head_terms(): grad_vals = inverse * weighted - cubed * values * along / head_size]
    concatenate x0 -> x1, local copies, waits for them, and re-layouts: none -> 5.96 us  [by_links(): all_acts = jnp.concatenate([acts, other_acts], axis=0)]
  transfers between devices with their start and end apart: 5 -> 37, of which waited for: 5 -> 19; matrix products, arithmetic and copies ran while one was open for 3% -> 24% of each run, Pallas kernels for 0% -> 0%
where the time goes in v1:
time: 202 us
  waiting for transfers between devices  81.8 us (40%)
  starting transfers between devices  64.5 us (32%)
  matrix products  32.5 us (16%)
  local copies, waits for them, and re-layouts  14.8 us (7%)
  other arithmetic  6.65 us (3%)
    ppermute x37, waiting for transfers between devices, send(): return lax.ppermute(value, AXES, pairs_of(move))  81.8 us
    ppermute x37, starting transfers between devices, send(): return lax.ppermute(value, AXES, pairs_of(move))  64.5 us
    dot_general x16, matrix products, dot(): return jnp.dot(left, right, preferred_element_type=jnp.float32)  18.8 us
    dot_general x16, matrix products, contract_tokens(): lax.dot_general(left, right, (((0,), (0,)), ((), ())), preferred_element_...  13.7 us
    unnamed x25, local copies, waits for them, and re-layouts  7.29 us
    concatenate x1, local copies, waits for them, and re-layouts, by_links(): all_acts = jnp.concatenate([acts, other_acts], axis=0)  5.96 us
  transfers between devices with their start and end apart: 37, of which 19 were waited for; matrix products, arithmetic and copies ran while one was open for 24% of the time, Pallas kernels for 0%

profile of v1, /device:TPU:11, one launch (start us, length us, event | category | flops | bytes accessed | tf_op | source)
XLA Modules:
  0.0 201.5 jit_solution(15038686605838083179)
XLA Ops:
  1.4 1.3 constant_dynamic-slice_fusion.1
  4.0 8.1 %collective-permute-done.1 = bf16[448,512]{0,1:T(8,128)(2,1)S(1)} collective-permute-done((bf16[448,512]{0,1:T(8,128)(2,1)S(1)}, bf16[448,512]{0,1:T(8,128)(2,1)S(1)}, u32[]{:S(2)}, u32[]{:S(2)}) %collective-permute-start.1) | collective-permute-done | bytes 458784 | tf_op jit(solution)/shard_map/ppermute | solution.py:87
  12.8 3.2 %collective-permute-start.6 = (bf16[896,256]{0,1:T(8,128)(2,1)S(1)}, bf16[896,256]{0,1:T(8,128)(2,1)S(1)}, u32[]{:S(2)}, u32[]{:S(2)}) collective-permute-start(bf16[896,256]{0,1:T(8,128)(2,1)S(1)} %slice.48), channel_id=1, source_target_pairs={{4,8},{5,9},{6,10},{7,11},{8,4},{9,5},{10,6},{11,7},{20,24},{21,25... | collective-permute-start | bytes 1376264 | tf_op jit(solution)/shard_map/ppermute | solution.py:87
  16.1 10.3 %collective-permute-done.6 = bf16[896,256]{0,1:T(8,128)(2,1)S(1)} collective-permute-done((bf16[896,256]{0,1:T(8,128)(2,1)S(1)}, bf16[896,256]{0,1:T(8,128)(2,1)S(1)}, u32[]{:S(2)}, u32[]{:S(2)}) %collective-permute-start.6) | collective-permute-done | bytes 458784 | tf_op jit(solution)/shard_map/ppermute | solution.py:87
  26.4 2.1 %collective-permute-start.7 = (bf16[896,256]{0,1:T(8,128)(2,1)S(1)}, bf16[896,256]{0,1:T(8,128)(2,1)}, u32[]{:S(2)}, u32[]{:S(2)}) collective-permute-start(bf16[896,256]{0,1:T(8,128)(2,1)S(1)} %collective-permute-done.6), channel_id=1, source_target_pairs={{4,0},{5,1},{6,2},{7,3},{8,12},{9,13},{10,14},{11,15},{20,16},{21,... | collective-permute-start | bytes 1376264 | tf_op jit(solution)/shard_map/ppermute | solution.py:87
  28.5 3.2 %collective-permute-start.8 = (bf16[896,256]{0,1:T(8,128)(2,1)S(1)}, bf16[896,256]{0,1:T(8,128)(2,1)}, u32[]{:S(2)}, u32[]{:S(2)}) collective-permute-start(bf16[896,256]{0,1:T(8,128)(2,1)S(1)} %collective-permute-done.3), channel_id=1, source_target_pairs={{4,8},{5,9},{6,10},{7,11},{8,4},{9,5},{10,6},{11,7},{20,24},{21,25... | collective-permute-start | bytes 1376264 | tf_op jit(solution)/shard_map/ppermute | solution.py:87
  32.6 1.5 collective-permute-start.14
  34.1 2.5 %collective-permute-done.7 = bf16[896,256]{0,1:T(8,128)(2,1)} collective-permute-done((bf16[896,256]{0,1:T(8,128)(2,1)S(1)}, bf16[896,256]{0,1:T(8,128)(2,1)}, u32[]{:S(2)}, u32[]{:S(2)}) %collective-permute-start.7) | collective-permute-done | bytes 458784 | tf_op jit(solution)/shard_map/ppermute | solution.py:87
  36.6 4.7 %collective-permute-done.8 = bf16[896,256]{0,1:T(8,128)(2,1)} collective-permute-done((bf16[896,256]{0,1:T(8,128)(2,1)S(1)}, bf16[896,256]{0,1:T(8,128)(2,1)}, u32[]{:S(2)}, u32[]{:S(2)}) %collective-permute-start.8) | collective-permute-done | bytes 458784 | tf_op jit(solution)/shard_map/ppermute | solution.py:87
  41.3 1.3 add.352
  42.5 2.1 %collective-permute-start.11 = (bf16[896,256]{0,1:T(8,128)(2,1)S(1)}, bf16[896,256]{0,1:T(8,128)(2,1)}, u32[]{:S(2)}, u32[]{:S(2)}) collective-permute-start(bf16[896,256]{0,1:T(8,128)(2,1)S(1)} %add.352), channel_id=1, source_target_pairs={{4,0},{5,1},{6,2},{7,3},{8,12},{9,13},{10,14},{11,15},{20,16},{21,... | collective-permute-start | bytes 1376264 | tf_op jit(solution)/shard_map/ppermute | solution.py:87
  44.6 5.9 %constant_dynamic-update-slice_fusion.1 = bf16[896,7168]{1,0:T(8,128)(2,1)} fusion(bf16[448,7168]{1,0:T(8,128)(2,1)} %param.7), kind=kLoop, calls=%fused_computation.206 | loop fusion | bytes 12845056
  53.8 1.3 collective-permute-start.13
  55.1 1.2 collective-permute-start.12
  56.3 6.0 %constant_dynamic-update-slice_fusion = bf16[896,7168]{1,0:T(8,128)(2,1)} fusion(bf16[896,7168]{1,0:T(8,128)(2,1)} %constant_dynamic-update-slice_fusion.1, bf16[448,7168]{1,0:T(8,128)(2,1)} %collective-permute-done), kind=kLoop, calls=%fused_computation.205 | loop fusion | bytes 12845056 | tf_op jit(solution)/shard_map/concatenate | solution.py:161
  62.8 4.6 %collective-permute-done.9 = bf16[896,256]{0,1:T(8,128)(2,1)S(1)} collective-permute-done((bf16[896,256]{0,1:T(8,128)(2,1)S(1)}, bf16[896,256]{0,1:T(8,128)(2,1)S(1)}, u32[]{:S(2)}, u32[]{:S(2)}) %collective-permute-start.9) | collective-permute-done | bytes 458784 | tf_op jit(solution)/shard_map/ppermute | solution.py:87
  68.6 2.0 %collective-permute-done.13 = bf16[896,256]{0,1:T(8,128)(2,1)S(1)} collective-permute-done((bf16[896,256]{0,1:T(8,128)(2,1)S(1)}, bf16[896,256]{0,1:T(8,128)(2,1)S(1)}, u32[]{:S(2)}, u32[]{:S(2)}) %collective-permute-start.13) | collective-permute-done | bytes 458784 | tf_op jit(solution)/shard_map/ppermute | solution.py:87
  70.9 6.3 %collective-permute-done.12 = bf16[896,256]{0,1:T(8,128)(2,1)S(1)} collective-permute-done((bf16[896,256]{0,1:T(8,128)(2,1)S(1)}, bf16[896,256]{0,1:T(8,128)(2,1)S(1)}, u32[]{:S(2)}, u32[]{:S(2)}) %collective-permute-start.12) | collective-permute-done | bytes 458784 | tf_op jit(solution)/shard_map/ppermute | solution.py:87
  78.5 2.3 %fusion.106 = f32[896,256]{0,1:T(8,128)S(1)} fusion(bf16[896,7168]{1,0:T(8,128)(2,1)} %constant_dynamic-update-slice_fusion, s32[]{:T(128)S(6)} %select_n.183, bf16[896,256]{0,1:T(8,128)(2,1)S(1)} %collective-permute-done.13, bf16[896,256]{0,1:T(8,128)(2,1)S(1)} %collective-permute-done.12, pred[]{:T(512)S(6)} %eq.6), kind=kOutput, calls=%fused_computation.82 | convolution fusion | flops 411271168 | bytes 3440645 | tf_op jit(solution)/shard_map/dot_general | solution.py:168
  80.8 2.7 %fusion.103 = f32[896,256]{0,1:T(8,128)S(1)} fusion(bf16[896,7168]{1,0:T(8,128)(2,1)} %constant_dynamic-update-slice_fusion, s32[]{:T(128)S(6)} %select_n.184, bf16[896,256]{0,1:T(8,128)(2,1)S(1)} %collective-permute-done.12, bf16[896,256]{0,1:T(8,128)(2,1)S(1)} %collective-permute-done.13, pred[]{:T(512)S(6)} %eq.6), kind=kOutput, calls=%fused_computation.79 | convolution fusion | flops 411271168 | bytes 3440645 | tf_op jit(solution)/shard_map/dot_general | solution.py:168
  83.5 2.2 %convolution_add_fusion.4 = f32[896,256]{0,1:T(8,128)S(1)} fusion(f32[896,256]{0,1:T(8,128)S(1)} %fusion.103, bf16[896,256]{0,1:T(8,128)(2,1)S(1)} %add.359, bf16[896,7168]{1,0:T(8,128)(2,1)} %constant_dynamic-update-slice_fusion, s32[]{:T(128)S(6)} %select_n.183), kind=kOutput, calls=%fused_computation.23 | convolution fusion | flops 411271168 | bytes 3899396 | tf_op jit(solution)/shard_map/dot_general | solution.py:168
  86.1 2.2 %fusion.121 = f32[896,256]{0,1:T(8,128)S(1)} fusion(bf16[896,7168]{1,0:T(8,128)(2,1)} %constant_dynamic-update-slice_fusion, s32[]{:T(128)S(6)} %select_n.176, bf16[896,256]{0,1:T(8,128)(2,1)S(1)} %collective-permute-done.5, bf16[896,256]{0,1:T(8,128)(2,1)S(1)} %collective-permute-done.4, pred[]{:T(512)S(6)} %eq.6), kind=kOutput, calls=%fused_computation.97 | convolution fusion | flops 411271168 | bytes 3440645 | tf_op jit(solution)/shard_map/dot_general | solution.py:168
  92.7 5.2 %collective-permute-done.16 = bf16[896,256]{0,1:T(8,128)(2,1)S(1)} collective-permute-done((bf16[896,256]{0,1:T(8,128)(2,1)S(1)}, bf16[896,256]{0,1:T(8,128)(2,1)S(1)}, u32[]{:S(2)}, u32[]{:S(2)}) %collective-permute-start.16) | collective-permute-done | bytes 458784 | tf_op jit(solution)/shard_map/ppermute | solution.py:87
  100.3 2.5 %collective-permute-done.17 = bf16[896,256]{0,1:T(8,128)(2,1)S(1)} collective-permute-done((bf16[896,256]{0,1:T(8,128)(2,1)S(1)}, bf16[896,256]{0,1:T(8,128)(2,1)S(1)}, u32[]{:S(2)}, u32[]{:S(2)}) %collective-permute-start.17) | collective-permute-done | bytes 458784 | tf_op jit(solution)/shard_map/ppermute | solution.py:87
  105.3 2.2 %collective-permute-done.18 = bf16[896,256]{0,1:T(8,128)(2,1)S(1)} collective-permute-done((bf16[896,256]{0,1:T(8,128)(2,1)S(1)}, bf16[896,256]{0,1:T(8,128)(2,1)S(1)}, u32[]{:S(2)}, u32[]{:S(2)}) %collective-permute-start.18) | collective-permute-done | bytes 458784 | tf_op jit(solution)/shard_map/ppermute | solution.py:87
  111.5 1.2 collective-permute-start.22
  113.8 3.5 %collective-permute-done.23 = bf16[896,256]{1,0:T(8,128)(2,1)S(1)} collective-permute-done((bf16[896,256]{1,0:T(8,128)(2,1)S(1)}, bf16[896,256]{1,0:T(8,128)(2,1)S(1)}, u32[]{:S(2)}, u32[]{:S(2)}) %collective-permute-start.23) | collective-permute-done | bytes 458784 | tf_op jit(solution)/shard_map/ppermute | solution.py:87
  118.0 1.6 collective-permute-start.24
  121.4 1.2 collective-permute-start.32
  122.7 4.8 %collective-permute-done.26 = bf16[896,256]{1,0:T(8,128)(2,1)S(1)} collective-permute-done((bf16[896,256]{1,0:T(8,128)(2,1)S(1)}, bf16[896,256]{1,0:T(8,128)(2,1)S(1)}, u32[]{:S(2)}, u32[]{:S(2)}) %collective-permute-start.26) | collective-permute-done | bytes 458784 | tf_op jit(solution)/shard_map/ppermute | solution.py:87
  128.2 1.6 collective-permute-start.27
  130.5 1.3 collective-permute-start.28
  133.6 5.9 %collective-permute-done.32 = bf16[896,256]{1,0:T(8,128)(2,1)S(1)} collective-permute-done((bf16[896,256]{1,0:T(8,128)(2,1)S(1)}, bf16[896,256]{1,0:T(8,128)(2,1)S(1)}, u32[]{:S(2)}, u32[]{:S(2)}) %collective-permute-start.32) | collective-permute-done | bytes 458784 | tf_op jit(solution)/shard_map/ppermute | solution.py:87
  140.5 1.7 collective-permute-start.33
  142.9 3.2 %collective-permute-start.34 = (bf16[896,256]{1,0:T(8,128)(2,1)S(1)}, bf16[896,256]{1,0:T(8,128)(2,1)S(1)}, u32[]{:S(2)}, u32[]{:S(2)}) collective-permute-start(bf16[896,256]{1,0:T(8,128)(2,1)S(1)} %fusion.91), channel_id=1, source_target_pairs={{4,8},{5,9},{6,10},{7,11},{8,4},{9,5},{10,6},{11,7},{20,24},{21,25... | collective-permute-start | bytes 1376264 | tf_op jit(solution)/shard_map/ppermute | solution.py:87
  146.8 1.3 collective-permute-start.19
  148.1 4.1 %collective-permute-done.20 = bf16[896,256]{1,0:T(8,128)(2,1)S(1)} collective-permute-done((bf16[896,256]{1,0:T(8,128)(2,1)S(1)}, bf16[896,256]{1,0:T(8,128)(2,1)S(1)}, u32[]{:S(2)}, u32[]{:S(2)}) %collective-permute-start.20) | collective-permute-done | bytes 458784 | tf_op jit(solution)/shard_map/ppermute | solution.py:87
  152.2 1.5 collective-permute-start.29
  154.4 1.7 collective-permute-start.21
  156.1 1.5 fusion.86
  157.6 2.1 %collective-permute-start.35 = (bf16[896,256]{1,0:T(8,128)(2,1)}, bf16[896,256]{1,0:T(8,128)(2,1)S(1)}, u32[]{:S(2)}, u32[]{:S(2)}) collective-permute-start(bf16[896,256]{1,0:T(8,128)(2,1)} %fusion.86), channel_id=1, source_target_pairs={{0,4},{1,5},{2,6},{3,7},{4,0},{5,1},{6,2},{7,3},{8,12},{9,13},{10,... | collective-permute-start | bytes 1376264 | tf_op jit(solution)/shard_map/ppermute | solution.py:87
  159.7 4.6 %collective-permute-done.29 = bf16[896,256]{1,0:T(8,128)(2,1)S(1)} collective-permute-done((bf16[896,256]{1,0:T(8,128)(2,1)S(1)}, bf16[896,256]{1,0:T(8,128)(2,1)S(1)}, u32[]{:S(2)}, u32[]{:S(2)}) %collective-permute-start.29) | collective-permute-done | bytes 458784 | tf_op jit(solution)/shard_map/ppermute | solution.py:87
  164.5 3.3 %collective-permute-start.30 = (bf16[896,256]{1,0:T(8,128)(2,1)S(1)}, bf16[896,256]{1,0:T(8,128)(2,1)}, u32[]{:S(2)}, u32[]{:S(2)}) collective-permute-start(bf16[896,256]{1,0:T(8,128)(2,1)S(1)} %add_convert_fusion), channel_id=1, source_target_pairs={{4,8},{5,9},{6,10},{7,11},{8,4},{9,5},{10,6},{11,7},{20,24},{21,25... | collective-permute-start | bytes 1376264 | tf_op jit(solution)/shard_map/ppermute | solution.py:87
  167.8 1.5 collective-permute-done.35
  169.2 6.9 %collective-permute-done.30 = bf16[896,256]{1,0:T(8,128)(2,1)} collective-permute-done((bf16[896,256]{1,0:T(8,128)(2,1)S(1)}, bf16[896,256]{1,0:T(8,128)(2,1)}, u32[]{:S(2)}, u32[]{:S(2)}) %collective-permute-start.30) | collective-permute-done | bytes 458784 | tf_op jit(solution)/shard_map/ppermute | solution.py:87
  176.1 2.3 %fusion.100 = f32[896,256]{1,0:T(8,128)S(1)} fusion(bf16[896,7168]{1,0:T(8,128)(2,1)} %constant_dynamic-update-slice_fusion, s32[]{:T(128)S(6)} %select_n.168, bf16[896,256]{1,0:T(8,128)(2,1)S(1)} %collective-permute-done.35, bf16[896,256]{1,0:T(8,128)(2,1)} %collective-permute-done.30, bf16[896,256]{1,0:T(8,128)(2,1)S(1)} %collective-permute-done.21, ...), kind=kOutput, calls=%fused_computation.76 | convolution fusion | flops 414253056 | bytes 4816900 | tf_op jit(solution)/shard_map/dot_general | solution.py:12
  178.4 20.3 %collective-permute-start.36 = (f32[448,256]{1,0:T(8,128)S(1)}, f32[448,256]{1,0:T(8,128)S(1)}, u32[]{:S(2)}, u32[]{:S(2)}) collective-permute-start(f32[448,256]{1,0:T(8,128)S(1)} %constant_dynamic-slice_fusion), channel_id=1, source_target_pairs={{0,1},{1,0},{2,3},{3,2},{4,5},{5,4},{6,7},{7,6},{8,9},{9,8},{10,11... | collective-permute-start | bytes 1376264 | tf_op jit(solution)/shard_map/ppermute | solution.py:87
  198.7 1.4 collective-permute-done.36
  (105 shorter events, 34.8 us)
Async XLA Ops:
  0.6 2.2 %copy-start.2 = (bf16[448,512]{1,0:T(8,128)(2,1)S(1)}, bf16[448,512]{1,0:T(8,128)(2,1)}, u32[]{:S(2)}) copy-start(bf16[448,512]{1,0:T(8,128)(2,1)} %param.9) | copy-start | bytes 1376260
  0.6 54.4 %collective-permute-start = (bf16[448,7168]{1,0:T(8,128)(2,1)}, bf16[448,7168]{1,0:T(8,128)(2,1)}, u32[]{:S(2)}, u32[]{:S(2)}) collective-permute-start(bf16[448,7168]{1,0:T(8,128)(2,1)} %param.7), channel_id=1, source_target_pairs={{0,1},{1,0},{2,3},{3,2},{4,5},{5,4},{6,7},{7,6},{8,9},{9,8},{10,11... | collective-permute-start | bytes 19267592 | tf_op jit(solution)/shard_map/ppermute | solution.py:87
  3.4 8.7 %collective-permute-start.1 = (bf16[448,512]{0,1:T(8,128)(2,1)S(1)}, bf16[448,512]{0,1:T(8,128)(2,1)S(1)}, u32[]{:S(2)}, u32[]{:S(2)}) collective-permute-start(bf16[448,512]{0,1:T(8,128)(2,1)S(1)} %pad_maximum_fusion), channel_id=1, source_target_pairs={{0,1},{1,0},{2,3},{3,2},{4,5},{5,4},{6,7},{7,6},{8,9},{9,8},{10,11... | collective-permute-start | bytes 1376264 | tf_op jit(solution)/shard_map/ppermute | solution.py:87
  12.8 13.6 %collective-permute-start.6 = (bf16[896,256]{0,1:T(8,128)(2,1)S(1)}, bf16[896,256]{0,1:T(8,128)(2,1)S(1)}, u32[]{:S(2)}, u32[]{:S(2)}) collective-permute-start(bf16[896,256]{0,1:T(8,128)(2,1)S(1)} %slice.48), channel_id=1, source_target_pairs={{4,8},{5,9},{6,10},{7,11},{8,4},{9,5},{10,6},{11,7},{20,24},{21,25... | collective-permute-start | bytes 1376264 | tf_op jit(solution)/shard_map/ppermute | solution.py:87
  16.0 12.5 %collective-permute-start.3 = (bf16[896,256]{0,1:T(8,128)(2,1)S(1)}, bf16[896,256]{0,1:T(8,128)(2,1)S(1)}, u32[]{:S(2)}, u32[]{:S(2)}) collective-permute-start(bf16[896,256]{0,1:T(8,128)(2,1)S(1)} %slice.48), channel_id=1, source_target_pairs={{0,4},{1,5},{2,6},{3,7},{4,0},{5,1},{6,2},{7,3},{8,12},{9,13},{10,... | collective-permute-start | bytes 1376264 | tf_op jit(solution)/shard_map/ppermute | solution.py:87
  26.4 10.2 %collective-permute-start.7 = (bf16[896,256]{0,1:T(8,128)(2,1)S(1)}, bf16[896,256]{0,1:T(8,128)(2,1)}, u32[]{:S(2)}, u32[]{:S(2)}) collective-permute-start(bf16[896,256]{0,1:T(8,128)(2,1)S(1)} %collective-permute-done.6), channel_id=1, source_target_pairs={{4,0},{5,1},{6,2},{7,3},{8,12},{9,13},{10,14},{11,15},{20,16},{21,... | collective-permute-start | bytes 1376264 | tf_op jit(solution)/shard_map/ppermute | solution.py:87
  28.5 12.8 %collective-permute-start.8 = (bf16[896,256]{0,1:T(8,128)(2,1)S(1)}, bf16[896,256]{0,1:T(8,128)(2,1)}, u32[]{:S(2)}, u32[]{:S(2)}) collective-permute-start(bf16[896,256]{0,1:T(8,128)(2,1)S(1)} %collective-permute-done.3), channel_id=1, source_target_pairs={{4,8},{5,9},{6,10},{7,11},{8,4},{9,5},{10,6},{11,7},{20,24},{21,25... | collective-permute-start | bytes 1376264 | tf_op jit(solution)/shard_map/ppermute | solution.py:87
  32.6 18.2 %collective-permute-start.14 = (bf16[448,256]{0,1:T(8,128)(2,1)}, bf16[448,256]{0,1:T(8,128)(2,1)S(1)}, u32[]{:S(2)}, u32[]{:S(2)}) collective-permute-start(bf16[448,256]{0,1:T(8,128)(2,1)} %pad_maximum_fusion.3), channel_id=1, source_target_pairs={{0,1},{1,0},{2,3},{3,2},{4,5},{5,4},{6,7},{7,6},{8,9},{9,8},{10,11... | collective-permute-start | bytes 688136 | tf_op jit(solution)/shard_map/ppermute | solution.py:87
  42.5 10.1 %collective-permute-start.11 = (bf16[896,256]{0,1:T(8,128)(2,1)S(1)}, bf16[896,256]{0,1:T(8,128)(2,1)}, u32[]{:S(2)}, u32[]{:S(2)}) collective-permute-start(bf16[896,256]{0,1:T(8,128)(2,1)S(1)} %add.352), channel_id=1, source_target_pairs={{4,0},{5,1},{6,2},{7,3},{8,12},{9,13},{10,14},{11,15},{20,16},{21,... | collective-permute-start | bytes 1376264 | tf_op jit(solution)/shard_map/ppermute | solution.py:87
  50.9 11.4 %collective-permute-start.2 = (bf16[896,256]{0,1:T(8,128)(2,1)S(1)}, bf16[896,256]{0,1:T(8,128)(2,1)S(1)}, u32[]{:S(2)}, u32[]{:S(2)}) collective-permute-start(bf16[896,256]{0,1:T(8,128)(2,1)S(1)} %slice.48), channel_id=1, source_target_pairs={{0,2},{1,3},{2,0},{3,1},{4,6},{5,7},{6,4},{7,5},{8,10},{9,11},{10,... | collective-permute-start | bytes 1376264 | tf_op jit(solution)/shard_map/ppermute | solution.py:87
  51.2 11.3 %collective-permute-start.4 = (bf16[896,256]{0,1:T(8,128)(2,1)S(1)}, bf16[896,256]{0,1:T(8,128)(2,1)S(1)}, u32[]{:S(2)}, u32[]{:S(2)}) collective-permute-start(bf16[896,256]{0,1:T(8,128)(2,1)S(1)} %collective-permute-done.3), channel_id=1, source_target_pairs={{0,2},{1,17},{2,0},{3,19},{4,6},{5,21},{6,4},{7,23},{8,10},{9,25},... | collective-permute-start | bytes 1376264 | tf_op jit(solution)/shard_map/ppermute | solution.py:87
  52.4 15.0 %collective-permute-start.9 = (bf16[896,256]{0,1:T(8,128)(2,1)S(1)}, bf16[896,256]{0,1:T(8,128)(2,1)S(1)}, u32[]{:S(2)}, u32[]{:S(2)}) collective-permute-start(bf16[896,256]{0,1:T(8,128)(2,1)S(1)} %add.352), channel_id=1, source_target_pairs={{0,2},{1,17},{2,0},{3,19},{4,6},{5,21},{6,4},{7,23},{8,10},{9,25},... | collective-permute-start | bytes 1376264 | tf_op jit(solution)/shard_map/ppermute | solution.py:87
  53.8 16.9 %collective-permute-start.13 = (bf16[896,256]{0,1:T(8,128)(2,1)S(1)}, bf16[896,256]{0,1:T(8,128)(2,1)S(1)}, u32[]{:S(2)}, u32[]{:S(2)}) collective-permute-start(bf16[896,256]{0,1:T(8,128)(2,1)S(1)} %add.359), channel_id=1, source_target_pairs={{0,16},{1,3},{2,18},{3,1},{4,20},{5,7},{6,22},{7,5},{8,24},{9,11},... | collective-permute-start | bytes 1376264 | tf_op jit(solution)/shard_map/ppermute | solution.py:87
  55.1 22.2 %collective-permute-start.12 = (bf16[896,256]{0,1:T(8,128)(2,1)S(1)}, bf16[896,256]{0,1:T(8,128)(2,1)S(1)}, u32[]{:S(2)}, u32[]{:S(2)}) collective-permute-start(bf16[896,256]{0,1:T(8,128)(2,1)S(1)} %add.359), channel_id=1, source_target_pairs={{0,2},{1,17},{2,0},{3,19},{4,6},{5,21},{6,4},{7,23},{8,10},{9,25},... | collective-permute-start | bytes 1376264 | tf_op jit(solution)/shard_map/ppermute | solution.py:87
  62.3 23.4 %collective-permute-start.5 = (bf16[896,256]{0,1:T(8,128)(2,1)S(1)}, bf16[896,256]{0,1:T(8,128)(2,1)S(1)}, u32[]{:S(2)}, u32[]{:S(2)}) collective-permute-start(bf16[896,256]{0,1:T(8,128)(2,1)S(1)} %collective-permute-done.3), channel_id=1, source_target_pairs={{0,16},{1,3},{2,18},{3,1},{4,20},{5,7},{6,22},{7,5},{8,24},{9,11},... | collective-permute-start | bytes 1376264 | tf_op jit(solution)/shard_map/ppermute | solution.py:87
  62.5 29.3 %collective-permute-start.15 = (bf16[896,256]{0,1:T(8,128)(2,1)S(1)}, bf16[896,256]{0,1:T(8,128)(2,1)S(1)}, u32[]{:S(2)}, u32[]{:S(2)}) collective-permute-start(bf16[896,256]{0,1:T(8,128)(2,1)S(1)} %collective-permute-done.2), channel_id=1, source_target_pairs={{0,16},{1,17},{2,18},{3,19},{4,20},{5,21},{6,22},{7,23},{8,24},{9,... | collective-permute-start | bytes 1376264 | tf_op jit(solution)/shard_map/ppermute | solution.py:87
  67.4 22.9 %collective-permute-start.10 = (bf16[896,256]{0,1:T(8,128)(2,1)S(1)}, bf16[896,256]{0,1:T(8,128)(2,1)S(1)}, u32[]{:S(2)}, u32[]{:S(2)}) collective-permute-start(bf16[896,256]{0,1:T(8,128)(2,1)S(1)} %add.352), channel_id=1, source_target_pairs={{0,16},{1,3},{2,18},{3,1},{4,20},{5,7},{6,22},{7,5},{8,24},{9,11},... | collective-permute-start | bytes 1376264 | tf_op jit(solution)/shard_map/ppermute | solution.py:87
  70.7 27.2 %collective-permute-start.16 = (bf16[896,256]{0,1:T(8,128)(2,1)S(1)}, bf16[896,256]{0,1:T(8,128)(2,1)S(1)}, u32[]{:S(2)}, u32[]{:S(2)}) collective-permute-start(bf16[896,256]{0,1:T(8,128)(2,1)S(1)} %collective-permute-done.4), channel_id=1, source_target_pairs={{0,16},{1,3},{2,18},{3,1},{4,20},{5,7},{6,22},{7,5},{8,24},{9,11},... | collective-permute-start | bytes 1376264 | tf_op jit(solution)/shard_map/ppermute | solution.py:87
  77.2 25.6 %collective-permute-start.17 = (bf16[896,256]{0,1:T(8,128)(2,1)S(1)}, bf16[896,256]{0,1:T(8,128)(2,1)S(1)}, u32[]{:S(2)}, u32[]{:S(2)}) collective-permute-start(bf16[896,256]{0,1:T(8,128)(2,1)S(1)} %collective-permute-done.9), channel_id=1, source_target_pairs={{0,16},{1,3},{2,18},{3,1},{4,20},{5,7},{6,22},{7,5},{8,24},{9,11},... | collective-permute-start | bytes 1376264 | tf_op jit(solution)/shard_map/ppermute | solution.py:87
  78.5 9.8 %copy-start = (bf16[896,7168]{1,0:T(8,128)(2,1)S(1)}, bf16[896,7168]{1,0:T(8,128)(2,1)}, u32[]{:S(2)}) copy-start(bf16[896,7168]{1,0:T(8,128)(2,1)} %constant_dynamic-update-slice_fusion) | copy-start | bytes 38535172
  85.7 21.7 %collective-permute-start.18 = (bf16[896,256]{0,1:T(8,128)(2,1)S(1)}, bf16[896,256]{0,1:T(8,128)(2,1)S(1)}, u32[]{:S(2)}, u32[]{:S(2)}) collective-permute-start(bf16[896,256]{0,1:T(8,128)(2,1)S(1)} %collective-permute-done.12), channel_id=1, source_target_pairs={{0,16},{1,3},{2,18},{3,1},{4,20},{5,7},{6,22},{7,5},{8,24},{9,11},... | collective-permute-start | bytes 1376264 | tf_op jit(solution)/shard_map/ppermute | solution.py:87
  105.2 3.0 %copy-start.5 = (f32[128]{0:T(128)S(1)}, f32[128]{0:T(128)}, u32[]{:S(2)}) copy-start(f32[128]{0:T(128)} %param.11) | copy-start | bytes 1540
  109.9 7.4 %collective-permute-start.23 = (bf16[896,256]{1,0:T(8,128)(2,1)S(1)}, bf16[896,256]{1,0:T(8,128)(2,1)S(1)}, u32[]{:S(2)}, u32[]{:S(2)}) collective-permute-start(bf16[896,256]{1,0:T(8,128)(2,1)S(1)} %convolution_convert_fusion.4), channel_id=1, source_target_pairs={{0,16},{1,3},{2,18},{3,1},{4,20},{5,7},{6,22},{7,5},{8,24},{9,11},... | collective-permute-start | bytes 1376264 | tf_op jit(solution)/shard_map/ppermute | solution.py:87
  111.5 18.3 %collective-permute-start.22 = (bf16[896,256]{1,0:T(8,128)(2,1)S(1)}, bf16[896,256]{1,0:T(8,128)(2,1)S(1)}, u32[]{:S(2)}, u32[]{:S(2)}) collective-permute-start(bf16[896,256]{1,0:T(8,128)(2,1)S(1)} %fusion.28), channel_id=1, source_target_pairs={{0,16},{1,3},{2,18},{3,1},{4,20},{5,7},{6,22},{7,5},{8,24},{9,11},... | collective-permute-start | bytes 1376264 | tf_op jit(solution)/shard_map/ppermute | solution.py:87
  113.5 14.0 %collective-permute-start.26 = (bf16[896,256]{1,0:T(8,128)(2,1)S(1)}, bf16[896,256]{1,0:T(8,128)(2,1)S(1)}, u32[]{:S(2)}, u32[]{:S(2)}) collective-permute-start(bf16[896,256]{1,0:T(8,128)(2,1)S(1)} %convolution_convert_fusion.2), channel_id=1, source_target_pairs={{0,16},{1,3},{2,18},{3,1},{4,20},{5,7},{6,22},{7,5},{8,24},{9,11},... | collective-permute-start | bytes 1376264 | tf_op jit(solution)/shard_map/ppermute | solution.py:87
  118.0 11.8 %collective-permute-start.24 = (bf16[896,256]{1,0:T(8,128)(2,1)S(1)}, bf16[896,256]{1,0:T(8,128)(2,1)S(1)}, u32[]{:S(2)}, u32[]{:S(2)}) collective-permute-start(bf16[896,256]{1,0:T(8,128)(2,1)S(1)} %fusion.70), channel_id=1, source_target_pairs={{0,2},{1,17},{2,0},{3,19},{4,6},{5,21},{6,4},{7,23},{8,10},{9,25},... | collective-permute-start | bytes 1376264 | tf_op jit(solution)/shard_map/ppermute | solution.py:87
  120.4 20.1 %collective-permute-start.25 = (bf16[896,256]{1,0:T(8,128)(2,1)S(1)}, bf16[896,256]{1,0:T(8,128)(2,1)S(1)}, u32[]{:S(2)}, u32[]{:S(2)}) collective-permute-start(bf16[896,256]{1,0:T(8,128)(2,1)S(1)} %fusion.34), channel_id=1, source_target_pairs={{0,16},{1,3},{2,18},{3,1},{4,20},{5,7},{6,22},{7,5},{8,24},{9,11},... | collective-permute-start | bytes 1376264 | tf_op jit(solution)/shard_map/ppermute | solution.py:87
  121.4 18.0 %collective-permute-start.32 = (bf16[896,256]{1,0:T(8,128)(2,1)S(1)}, bf16[896,256]{1,0:T(8,128)(2,1)S(1)}, u32[]{:S(2)}, u32[]{:S(2)}) collective-permute-start(bf16[896,256]{1,0:T(8,128)(2,1)S(1)} %convolution_convert_fusion), channel_id=1, source_target_pairs={{0,16},{1,3},{2,18},{3,1},{4,20},{5,7},{6,22},{7,5},{8,24},{9,11},... | collective-permute-start | bytes 1376264 | tf_op jit(solution)/shard_map/ppermute | solution.py:87
  128.2 14.0 %collective-permute-start.27 = (bf16[896,256]{1,0:T(8,128)(2,1)S(1)}, bf16[896,256]{1,0:T(8,128)(2,1)S(1)}, u32[]{:S(2)}, u32[]{:S(2)}) collective-permute-start(bf16[896,256]{1,0:T(8,128)(2,1)S(1)} %fusion.61), channel_id=1, source_target_pairs={{0,2},{1,17},{2,0},{3,19},{4,6},{5,21},{6,4},{7,23},{8,10},{9,25},... | collective-permute-start | bytes 1376264 | tf_op jit(solution)/shard_map/ppermute | solution.py:87
  130.5 11.6 %collective-permute-start.28 = (bf16[896,256]{1,0:T(8,128)(2,1)S(1)}, bf16[896,256]{1,0:T(8,128)(2,1)S(1)}, u32[]{:S(2)}, u32[]{:S(2)}) collective-permute-start(bf16[896,256]{1,0:T(8,128)(2,1)S(1)} %fusion.95), channel_id=1, source_target_pairs={{0,4},{1,5},{2,6},{3,7},{12,8},{13,9},{14,10},{15,11},{16,20},{17,... | collective-permute-start | bytes 1376264 | tf_op jit(solution)/shard_map/ppermute | solution.py:87
  132.5 21.9 %collective-permute-start.31 = (bf16[896,256]{1,0:T(8,128)(2,1)S(1)}, bf16[896,256]{1,0:T(8,128)(2,1)S(1)}, u32[]{:S(2)}, u32[]{:S(2)}) collective-permute-start(bf16[896,256]{1,0:T(8,128)(2,1)S(1)} %fusion.40), channel_id=1, source_target_pairs={{0,16},{1,3},{2,18},{3,1},{4,20},{5,7},{6,22},{7,5},{8,24},{9,11},... | collective-permute-start | bytes 1376264 | tf_op jit(solution)/shard_map/ppermute | solution.py:87
  139.5 12.7 %collective-permute-start.20 = (bf16[896,256]{1,0:T(8,128)(2,1)S(1)}, bf16[896,256]{1,0:T(8,128)(2,1)S(1)}, u32[]{:S(2)}, u32[]{:S(2)}) collective-permute-start(bf16[896,256]{1,0:T(8,128)(2,1)S(1)} %convolution_convert_fusion.6), channel_id=1, source_target_pairs={{0,16},{1,3},{2,18},{3,1},{4,20},{5,7},{6,22},{7,5},{8,24},{9,11},... | collective-permute-start | bytes 1376264 | tf_op jit(solution)/shard_map/ppermute | solution.py:87
  140.5 15.7 %collective-permute-start.33 = (bf16[896,256]{1,0:T(8,128)(2,1)S(1)}, bf16[896,256]{1,0:T(8,128)(2,1)S(1)}, u32[]{:S(2)}, u32[]{:S(2)}) collective-permute-start(bf16[896,256]{1,0:T(8,128)(2,1)S(1)} %fusion.52), channel_id=1, source_target_pairs={{0,2},{1,17},{2,0},{3,19},{4,6},{5,21},{6,4},{7,23},{8,10},{9,25},... | collective-permute-start | bytes 1376264 | tf_op jit(solution)/shard_map/ppermute | solution.py:87
  142.9 13.3 %collective-permute-start.34 = (bf16[896,256]{1,0:T(8,128)(2,1)S(1)}, bf16[896,256]{1,0:T(8,128)(2,1)S(1)}, u32[]{:S(2)}, u32[]{:S(2)}) collective-permute-start(bf16[896,256]{1,0:T(8,128)(2,1)S(1)} %fusion.91), channel_id=1, source_target_pairs={{4,8},{5,9},{6,10},{7,11},{8,4},{9,5},{10,6},{11,7},{20,24},{21,25... | collective-permute-start | bytes 1376264 | tf_op jit(solution)/shard_map/ppermute | solution.py:87
  146.8 20.9 %collective-permute-start.19 = (bf16[896,256]{1,0:T(8,128)(2,1)S(1)}, bf16[896,256]{1,0:T(8,128)(2,1)S(1)}, u32[]{:S(2)}, u32[]{:S(2)}) collective-permute-start(bf16[896,256]{1,0:T(8,128)(2,1)S(1)} %fusion.22), channel_id=1, source_target_pairs={{0,16},{1,3},{2,18},{3,1},{4,20},{5,7},{6,22},{7,5},{8,24},{9,11},... | collective-permute-start | bytes 1376264 | tf_op jit(solution)/shard_map/ppermute | solution.py:87
  152.2 12.2 %collective-permute-start.29 = (bf16[896,256]{1,0:T(8,128)(2,1)S(1)}, bf16[896,256]{1,0:T(8,128)(2,1)S(1)}, u32[]{:S(2)}, u32[]{:S(2)}) collective-permute-start(bf16[896,256]{1,0:T(8,128)(2,1)S(1)} %fusion.91), channel_id=1, source_target_pairs={{0,4},{1,5},{2,6},{3,7},{12,8},{13,9},{14,10},{15,11},{16,20},{17,... | collective-permute-start | bytes 1376264 | tf_op jit(solution)/shard_map/ppermute | solution.py:87
  154.4 13.3 %collective-permute-start.21 = (bf16[896,256]{1,0:T(8,128)(2,1)S(1)}, bf16[896,256]{1,0:T(8,128)(2,1)S(1)}, u32[]{:S(2)}, u32[]{:S(2)}) collective-permute-start(bf16[896,256]{1,0:T(8,128)(2,1)S(1)} %fusion.79), channel_id=1, source_target_pairs={{0,2},{1,17},{2,0},{3,19},{4,6},{5,21},{6,4},{7,23},{8,10},{9,25},... | collective-permute-start | bytes 1376264 | tf_op jit(solution)/shard_map/ppermute | solution.py:87
  157.6 11.6 %collective-permute-start.35 = (bf16[896,256]{1,0:T(8,128)(2,1)}, bf16[896,256]{1,0:T(8,128)(2,1)S(1)}, u32[]{:S(2)}, u32[]{:S(2)}) collective-permute-start(bf16[896,256]{1,0:T(8,128)(2,1)} %fusion.86), channel_id=1, source_target_pairs={{0,4},{1,5},{2,6},{3,7},{4,0},{5,1},{6,2},{7,3},{8,12},{9,13},{10,... | collective-permute-start | bytes 1376264 | tf_op jit(solution)/shard_map/ppermute | solution.py:87
  164.5 11.7 %collective-permute-start.30 = (bf16[896,256]{1,0:T(8,128)(2,1)S(1)}, bf16[896,256]{1,0:T(8,128)(2,1)}, u32[]{:S(2)}, u32[]{:S(2)}) collective-permute-start(bf16[896,256]{1,0:T(8,128)(2,1)S(1)} %add_convert_fusion), channel_id=1, source_target_pairs={{4,8},{5,9},{6,10},{7,11},{8,4},{9,5},{10,6},{11,7},{20,24},{21,25... | collective-permute-start | bytes 1376264 | tf_op jit(solution)/shard_map/ppermute | solution.py:87
  178.4 21.7 %collective-permute-start.36 = (f32[448,256]{1,0:T(8,128)S(1)}, f32[448,256]{1,0:T(8,128)S(1)}, u32[]{:S(2)}, u32[]{:S(2)}) collective-permute-start(f32[448,256]{1,0:T(8,128)S(1)} %constant_dynamic-slice_fusion), channel_id=1, source_target_pairs={{0,1},{1,0},{2,3},{3,2},{4,5},{5,4},{6,7},{7,6},{8,9},{9,8},{10,11... | collective-permute-start | bytes 1376264 | tf_op jit(solution)/shard_map/ppermute | solution.py:87
  198.7 1.6 copy-start.1
  198.7 1.6 copy-start.3
  198.7 1.6 copy-start.4

commit v2 on v1

--- a/solution.py
+++ b/solution.py
@@ -3,6 +3,8 @@
 import jax
 import jax.numpy as jnp
 from jax import lax
+from jax.experimental import pallas as pl
+from jax.experimental.pallas import tpu as pltpu
 from jax.sharding import PartitionSpec as P
 
 AXES = ("dp", "fsdp")
@@ -83,8 +85,26 @@
     return found
 
 
-def send(value, move):
-    return lax.ppermute(value, AXES, pairs_of(move))
+def send(value, move, name="exchange"):
+    with jax.named_scope(name):
+        return lax.ppermute(value, AXES, pairs_of(move))
+
+
+def after(value, *earlier):
+    return lax.optimization_barrier((value, *earlier))[0]
+
+
+class Order:
+    def __init__(self, token):
+        self.token = token
+
+    def wait(self, *values):
+        *values, self.token = lax.optimization_barrier((*values, self.token))
+        return values if len(values) > 1 else values[0]
+
+    def run(self, operation, *values):
+        *values, self.token = lax.optimization_barrier((*values, self.token))
+        return self.wait(operation(*values))
 
 
 def to_core(y, z, x, c):
@@ -107,14 +127,151 @@
     return to_y(y, z, x, c) if c == 0 else to_x(y, z, x, c)
 
 
+def to_corner(y, z, x, c):
+    return to_x(y, z, x, c) if c == 0 else to_y(y, z, x, c)
+
+
 def to_z(steps):
     return lambda y, z, x, c: (y, steps[z], x, c) if z in steps else None
 
 
-Z_PAIR = to_z({0: 1, 1: 0, 2: 3, 3: 2})
+Z_ONE = to_z({0: 1, 1: 0, 2: 3, 3: 2})
+Z_IN = to_z({0: 1, 3: 2})
 Z_MIDDLE = to_z({1: 2, 2: 1})
 Z_OUT = to_z({1: 0, 2: 3})
-Z_IN = to_z({0: 1, 3: 2})
+
+
+VMEM = pl.BlockSpec(memory_space=pltpu.VMEM)
+SMEM = pl.BlockSpec(memory_space=pltpu.SMEM)
+
+
+def call(kernel, outs, scalars, *operands, name):
+    return pl.pallas_call(
+        kernel,
+        out_shape=outs,
+        in_specs=[SMEM] + [VMEM] * len(operands),
+        out_specs=jax.tree.map(lambda _: VMEM, outs),
+        cost_estimate=pl.CostEstimate(flops=10**9, bytes_accessed=10**7, transcendentals=0),
+        compiler_params=pltpu.CompilerParams(vmem_limit_bytes=24 * 2**20),
+        name=name,
+    )(jnp.stack(scalars).astype(jnp.int32), *operands)
+
+
+def dot(left, right):
+    return jnp.dot(left, right, preferred_element_type=jnp.float32)
+
+
+def halves(tokens):
+    half = tokens.shape[0] // 2
+    return pl.ds(0, half), pl.ds(half, half)
+
+
+def spread(block, x, core, rights, tokens_ref, got_ref, kept_ref):
+    width = rights[0].shape[0] // 2
+    depth = got_ref.shape[2]
+    own_first = core == 0
+    for begin in range(0, depth, 256):
+        size = min(256, depth - begin)
+        out = pl.ds(begin, size)
+
+        def products(place):
+            at = pl.ds(pl.multiple_of((2 * block + place) * depth, 128) + begin, size)
+            return sum(
+                dot(right[...], tokens_ref[rows, at])
+                for right, rows in zip(rights, halves(tokens_ref))
+            )
+
+        near, far = products(x), products(1 - x)
+        second = jnp.where(own_first, near[width:], far[:width])
+        first = jnp.where(own_first, far[:width], near[width:])
+        got_ref[0, :, out] = far[width:].astype(jnp.bfloat16)
+        got_ref[1, :, out] = second.astype(jnp.bfloat16)
+        kept_ref[0, :, out] = first
+        kept_ref[1, :, out] = near[:width]
+
+
+def spread_shapes(width, depth):
+    return [
+        jax.ShapeDtypeStruct((2, width, depth), jnp.bfloat16),
+        jax.ShapeDtypeStruct((2, width, depth), jnp.float32),
+    ]
+
+
+def contract(scalars, depth, tokens, right_a, right_b):
+    def kernel(at_ref, tokens_ref, right_a, right_b, got_ref, kept_ref):
+        place = at_ref[0], at_ref[1], at_ref[2]
+        spread(*place, (right_a, right_b), tokens_ref, got_ref, kept_ref)
+
+    shapes = spread_shapes(right_a.shape[0] // 2, depth)
+    return call(kernel, shapes, scalars, tokens, right_a, right_b, name="contract")
+
+
+def head_gradients(scalars, depth, tokens, sums, own_up, other_up, norm_gain):
+    half = tokens.shape[0] // 2
+    width = sums[0].shape[1]
+    head = norm_gain.shape[0]
+
+    def kernel(
+        at_ref, tokens_ref, own_ref, both_ref, first_ref, second_ref, up_a, up_b, gain_ref,
+        right_a, right_b, got_ref, kept_ref,
+    ):
+        gain = gain_ref[...]
+        own_first = at_ref[2] == 0
+        for part, (up, right) in enumerate(((up_a, right_a), (up_b, right_b))):
+            for begin in range(0, half, 128):
+                size = min(128, half - begin)
+                within = pl.ds(begin, size)
+                at = pl.ds(part * half + begin, size)
+                weighted = up[within, :].astype(jnp.float32)
+                first, second = first_ref[at, :], second_ref[at, :]
+                here = own_ref[at, :] + jnp.where(own_first, first, second)
+                there = both_ref[at, :] + jnp.where(own_first, second, first)
+                for side, product in enumerate((here, there)):
+                    pair = head_terms(
+                        product[:, :head],
+                        product[:, head:],
+                        weighted[:, side * head : (side + 1) * head] * gain,
+                    )
+                    for i, value in enumerate(pair):
+                        features = pl.ds((2 * side + i) * head, head)
+                        right[features, within] = value.T.astype(jnp.bfloat16)
+        place = at_ref[0], at_ref[1], at_ref[2]
+        spread(*place, (right_a, right_b), tokens_ref, got_ref, kept_ref)
+
+    return call(
+        kernel,
+        [jax.ShapeDtypeStruct((2 * width, half), jnp.bfloat16)] * 2 + spread_shapes(width, depth),
+        scalars,
+        tokens,
+        *sums,
+        own_up,
+        other_up,
+        norm_gain.reshape(1, head),
+        name="head_gradients",
+    )
+
+
+def by_rows(kept, got, *terms):
+    width, depth = terms[0].shape
+    terms = (kept, got, *terms)
+
+    def kernel(kept_ref, got_ref, *refs):
+        *term_refs, out_ref = refs
+        for begin in range(0, depth, 128):
+            size = min(128, depth - begin)
+            at = pl.ds(begin, size)
+            total = kept_ref[1, :, at] + got_ref[1, :, at].astype(jnp.float32)
+            for ref in term_refs:
+                total += ref[:, at].astype(jnp.float32)
+            out_ref[at, :] = total.T
+
+    return pl.pallas_call(
+        kernel,
+        out_shape=jax.ShapeDtypeStruct((depth, width), jnp.float32),
+        in_specs=[VMEM] * len(terms),
+        out_specs=VMEM,
+        name="by_rows",
+    )(*terms)
 
 
 def by_links(acts, upstream, k_weight, probe, norm_gain, momentum, curvature):
@@ -132,14 +289,13 @@
 
     leaving = jnp.concatenate(weights_for(1 - c, y) + weights_for(1 - c, 1 - y), axis=1)
     staying = jnp.concatenate(weights_for(c, y) + weights_for(c, 1 - y), axis=1)
-    coming = send(leaving, to_core)
-    other_acts = send(acts, to_core)
-    other_up = send(
-        jnp.concatenate(
-            [column(upstream, 2 * y + 1 - c), column(upstream, 2 * (1 - y) + 1 - c)], axis=1
-        ),
-        to_core,
-    )
+    coming = send(leaving, to_core, "coming")
+    def upstream_for(core):
+        return jnp.concatenate(
+            [column(upstream, 2 * y + core), column(upstream, 2 * (1 - y) + core)], axis=1
+        )
+
+    own_up, other_up = upstream_for(c), send(upstream_for(1 - c), to_core, "other_up")
     chip_rows = jnp.where(
         own_first,
         jnp.concatenate([staying, coming], axis=0),
@@ -147,86 +303,116 @@
     )
     mine, beside = chip_rows[:, : 2 * head], chip_rows[:, 2 * head :]
 
-    one = send(mine, Z_PAIR)
-    near = send(mine, Z_MIDDLE)
-    two = send(near, Z_OUT) + send(one, Z_MIDDLE)
-    three = near + send(two, Z_OUT)
-
-    across = send(mine, to_x)
-    units = [(mine, across, beside, send(across, to_y))]
-    for held in (one, two, three):
-        first = send(held, to_first)
-        units.append((held, first, send(held, to_second), send(first, to_second)))
-
-    all_acts = jnp.concatenate([acts, other_acts], axis=0)
-
-    def block_of(slot, flip_x):
+    order = Order(momentum)
+    other_acts = send(after(acts, chip_rows), to_core, "other_acts")
+    one = send(mine, Z_ONE, "one")
+    near = send(mine, Z_MIDDLE, "near")
+    across = send(mine, to_x, "across")
+    other_up = order.wait(other_up)
+    one, near = order.wait(one, near)
+    two_out = send(near, Z_OUT, "two_out")
+    two_in = send(one, Z_MIDDLE, "two_in")
+    other_acts, one = order.wait(other_acts, one)
+    one_first = send(one, to_first, "one_first")
+    one_second = send(one, to_second, "one_second")
+    corner = order.run(lambda a, b: jnp.where(own_first, a, b), beside, across)
+    corner = send(corner, to_corner, "corner")
+    tokens = order.run(lambda a, b: jnp.concatenate([a, b], axis=0), acts, other_acts)
+
+    def block_of(held, slot, flip_x):
         start = ((z ^ slot) * 2 + (x ^ flip_x)) * (2 * rows)
-        return lax.dynamic_slice_in_dim(all_acts, start, 2 * rows, 1)
-
-    def dot(left, right):
-        return jnp.dot(left, right, preferred_element_type=jnp.float32)
-
-    here = there = None
-    for slot in range(4):
-        own, first, second, both = units[slot]
-        if slot == 0:
-            flip_y, flip_x = second, first
-        else:
-            flip_x = jnp.where(own_first, first, second)
-            flip_y = jnp.where(own_first, second, first)
-        near_x, far_x = block_of(slot, 0), block_of(slot, 1)
-        a = dot(near_x, own) + dot(far_x, flip_x)
-        b = dot(near_x, flip_y) + dot(far_x, both)
-        here = a if here is None else here + a
-        there = b if there is None else there + b
-
-    def stacked(projections, side, other):
-        weighted = (
-            jnp.concatenate([column(upstream, 2 * side + c), other], axis=0).astype(jnp.float32)
-            * norm_gain
-        )
-        pair = head_terms(projections[:, :head], projections[:, head:], weighted)
-        return jnp.concatenate(pair, axis=1).astype(jnp.bfloat16)
-
-    right_here = stacked(here, y, other_up[:, :head])
-    right_there = stacked(there, 1 - y, other_up[:, head:])
-    right_first = jnp.where(own_first, right_here, right_there)
-    right_second = jnp.where(own_first, right_there, right_here)
-
-    def partial(slot, flip_x, right):
-        return contract_tokens(block_of(slot, flip_x), right).astype(jnp.bfloat16)
-
-    def plus(*terms):
-        total = terms[0].astype(jnp.float32)
-        for term in terms[1:]:
-            total = total + term.astype(jnp.float32)
-        return total.astype(jnp.bfloat16)
-
-    def over_plane(slot):
-        far = partial(slot, 1, right_there)
-        second = partial(slot, c, right_second)
-        first = partial(slot, 1 - c, right_first)
-        own = partial(slot, 0, right_here)
-        first = plus(first, send(far, to_second))
-        return own, send(second, to_second), send(first, to_first)
-
-    three = plus(*over_plane(3))
-    two = plus(*over_plane(2), send(three, Z_IN))
-    three = plus(three, send(two, Z_IN))
-    one = plus(*over_plane(1), send(two, Z_MIDDLE))
-    owned = over_plane(0) + (send(three, Z_MIDDLE), send(one, Z_PAIR))
-    owned = functools.reduce(lambda s, t: s + t.astype(jnp.float32), owned, jnp.float32(0))
+        return lax.dynamic_slice_in_dim(held, start, 2 * rows, 1)
+
+    def add_product(total, slot, flip_x, unit):
+        def product(unit, held, *before):
+            found = jnp.dot(block_of(held, slot, flip_x), unit, preferred_element_type=jnp.float32)
+            return sum(before, found)
+
+        return order.run(product, unit, tokens, *(() if total is None else (total,)))
+
+    own_sum = add_product(None, 0, 0, mine)
+    both_sum = add_product(None, 0, 0, beside)
+    own_sum = add_product(own_sum, 0, 1, across)
+    two_out, two_in = order.wait(two_out, two_in)
+    two = order.run(jnp.add, two_out, two_in)
+    three_out = send(two, Z_OUT, "three_out")
+    two_first = send(two, to_first, "two_first")
+    own_sum = add_product(own_sum, 1, 0, one)
+    one_first = order.wait(one_first)
+    one_both = send(one_first, to_second, "one_both")
+    corner, two = order.wait(corner, two)
+    two_second = send(two, to_second, "two_second")
+    both_sum = add_product(both_sum, 0, 1, corner)
+    first_sum = add_product(None, 1, 1 - c, one_first)
+    second_sum = add_product(None, 1, c, one_second)
+    own_sum = add_product(own_sum, 2, 0, two)
+    three = order.run(jnp.add, near, three_out)
+    three_first = send(three, to_first, "three_first")
+    three_second = send(three, to_second, "three_second")
+    both_sum = add_product(both_sum, 1, 1, one_both)
+    two_first = order.wait(two_first)
+    two_both = send(two_first, to_second, "two_both")
+    first_sum = add_product(first_sum, 2, 1 - c, two_first)
+    own_sum = add_product(own_sum, 3, 0, three)
+    second_sum = add_product(second_sum, 2, c, two_second)
+    three_first = order.wait(three_first)
+    three_both = send(three_first, to_second, "three_both")
+    first_sum = add_product(first_sum, 3, 1 - c, three_first)
+    both_sum = add_product(both_sum, 2, 1, two_both)
+    second_sum = add_product(second_sum, 3, c, three_second)
+    both_sum = add_product(both_sum, 3, 1, three_both)
+
+    sums = (own_sum, both_sum, first_sum, second_sum)
+    right_a, right_b, leaving_3, kept_3 = head_gradients(
+        (z ^ 3, x, c), 2 * rows, tokens, sums, own_up, other_up, norm_gain
+    )
+
+    def partial(slot):
+        def product(*operands):
+            return contract((z ^ slot, x, c), 2 * rows, *operands)
+
+        return order.run(product, tokens, right_a, right_b)
+
+    def total_of(*terms):
+        return sum((t.astype(jnp.float32) for t in terms[1:]), terms[0].astype(jnp.float32))
+
+    def rounded(part, kept, got, *more):
+        def total(kept, got, *more):
+            return total_of(kept[part], got[part], *more).astype(jnp.bfloat16)
+
+        return order.run(total, kept, got, *more)
+
+    seconds_3 = send(leaving_3, to_second, "seconds_3")
+    leaving_2, kept_2 = partial(2)
+    seconds_2 = send(leaving_2, to_second, "seconds_2")
+    leaving_1, kept_1 = partial(1)
+    seconds_1 = send(leaving_1, to_second, "seconds_1")
+    leaving_0, kept_0 = partial(0)
+    seconds_0 = send(leaving_0, to_second, "seconds_0")
+    first_3 = send(rounded(0, kept_3, seconds_3), to_first, "first_3")
+    first_2 = send(rounded(0, kept_2, seconds_2), to_first, "first_2")
+    sum_3 = rounded(1, kept_3, seconds_3, first_3)
+    three_in = send(sum_3, Z_IN, "three_in")
+    first_1 = send(rounded(0, kept_1, seconds_1), to_first, "first_1")
+    sum_2 = rounded(1, kept_2, seconds_2, first_2, three_in)
+    two_in = send(sum_2, Z_IN, "two_in")
+    two = send(sum_2, Z_MIDDLE, "two")
+    sum_3 = order.run(lambda *t: total_of(*t).astype(jnp.bfloat16), sum_3, two_in)
+    three = send(sum_3, Z_MIDDLE, "three")
+    two = order.wait(two)
+    one = send(rounded(1, kept_1, seconds_1, first_1, two), Z_ONE, "one")
+    first_0 = send(rounded(0, kept_0, seconds_0), to_first, "first_0")
+    owned = order.run(by_rows, kept_0, seconds_0, three, first_0, one)
 
     kept = lax.dynamic_slice_in_dim(owned, c * rows, rows, 0)
     given = lax.dynamic_slice_in_dim(owned, (1 - c) * rows, rows, 0)
-    taken = send(given, to_core)
+    taken = send(given, to_core, "taken")
     left = jnp.where(own_first, kept, taken)
     right = jnp.where(own_first, taken, kept)
     grad_share = jnp.concatenate([left[:, :head], right[:, :head]], axis=1)
     hvp_share = jnp.concatenate([left[:, head:], right[:, head:]], axis=1)
     probe_cols = lax.dynamic_slice_in_dim(probe, y * 2 * head, 2 * head, 1).astype(jnp.float32)
-    return step_outputs(momentum, curvature, probe_cols, grad_share, hvp_share)
+    return step_outputs(order.token, curvature, probe_cols, grad_share, hvp_share)
 
 
 def solution(mesh):

time: 202 us -> 170 us (0.84); the launches traced: 202 us -> 167 us
  starting transfers between devices: 64.5 us -> 40.3 us
  matrix products: 32.5 us -> 10.3 us
  Pallas kernels: 0 us -> 16.7 us
  local copies, waits for them, and re-layouts: 14.8 us -> 4.44 us
  other arithmetic: 6.65 us -> 11.8 us
    ppermute x37 -> x33, starting transfers between devices: 64.5 us -> 40.3 us  [send(): return lax.ppermute(value, AXES, pairs_of(move))]
    dot_general x32 -> x16, matrix products: 32.5 us -> 10.3 us  [product(): jnp.dot(block_of(held, slot, flip_x), unit, preferred_element_type=jnp.fl...]
    pallas_call x0 -> x5, Pallas kernels: none -> 16.7 us  [the longest x4 13.4 us: call(): pl.pallas_call(kernel, out_shape=outs, in_specs=[SMEM] + [VMEM] * len(ope...]
    unnamed x25 -> x18, local copies, waits for them, and re-layouts: 7.29 us -> 0.79 us
    concatenate x1 -> x3, other arithmetic: 0.73 us -> 6.83 us  [the longest x1 6.77 us: by_links(): jnp.concatenate([a, b], axis=0)]
    concatenate x1 -> x0, local copies, waits for them, and re-layouts: 5.96 us -> none  [by_links(): all_acts = jnp.concatenate([acts, other_acts], axis=0)]
    add x2, other arithmetic: 2.39 us -> 0.26 us  [run(): return self.wait(operation(*values))]
    ppermute x37 -> x33, waiting for transfers between devices: 81.8 us -> 82.5 us  [send(): return lax.ppermute(value, AXES, pairs_of(move))]
  transfers between devices with their start and end apart: 37 -> 33, of which waited for: 19 -> 19; matrix products, arithmetic and copies ran while one was open for 24% -> 11% of each run, Pallas kernels for 0% -> 5%
where the time goes in v2:
time: 170 us; the launch traced here: 167 us
  waiting for transfers between devices  82.5 us (49%)
  starting transfers between devices  40.3 us (24%)
  Pallas kernels  16.7 us (10%)
  other arithmetic  11.8 us (7%)
  matrix products  10.3 us (6%)
  local copies, waits for them, and re-layouts  4.44 us (3%)
    ppermute x33, waiting for transfers between devices, send(): return lax.ppermute(value, AXES, pairs_of(move))  82.5 us
    ppermute x33, starting transfers between devices, send(): return lax.ppermute(value, AXES, pairs_of(move))  40.3 us
    pallas_call x4, Pallas kernels, call(): pl.pallas_call(kernel, out_shape=outs, in_specs=[SMEM] + [VMEM] * len(ope...  13.4 us
    dot_general x16, matrix products, product(): jnp.dot(block_of(held, slot, flip_x), unit, preferred_element_type=jnp.fl...  10.3 us
    concatenate x1, other arithmetic, by_links(): jnp.concatenate([a, b], axis=0)  6.77 us
  transfers between devices with their start and end apart: 33, of which 19 were waited for; matrix products, arithmetic and copies ran while one was open for 11% of the time, Pallas kernels for 5%

profile of v2, /device:TPU:11, one launch (start us, length us, event | category | flops | bytes accessed | tf_op | source)
XLA Modules:
  0.0 167.2 jit_solution(17633722238850257566)
XLA Ops:
  0.7 1.1 constant_dynamic-slice_fusion.12
  1.8 1.4 constant_dynamic-slice_fusion.2
  4.0 1.4 collective-permute-done
  6.3 3.2 %collective-permute-start.3 = (bf16[896,256]{1,0:T(8,128)(2,1)S(1)}, bf16[896,256]{1,0:T(8,128)(2,1)S(1)}, u32[]{:S(2)}, u32[]{:S(2)}) collective-permute-start(bf16[896,256]{1,0:T(8,128)(2,1)S(1)} %get-tuple-element.236), channel_id=1, source_target_pairs={{4,8},{5,9},{6,10},{7,11},{8,4},{9,5},{10,6},{11,7},{20,24},{21,25... | collective-permute-start | bytes 1376264 | tf_op jit(solution)/shard_map/near/ppermute | solution.py:90
  10.8 5.7 %collective-permute-done.4.up_b = bf16[448,256]{1,0:T(8,128)(2,1)S(1)} collective-permute-done((bf16[448,256]{1,0:T(8,128)(2,1)S(1)}, bf16[448,256]{1,0:T(8,128)(2,1)S(1)}, u32[]{:S(2)}, u32[]{:S(2)}) %collective-permute-start.4) | collective-permute-done | bytes 229408 | tf_op jit(solution)/shard_map/other_up/ppermute | solution.py:90
  16.5 3.6 %collective-permute-done.3 = bf16[896,256]{1,0:T(8,128)(2,1)S(1)} collective-permute-done((bf16[896,256]{1,0:T(8,128)(2,1)S(1)}, bf16[896,256]{1,0:T(8,128)(2,1)S(1)}, u32[]{:S(2)}, u32[]{:S(2)}) %collective-permute-start.3) | collective-permute-done | bytes 458784 | tf_op jit(solution)/shard_map/near/ppermute | solution.py:90
  20.2 1.1 collective-permute-done.2
  21.2 2.1 %collective-permute-start.7 = (bf16[896,256]{1,0:T(8,128)(2,1)S(1)}, bf16[896,256]{1,0:T(8,128)(2,1)S(1)}, u32[]{:S(2)}, u32[]{:S(2)}) collective-permute-start(bf16[896,256]{1,0:T(8,128)(2,1)S(1)} %collective-permute-done.2), channel_id=1, source_target_pairs={{4,8},{5,9},{6,10},{7,11},{8,4},{9,5},{10,6},{11,7},{20,24},{21,25... | collective-permute-start | bytes 1376264 | tf_op jit(solution)/shard_map/two_in/ppermute | solution.py:90
  23.4 1.3 collective-permute-start.6
  25.0 1.2 collective-permute-start.10
  26.6 6.8 %pad_maximum_fusion.tokens_ref = bf16[896,7168]{1,0:T(8,128)(2,1)S(1)} fusion(bf16[448,7168]{1,0:T(8,128)(2,1)} %collective-permute-done.1, bf16[448,7168]{1,0:T(8,128)(2,1)} %param.7), kind=kLoop, calls=%fused_computation | loop fusion | flops 25690112 | bytes 25690112 | tf_op jit(solution)/shard_map/concatenate | solution.py:320
  35.5 1.3 collective-permute-start.12
  36.8 2.2 %collective-permute-start.8 = (bf16[896,256]{1,0:T(8,128)(2,1)S(1)}, bf16[896,256]{1,0:T(8,128)(2,1)S(1)}, u32[]{:S(2)}, u32[]{:S(2)}) collective-permute-start(bf16[896,256]{1,0:T(8,128)(2,1)S(1)} %add.261), channel_id=1, source_target_pairs={{4,0},{5,1},{6,2},{7,3},{8,12},{9,13},{10,14},{11,15},{20,16},{21,... | collective-permute-start | bytes 1376264 | tf_op jit(solution)/shard_map/three_out/ppermute | solution.py:90
  39.7 2.8 %collective-permute-done.9 = bf16[896,256]{1,0:T(8,128)(2,1)S(1)} collective-permute-done((bf16[896,256]{1,0:T(8,128)(2,1)S(1)}, bf16[896,256]{1,0:T(8,128)(2,1)S(1)}, u32[]{:S(2)}, u32[]{:S(2)}) %collective-permute-start.9) | collective-permute-done | bytes 458784 | tf_op jit(solution)/shard_map/corner/ppermute | solution.py:90
  43.1 1.3 collective-permute-start.13
  47.1 1.0 collective-permute-start.18
  48.1 1.2 collective-permute-start.14
  49.3 2.7 %collective-permute-done.13 = bf16[896,256]{1,0:T(8,128)(2,1)S(1)} collective-permute-done((bf16[896,256]{1,0:T(8,128)(2,1)S(1)}, bf16[896,256]{1,0:T(8,128)(2,1)S(1)}, u32[]{:S(2)}, u32[]{:S(2)}) %collective-permute-start.13) | collective-permute-done | bytes 458784 | tf_op jit(solution)/shard_map/one_both/ppermute | solution.py:90
  54.4 6.1 %collective-permute-done.15 = bf16[896,256]{1,0:T(8,128)(2,1)S(1)} collective-permute-done((bf16[896,256]{1,0:T(8,128)(2,1)S(1)}, bf16[896,256]{1,0:T(8,128)(2,1)S(1)}, u32[]{:S(2)}, u32[]{:S(2)}) %collective-permute-start.15) | collective-permute-done | bytes 458784 | tf_op jit(solution)/shard_map/two_second/ppermute | solution.py:90
  61.9 9.8 %collective-permute-done.17 = bf16[896,256]{1,0:T(8,128)(2,1)S(1)} collective-permute-done((bf16[896,256]{1,0:T(8,128)(2,1)S(1)}, bf16[896,256]{1,0:T(8,128)(2,1)S(1)}, u32[]{:S(2)}, u32[]{:S(2)}) %collective-permute-start.17) | collective-permute-done | bytes 458784 | tf_op jit(solution)/shard_map/two_both/ppermute | solution.py:90
  73.0 3.6 %collective-permute-done.16 = bf16[896,256]{1,0:T(8,128)(2,1)S(1)} collective-permute-done((bf16[896,256]{1,0:T(8,128)(2,1)S(1)}, bf16[896,256]{1,0:T(8,128)(2,1)S(1)}, u32[]{:S(2)}, u32[]{:S(2)}) %collective-permute-start.16) | collective-permute-done | bytes 458784 | tf_op jit(solution)/shard_map/three_both/ppermute | solution.py:90
  77.3 4.4 %head_gradients.1 = (bf16[512,448]{1,0:T(8,128)(2,1)S(1)}, bf16[512,448]{1,0:T(8,128)(2,1)S(1)}, bf16[2,256,896]{2,1,0:T(8,128)(2,1)S(1)}, f32[2,256,896]{2,1,0:T(8,128)S(1)}) custom-call(s32[3]{0:T(128)S(1)} %get-tuple-element.459.at_ref, bf16[896,7168]{1,0:T(8,128)(2,1)S(1)} %pad_maximum_fusion.tokens_ref, f32[896,256]{1,0:T(8,128)S(1)} %fusion.50.own_ref, ...), custom_call_target="tpu_custom_call" | custom-call | flops 1000000000 | bytes 10000000 | tf_op jit(solution)/shard_map/head_gradients/pallas_call | solution.py:149
  82.1 2.9 %contract.3 = (bf16[2,256,896]{2,1,0:T(8,128)(2,1)S(1)}, f32[2,256,896]{2,1,0:T(8,128)S(1)}) custom-call(s32[3]{0:T(128)S(1)} %get-tuple-element.461.at_ref, bf16[896,7168]{1,0:T(8,128)(2,1)S(1)} %pad_maximum_fusion.tokens_ref, bf16[512,448]{1,0:T(8,128)(2,1)S(1)} %get-tuple-element.366.right_a, bf16[512,448]{1,0:T(8,128)(2,1)S(1)} %get-tuple-element.367.right_b), custom_call_target="tpu_custom_call" | custom-call | flops 1000000000 | bytes 10000000 | tf_op jit(solution)/shard_map/contract/pallas_call | solution.py:149
  85.1 1.3 collective-permute-start.22
  86.3 3.1 %contract.4 = (bf16[2,256,896]{2,1,0:T(8,128)(2,1)S(1)}, f32[2,256,896]{2,1,0:T(8,128)S(1)}) custom-call(s32[3]{0:T(128)S(1)} %get-tuple-element.460.at_ref, bf16[896,7168]{1,0:T(8,128)(2,1)S(1)} %pad_maximum_fusion.tokens_ref, bf16[512,448]{1,0:T(8,128)(2,1)S(1)} %get-tuple-element.366.right_a, bf16[512,448]{1,0:T(8,128)(2,1)S(1)} %get-tuple-element.367.right_b), custom_call_target="tpu_custom_call" | custom-call | flops 1000000000 | bytes 10000000 | tf_op jit(solution)/shard_map/contract/pallas_call | solution.py:149
  89.5 2.9 %contract.5 = (bf16[2,256,896]{2,1,0:T(8,128)(2,1)S(1)}, f32[2,256,896]{2,1,0:T(8,128)S(1)}) custom-call(s32[3]{0:T(128)S(1)} %get-tuple-element.458.at_ref, bf16[896,7168]{1,0:T(8,128)(2,1)S(1)} %pad_maximum_fusion.tokens_ref, bf16[512,448]{1,0:T(8,128)(2,1)S(1)} %get-tuple-element.366.right_a, bf16[512,448]{1,0:T(8,128)(2,1)S(1)} %get-tuple-element.367.right_b), custom_call_target="tpu_custom_call" | custom-call | flops 1000000000 | bytes 10000000 | tf_op jit(solution)/shard_map/contract/pallas_call | solution.py:149
  92.4 1.9 %collective-permute-done.20 = bf16[2,256,896]{2,1,0:T(8,128)(2,1)S(1)} collective-permute-done((bf16[2,256,896]{2,1,0:T(8,128)(2,1)S(1)}, bf16[2,256,896]{2,1,0:T(8,128)(2,1)S(1)}, u32[]{:S(2)}, u32[]{:S(2)}) %collective-permute-start.20) | collective-permute-done | bytes 917536 | tf_op jit(solution)/shard_map/seconds_3/ppermute | solution.py:90
  94.4 1.3 collective-permute-start.21
  96.0 13.1 %collective-permute-done.22 = bf16[2,256,896]{2,1,0:T(8,128)(2,1)S(1)} collective-permute-done((bf16[2,256,896]{2,1,0:T(8,128)(2,1)S(1)}, bf16[2,256,896]{2,1,0:T(8,128)(2,1)S(1)}, u32[]{:S(2)}, u32[]{:S(2)}) %collective-permute-start.22) | collective-permute-done | bytes 917536 | tf_op jit(solution)/shard_map/seconds_2/ppermute | solution.py:90
  109.2 1.3 collective-permute-start.23
  110.7 1.3 collective-permute-start.24
  112.0 11.9 %collective-permute-done.25 = bf16[2,256,896]{2,1,0:T(8,128)(2,1)S(1)} collective-permute-done((bf16[2,256,896]{2,1,0:T(8,128)(2,1)S(1)}, bf16[2,256,896]{2,1,0:T(8,128)(2,1)S(1)}, u32[]{:S(2)}, u32[]{:S(2)}) %collective-permute-start.25) | collective-permute-done | bytes 917536 | tf_op jit(solution)/shard_map/seconds_1/ppermute | solution.py:90
  124.1 1.3 collective-permute-start.26
  125.5 3.2 %collective-permute-start.29 = (bf16[256,896]{1,0:T(8,128)(2,1)S(1)}, bf16[256,896]{1,0:T(8,128)(2,1)S(1)}, u32[]{:S(2)}, u32[]{:S(2)}) collective-permute-start(bf16[256,896]{1,0:T(8,128)(2,1)S(1)} %fusion.71), channel_id=1, source_target_pairs={{4,8},{5,9},{6,10},{7,11},{8,4},{9,5},{10,6},{11,7},{20,24},{21,25... | collective-permute-start | bytes 1376264 | tf_op jit(solution)/shard_map/two/ppermute | solution.py:90
  128.7 1.3 collective-permute-start.28
  130.0 6.5 %collective-permute-done.26 = bf16[256,896]{1,0:T(8,128)(2,1)S(1)} collective-permute-done((bf16[256,896]{1,0:T(8,128)(2,1)S(1)}, bf16[256,896]{1,0:T(8,128)(2,1)S(1)}, u32[]{:S(2)}, u32[]{:S(2)}) %collective-permute-start.26) | collective-permute-done | bytes 458784 | tf_op jit(solution)/shard_map/two_in/ppermute | solution.py:90
  136.6 3.2 %collective-permute-start.27 = (bf16[256,896]{1,0:T(8,128)(2,1)S(1)}, bf16[256,896]{1,0:T(8,128)(2,1)S(1)}, u32[]{:S(2)}, u32[]{:S(2)}) collective-permute-start(bf16[256,896]{1,0:T(8,128)(2,1)S(1)} %add_convert_fusion.1), channel_id=1, source_target_pairs={{4,8},{5,9},{6,10},{7,11},{8,4},{9,5},{10,6},{11,7},{20,24},{21,25... | collective-permute-start | bytes 1376264 | tf_op jit(solution)/shard_map/three/ppermute | solution.py:90
  139.8 1.5 collective-permute-done.28
  142.4 1.3 collective-permute-start.30
  143.7 2.8 %collective-permute-start.31 = (bf16[256,896]{1,0:T(8,128)(2,1)}, bf16[256,896]{1,0:T(8,128)(2,1)S(1)}, u32[]{:S(2)}, u32[]{:S(2)}) collective-permute-start(bf16[256,896]{1,0:T(8,128)(2,1)} %fusion.69), channel_id=1, source_target_pairs={{0,4},{1,5},{2,6},{3,7},{4,0},{5,1},{6,2},{7,3},{8,12},{9,13},{10,... | collective-permute-start | bytes 1376264 | tf_op jit(solution)/shard_map/one/ppermute | solution.py:90
  146.8 3.3 %collective-permute-done.30.refs_1_ = bf16[256,896]{1,0:T(8,128)(2,1)S(1)} collective-permute-done((bf16[256,896]{1,0:T(8,128)(2,1)S(1)}, bf16[256,896]{1,0:T(8,128)(2,1)S(1)}, u32[]{:S(2)}, u32[]{:S(2)}) %collective-permute-start.30) | collective-permute-done | bytes 458784 | tf_op jit(solution)/shard_map/first_0/ppermute | solution.py:90
  150.1 5.2 %collective-permute-done.31.refs_2_ = bf16[256,896]{1,0:T(8,128)(2,1)S(1)} collective-permute-done((bf16[256,896]{1,0:T(8,128)(2,1)}, bf16[256,896]{1,0:T(8,128)(2,1)S(1)}, u32[]{:S(2)}, u32[]{:S(2)}) %collective-permute-start.31) | collective-permute-done | bytes 458784 | tf_op jit(solution)/shard_map/one/ppermute | solution.py:90
  156.0 3.4 %by_rows.1 = f32[896,256]{1,0:T(8,128)} custom-call(f32[2,256,896]{2,1,0:T(8,128)} %copy-done, bf16[2,256,896]{2,1,0:T(8,128)(2,1)} %copy-done.2, bf16[256,896]{1,0:T(8,128)(2,1)} %copy-done.4, bf16[256,896]{1,0:T(8,128)(2,1)} %copy-done.5, bf16[256,896]{1,0:T(8,128)(2,1)} %copy-done.6), custom_call_target="tpu_custom_call" | custom-call | tf_op jit(solution)/shard_map/by_rows/pallas_call | solution.py:268
  159.4 1.0 constant_dynamic-slice_fusion
  160.5 3.0 %collective-permute-start.32 = (f32[448,256]{1,0:T(8,128)S(1)}, f32[448,256]{1,0:T(8,128)S(1)}, u32[]{:S(2)}, u32[]{:S(2)}) collective-permute-start(f32[448,256]{1,0:T(8,128)S(1)} %constant_dynamic-slice_fusion), channel_id=1, source_target_pairs={{0,1},{1,0},{2,3},{3,2},{4,5},{5,4},{6,7},{7,6},{8,9},{9,8},{10,11... | collective-permute-start | bytes 1376264 | tf_op jit(solution)/shard_map/taken/ppermute | solution.py:90
  163.4 1.4 collective-permute-done.32
  164.9 1.1 dynamic-slice_select_fusion.1
  166.1 1.2 divide_clamp_fusion
  (83 shorter events, 19.0 us)
Async XLA Ops:
  3.2 2.2 %collective-permute-start = (bf16[448,512]{1,0:T(8,128)(2,1)S(1)}, bf16[448,512]{1,0:T(8,128)(2,1)S(1)}, u32[]{:S(2)}, u32[]{:S(2)}) collective-permute-start(bf16[448,512]{1,0:T(8,128)(2,1)S(1)} %pad_maximum_fusion.1), channel_id=1, source_target_pairs={{0,1},{1,0},{2,3},{3,2},{4,5},{5,4},{6,7},{7,6},{8,9},{9,8},{10,11... | collective-permute-start | bytes 1376264 | tf_op jit(solution)/shard_map/coming/ppermute | solution.py:90
  5.8 18.9 %collective-permute-start.1 = (bf16[448,7168]{1,0:T(8,128)(2,1)}, bf16[448,7168]{1,0:T(8,128)(2,1)}, u32[]{:S(2)}, u32[]{:S(2)}) collective-permute-start(bf16[448,7168]{1,0:T(8,128)(2,1)} %param.7), channel_id=1, source_target_pairs={{0,1},{1,0},{2,3},{3,2},{4,5},{5,4},{6,7},{7,6},{8,9},{9,8},{10,11... | collective-permute-start | bytes 19267592 | tf_op jit(solution)/shard_map/other_acts/ppermute | solution.py:90
  6.3 13.9 %collective-permute-start.3 = (bf16[896,256]{1,0:T(8,128)(2,1)S(1)}, bf16[896,256]{1,0:T(8,128)(2,1)S(1)}, u32[]{:S(2)}, u32[]{:S(2)}) collective-permute-start(bf16[896,256]{1,0:T(8,128)(2,1)S(1)} %get-tuple-element.236), channel_id=1, source_target_pairs={{4,8},{5,9},{6,10},{7,11},{8,4},{9,5},{10,6},{11,7},{20,24},{21,25... | collective-permute-start | bytes 1376264 | tf_op jit(solution)/shard_map/near/ppermute | solution.py:90
  9.5 11.7 %collective-permute-start.2 = (bf16[896,256]{1,0:T(8,128)(2,1)S(1)}, bf16[896,256]{1,0:T(8,128)(2,1)S(1)}, u32[]{:S(2)}, u32[]{:S(2)}) collective-permute-start(bf16[896,256]{1,0:T(8,128)(2,1)S(1)} %get-tuple-element.236), channel_id=1, source_target_pairs={{0,4},{1,5},{2,6},{3,7},{4,0},{5,1},{6,2},{7,3},{8,12},{9,13},{10,... | collective-permute-start | bytes 1376264 | tf_op jit(solution)/shard_map/one/ppermute | solution.py:90
  9.6 16.7 %collective-permute-start.5 = (bf16[896,256]{1,0:T(8,128)(2,1)S(1)}, bf16[896,256]{1,0:T(8,128)(2,1)S(1)}, u32[]{:S(2)}, u32[]{:S(2)}) collective-permute-start(bf16[896,256]{1,0:T(8,128)(2,1)S(1)} %get-tuple-element.236), channel_id=1, source_target_pairs={{0,2},{1,3},{2,0},{3,1},{4,6},{5,7},{6,4},{7,5},{8,10},{9,11},{10,... | collective-permute-start | bytes 1376264 | tf_op jit(solution)/shard_map/across/ppermute | solution.py:90
  9.9 6.6 %collective-permute-start.4 = (bf16[448,256]{1,0:T(8,128)(2,1)S(1)}, bf16[448,256]{1,0:T(8,128)(2,1)S(1)}, u32[]{:S(2)}, u32[]{:S(2)}) collective-permute-start(bf16[448,256]{1,0:T(8,128)(2,1)S(1)} %pad_maximum_fusion.2), channel_id=1, source_target_pairs={{0,1},{1,0},{2,3},{3,2},{4,5},{5,4},{6,7},{7,6},{8,9},{9,8},{10,11... | collective-permute-start | bytes 688136 | tf_op jit(solution)/shard_map/other_up/ppermute | solution.py:90
  21.2 14.1 %collective-permute-start.7 = (bf16[896,256]{1,0:T(8,128)(2,1)S(1)}, bf16[896,256]{1,0:T(8,128)(2,1)S(1)}, u32[]{:S(2)}, u32[]{:S(2)}) collective-permute-start(bf16[896,256]{1,0:T(8,128)(2,1)S(1)} %collective-permute-done.2), channel_id=1, source_target_pairs={{4,8},{5,9},{6,10},{7,11},{8,4},{9,5},{10,6},{11,7},{20,24},{21,25... | collective-permute-start | bytes 1376264 | tf_op jit(solution)/shard_map/two_in/ppermute | solution.py:90
  23.4 12.0 %collective-permute-start.6 = (bf16[896,256]{1,0:T(8,128)(2,1)S(1)}, bf16[896,256]{1,0:T(8,128)(2,1)S(1)}, u32[]{:S(2)}, u32[]{:S(2)}) collective-permute-start(bf16[896,256]{1,0:T(8,128)(2,1)S(1)} %collective-permute-done.3), channel_id=1, source_target_pairs={{4,0},{5,1},{6,2},{7,3},{8,12},{9,13},{10,14},{11,15},{20,16},{21,... | collective-permute-start | bytes 1376264 | tf_op jit(solution)/shard_map/two_out/ppermute | solution.py:90
  24.7 20.6 %collective-permute-start.11 = (bf16[896,256]{1,0:T(8,128)(2,1)S(1)}, bf16[896,256]{1,0:T(8,128)(2,1)S(1)}, u32[]{:S(2)}, u32[]{:S(2)}) collective-permute-start(bf16[896,256]{1,0:T(8,128)(2,1)S(1)} %collective-permute-done.2), channel_id=1, source_target_pairs={{0,16},{1,3},{2,18},{3,1},{4,20},{5,7},{6,22},{7,5},{8,24},{9,11},... | collective-permute-start | bytes 1376264 | tf_op jit(solution)/shard_map/one_second/ppermute | solution.py:90
  25.0 14.6 %collective-permute-start.10 = (bf16[896,256]{1,0:T(8,128)(2,1)S(1)}, bf16[896,256]{1,0:T(8,128)(2,1)S(1)}, u32[]{:S(2)}, u32[]{:S(2)}) collective-permute-start(bf16[896,256]{1,0:T(8,128)(2,1)S(1)} %collective-permute-done.2), channel_id=1, source_target_pairs={{0,2},{1,17},{2,0},{3,19},{4,6},{5,21},{6,4},{7,23},{8,10},{9,25},... | collective-permute-start | bytes 1376264 | tf_op jit(solution)/shard_map/one_first/ppermute | solution.py:90
  26.3 16.2 %collective-permute-start.9 = (bf16[896,256]{1,0:T(8,128)(2,1)S(1)}, bf16[896,256]{1,0:T(8,128)(2,1)S(1)}, u32[]{:S(2)}, u32[]{:S(2)}) collective-permute-start(bf16[896,256]{1,0:T(8,128)(2,1)S(1)} %broadcast_select_fusion), channel_id=1, source_target_pairs={{0,2},{1,17},{2,0},{3,19},{4,6},{5,21},{6,4},{7,23},{8,10},{9,25},... | collective-permute-start | bytes 1376264 | tf_op jit(solution)/shard_map/corner/ppermute | solution.py:90
  35.5 17.2 %collective-permute-start.12 = (bf16[896,256]{1,0:T(8,128)(2,1)S(1)}, bf16[896,256]{1,0:T(8,128)(2,1)S(1)}, u32[]{:S(2)}, u32[]{:S(2)}) collective-permute-start(bf16[896,256]{1,0:T(8,128)(2,1)S(1)} %add.261), channel_id=1, source_target_pairs={{0,2},{1,17},{2,0},{3,19},{4,6},{5,21},{6,4},{7,23},{8,10},{9,25},... | collective-permute-start | bytes 1376264 | tf_op jit(solution)/shard_map/two_first/ppermute | solution.py:90
  36.8 10.1 %collective-permute-start.8 = (bf16[896,256]{1,0:T(8,128)(2,1)S(1)}, bf16[896,256]{1,0:T(8,128)(2,1)S(1)}, u32[]{:S(2)}, u32[]{:S(2)}) collective-permute-start(bf16[896,256]{1,0:T(8,128)(2,1)S(1)} %add.261), channel_id=1, source_target_pairs={{4,0},{5,1},{6,2},{7,3},{8,12},{9,13},{10,14},{11,15},{20,16},{21,... | collective-permute-start | bytes 1376264 | tf_op jit(solution)/shard_map/three_out/ppermute | solution.py:90
  43.1 8.9 %collective-permute-start.13 = (bf16[896,256]{1,0:T(8,128)(2,1)S(1)}, bf16[896,256]{1,0:T(8,128)(2,1)S(1)}, u32[]{:S(2)}, u32[]{:S(2)}) collective-permute-start(bf16[896,256]{1,0:T(8,128)(2,1)S(1)} %collective-permute-done.10), channel_id=1, source_target_pairs={{0,16},{1,3},{2,18},{3,1},{4,20},{5,7},{6,22},{7,5},{8,24},{9,11},... | collective-permute-start | bytes 1376264 | tf_op jit(solution)/shard_map/one_both/ppermute | solution.py:90
  44.4 16.1 %collective-permute-start.15 = (bf16[896,256]{1,0:T(8,128)(2,1)S(1)}, bf16[896,256]{1,0:T(8,128)(2,1)S(1)}, u32[]{:S(2)}, u32[]{:S(2)}) collective-permute-start(bf16[896,256]{1,0:T(8,128)(2,1)S(1)} %add.261), channel_id=1, source_target_pairs={{0,16},{1,3},{2,18},{3,1},{4,20},{5,7},{6,22},{7,5},{8,24},{9,11},... | collective-permute-start | bytes 1376264 | tf_op jit(solution)/shard_map/two_second/ppermute | solution.py:90
  47.1 25.3 %collective-permute-start.18 = (bf16[896,256]{1,0:T(8,128)(2,1)S(1)}, bf16[896,256]{1,0:T(8,128)(2,1)S(1)}, u32[]{:S(2)}, u32[]{:S(2)}) collective-permute-start(bf16[896,256]{1,0:T(8,128)(2,1)S(1)} %add.273), channel_id=1, source_target_pairs={{0,16},{1,3},{2,18},{3,1},{4,20},{5,7},{6,22},{7,5},{8,24},{9,11},... | collective-permute-start | bytes 1376264 | tf_op jit(solution)/shard_map/three_second/ppermute | solution.py:90
  48.1 13.1 %collective-permute-start.14 = (bf16[896,256]{1,0:T(8,128)(2,1)S(1)}, bf16[896,256]{1,0:T(8,128)(2,1)S(1)}, u32[]{:S(2)}, u32[]{:S(2)}) collective-permute-start(bf16[896,256]{1,0:T(8,128)(2,1)S(1)} %add.273), channel_id=1, source_target_pairs={{0,2},{1,17},{2,0},{3,19},{4,6},{5,21},{6,4},{7,23},{8,10},{9,25},... | collective-permute-start | bytes 1376264 | tf_op jit(solution)/shard_map/three_first/ppermute | solution.py:90
  52.7 19.0 %collective-permute-start.17 = (bf16[896,256]{1,0:T(8,128)(2,1)S(1)}, bf16[896,256]{1,0:T(8,128)(2,1)S(1)}, u32[]{:S(2)}, u32[]{:S(2)}) collective-permute-start(bf16[896,256]{1,0:T(8,128)(2,1)S(1)} %collective-permute-done.12), channel_id=1, source_target_pairs={{0,16},{1,3},{2,18},{3,1},{4,20},{5,7},{6,22},{7,5},{8,24},{9,11},... | collective-permute-start | bytes 1376264 | tf_op jit(solution)/shard_map/two_both/ppermute | solution.py:90
  61.2 15.5 %collective-permute-start.16 = (bf16[896,256]{1,0:T(8,128)(2,1)S(1)}, bf16[896,256]{1,0:T(8,128)(2,1)S(1)}, u32[]{:S(2)}, u32[]{:S(2)}) collective-permute-start(bf16[896,256]{1,0:T(8,128)(2,1)S(1)} %collective-permute-done.14), channel_id=1, source_target_pairs={{0,16},{1,3},{2,18},{3,1},{4,20},{5,7},{6,22},{7,5},{8,24},{9,11},... | collective-permute-start | bytes 1376264 | tf_op jit(solution)/shard_map/three_both/ppermute | solution.py:90
  73.0 4.3 %copy-start.1 = (f32[128]{0:T(128)S(1)}, f32[128]{0:T(128)}, u32[]{:S(2)}) copy-start(f32[128]{0:T(128)} %param.11) | copy-start | bytes 1540
  81.7 12.6 %collective-permute-start.20 = (bf16[2,256,896]{2,1,0:T(8,128)(2,1)S(1)}, bf16[2,256,896]{2,1,0:T(8,128)(2,1)S(1)}, u32[]{:S(2)}, u32[]{:S(2)}) collective-permute-start(bf16[2,256,896]{2,1,0:T(8,128)(2,1)S(1)} %get-tuple-element.374), channel_id=1, source_target_pairs={{0,16},{1,3},{2,18},{3,1},{4,20},{5,7},{6,22},{7,5},{8,24},{9,11},... | collective-permute-start | bytes 2752520 | tf_op jit(solution)/shard_map/seconds_3/ppermute | solution.py:90
  85.1 24.0 %collective-permute-start.22 = (bf16[2,256,896]{2,1,0:T(8,128)(2,1)S(1)}, bf16[2,256,896]{2,1,0:T(8,128)(2,1)S(1)}, u32[]{:S(2)}, u32[]{:S(2)}) collective-permute-start(bf16[2,256,896]{2,1,0:T(8,128)(2,1)S(1)} %get-tuple-element.381), channel_id=1, source_target_pairs={{0,16},{1,3},{2,18},{3,1},{4,20},{5,7},{6,22},{7,5},{8,24},{9,11},... | collective-permute-start | bytes 2752520 | tf_op jit(solution)/shard_map/seconds_2/ppermute | solution.py:90
  92.4 49.9 %copy-start = (f32[2,256,896]{2,1,0:T(8,128)}, f32[2,256,896]{2,1,0:T(8,128)S(1)}, u32[]{:S(2)}) copy-start(f32[2,256,896]{2,1,0:T(8,128)S(1)} %get-tuple-element.427.kept_ref) | copy-start | bytes 5505028
  94.4 16.1 %collective-permute-start.21 = (bf16[256,896]{1,0:T(8,128)(2,1)S(1)}, bf16[256,896]{1,0:T(8,128)(2,1)S(1)}, u32[]{:S(2)}, u32[]{:S(2)}) collective-permute-start(bf16[256,896]{1,0:T(8,128)(2,1)S(1)} %fusion.73), channel_id=1, source_target_pairs={{0,2},{1,17},{2,0},{3,19},{4,6},{5,21},{6,4},{7,23},{8,10},{9,25},... | collective-permute-start | bytes 1376264 | tf_op jit(solution)/shard_map/first_3/ppermute | solution.py:90
  95.7 28.1 %collective-permute-start.25 = (bf16[2,256,896]{2,1,0:T(8,128)(2,1)S(1)}, bf16[2,256,896]{2,1,0:T(8,128)(2,1)S(1)}, u32[]{:S(2)}, u32[]{:S(2)}) collective-permute-start(bf16[2,256,896]{2,1,0:T(8,128)(2,1)S(1)} %get-tuple-element.394), channel_id=1, source_target_pairs={{0,16},{1,3},{2,18},{3,1},{4,20},{5,7},{6,22},{7,5},{8,24},{9,11},... | collective-permute-start | bytes 2752520 | tf_op jit(solution)/shard_map/seconds_1/ppermute | solution.py:90
  109.2 14.7 %collective-permute-start.23 = (bf16[256,896]{1,0:T(8,128)(2,1)S(1)}, bf16[256,896]{1,0:T(8,128)(2,1)S(1)}, u32[]{:S(2)}, u32[]{:S(2)}) collective-permute-start(bf16[256,896]{1,0:T(8,128)(2,1)S(1)} %fusion.74), channel_id=1, source_target_pairs={{0,2},{1,17},{2,0},{3,19},{4,6},{5,21},{6,4},{7,23},{8,10},{9,25},... | collective-permute-start | bytes 1376264 | tf_op jit(solution)/shard_map/first_2/ppermute | solution.py:90
  110.7 13.3 %collective-permute-start.24 = (bf16[256,896]{1,0:T(8,128)(2,1)S(1)}, bf16[256,896]{1,0:T(8,128)(2,1)S(1)}, u32[]{:S(2)}, u32[]{:S(2)}) collective-permute-start(bf16[256,896]{1,0:T(8,128)(2,1)S(1)} %fusion.72), channel_id=1, source_target_pairs={{0,4},{1,5},{2,6},{3,7},{12,8},{13,9},{14,10},{15,11},{16,20},{17,... | collective-permute-start | bytes 1376264 | tf_op jit(solution)/shard_map/three_in/ppermute | solution.py:90
  124.1 12.4 %collective-permute-start.26 = (bf16[256,896]{1,0:T(8,128)(2,1)S(1)}, bf16[256,896]{1,0:T(8,128)(2,1)S(1)}, u32[]{:S(2)}, u32[]{:S(2)}) collective-permute-start(bf16[256,896]{1,0:T(8,128)(2,1)S(1)} %fusion.71), channel_id=1, source_target_pairs={{0,4},{1,5},{2,6},{3,7},{12,8},{13,9},{14,10},{15,11},{16,20},{17,... | collective-permute-start | bytes 1376264 | tf_op jit(solution)/shard_map/two_in/ppermute | solution.py:90
  125.4 16.8 %collective-permute-start.19 = (bf16[2,256,896]{2,1,0:T(8,128)(2,1)S(1)}, bf16[2,256,896]{2,1,0:T(8,128)(2,1)S(1)}, u32[]{:S(2)}, u32[]{:S(2)}) collective-permute-start(bf16[2,256,896]{2,1,0:T(8,128)(2,1)S(1)} %get-tuple-element.372), channel_id=1, source_target_pairs={{0,16},{1,3},{2,18},{3,1},{4,20},{5,7},{6,22},{7,5},{8,24},{9,11},... | collective-permute-start | bytes 2752520 | tf_op jit(solution)/shard_map/seconds_0/ppermute | solution.py:90
  125.5 11.1 %collective-permute-start.29 = (bf16[256,896]{1,0:T(8,128)(2,1)S(1)}, bf16[256,896]{1,0:T(8,128)(2,1)S(1)}, u32[]{:S(2)}, u32[]{:S(2)}) collective-permute-start(bf16[256,896]{1,0:T(8,128)(2,1)S(1)} %fusion.71), channel_id=1, source_target_pairs={{4,8},{5,9},{6,10},{7,11},{8,4},{9,5},{10,6},{11,7},{20,24},{21,25... | collective-permute-start | bytes 1376264 | tf_op jit(solution)/shard_map/two/ppermute | solution.py:90
  128.7 12.6 %collective-permute-start.28 = (bf16[256,896]{1,0:T(8,128)(2,1)S(1)}, bf16[256,896]{1,0:T(8,128)(2,1)S(1)}, u32[]{:S(2)}, u32[]{:S(2)}) collective-permute-start(bf16[256,896]{1,0:T(8,128)(2,1)S(1)} %fusion.75), channel_id=1, source_target_pairs={{0,2},{1,17},{2,0},{3,19},{4,6},{5,21},{6,4},{7,23},{8,10},{9,25},... | collective-permute-start | bytes 1376264 | tf_op jit(solution)/shard_map/first_1/ppermute | solution.py:90
  136.6 10.2 %collective-permute-start.27 = (bf16[256,896]{1,0:T(8,128)(2,1)S(1)}, bf16[256,896]{1,0:T(8,128)(2,1)S(1)}, u32[]{:S(2)}, u32[]{:S(2)}) collective-permute-start(bf16[256,896]{1,0:T(8,128)(2,1)S(1)} %add_convert_fusion.1), channel_id=1, source_target_pairs={{4,8},{5,9},{6,10},{7,11},{8,4},{9,5},{10,6},{11,7},{20,24},{21,25... | collective-permute-start | bytes 1376264 | tf_op jit(solution)/shard_map/three/ppermute | solution.py:90
  142.3 13.0 %copy-start.2 = (bf16[2,256,896]{2,1,0:T(8,128)(2,1)}, bf16[2,256,896]{2,1,0:T(8,128)(2,1)S(1)}, u32[]{:S(2)}) copy-start(bf16[2,256,896]{2,1,0:T(8,128)(2,1)S(1)} %collective-permute-done.19.got_ref) | copy-start | bytes 2752516
  142.4 7.7 %collective-permute-start.30 = (bf16[256,896]{1,0:T(8,128)(2,1)S(1)}, bf16[256,896]{1,0:T(8,128)(2,1)S(1)}, u32[]{:S(2)}, u32[]{:S(2)}) collective-permute-start(bf16[256,896]{1,0:T(8,128)(2,1)S(1)} %fusion.76), channel_id=1, source_target_pairs={{0,2},{1,17},{2,0},{3,19},{4,6},{5,21},{6,4},{7,23},{8,10},{9,25},... | collective-permute-start | bytes 1376264 | tf_op jit(solution)/shard_map/first_0/ppermute | solution.py:90
  143.7 11.6 %collective-permute-start.31 = (bf16[256,896]{1,0:T(8,128)(2,1)}, bf16[256,896]{1,0:T(8,128)(2,1)S(1)}, u32[]{:S(2)}, u32[]{:S(2)}) collective-permute-start(bf16[256,896]{1,0:T(8,128)(2,1)} %fusion.69), channel_id=1, source_target_pairs={{0,4},{1,5},{2,6},{3,7},{4,0},{5,1},{6,2},{7,3},{8,12},{9,13},{10,... | collective-permute-start | bytes 1376264 | tf_op jit(solution)/shard_map/one/ppermute | solution.py:90
  146.8 8.4 %copy-start.4 = (bf16[256,896]{1,0:T(8,128)(2,1)}, bf16[256,896]{1,0:T(8,128)(2,1)S(1)}, u32[]{:S(2)}) copy-start(bf16[256,896]{1,0:T(8,128)(2,1)S(1)} %collective-permute-done.27.refs_0_) | copy-start | bytes 1376260
  150.1 5.2 %copy-start.5 = (bf16[256,896]{1,0:T(8,128)(2,1)}, bf16[256,896]{1,0:T(8,128)(2,1)S(1)}, u32[]{:S(2)}) copy-start(bf16[256,896]{1,0:T(8,128)(2,1)S(1)} %collective-permute-done.30.refs_1_) | copy-start | bytes 1376260
  155.3 0.8 copy-start.6
  160.5 4.4 %collective-permute-start.32 = (f32[448,256]{1,0:T(8,128)S(1)}, f32[448,256]{1,0:T(8,128)S(1)}, u32[]{:S(2)}, u32[]{:S(2)}) collective-permute-start(f32[448,256]{1,0:T(8,128)S(1)} %constant_dynamic-slice_fusion), channel_id=1, source_target_pairs={{0,1},{1,0},{2,3},{3,2},{4,5},{5,4},{6,7},{7,6},{8,9},{9,8},{10,11... | collective-permute-start | bytes 1376264 | tf_op jit(solution)/shard_map/taken/ppermute | solution.py:90
  163.4 2.6 %copy-start.3 = (bf16[448,512]{1,0:T(8,128)(2,1)S(1)}, bf16[448,512]{1,0:T(8,128)(2,1)}, u32[]{:S(2)}) copy-start(bf16[448,512]{1,0:T(8,128)(2,1)} %param.10) | copy-start | bytes 1376260
  163.4 2.6 %copy-start.7 = (f32[448,256]{1,0:T(8,128)S(1)}, f32[448,256]{1,0:T(8,128)}, u32[]{:S(2)}) copy-start(f32[448,256]{1,0:T(8,128)} %param.13) | copy-start | bytes 1376260
  163.4 2.6 %copy-start.8 = (f32[448,256]{1,0:T(8,128)S(1)}, f32[448,256]{1,0:T(8,128)}, u32[]{:S(2)}) copy-start(f32[448,256]{1,0:T(8,128)} %param.12) | copy-start | bytes 1376260

commit v3 on v2

--- a/solution.py
+++ b/solution.py
@@ -145,13 +145,13 @@
 SMEM = pl.BlockSpec(memory_space=pltpu.SMEM)
 
 
-def call(kernel, outs, scalars, *operands, name):
+def call(kernel, outs, scalars, *operands, name, cost=10**7):
     return pl.pallas_call(
         kernel,
         out_shape=outs,
         in_specs=[SMEM] + [VMEM] * len(operands),
         out_specs=jax.tree.map(lambda _: VMEM, outs),
-        cost_estimate=pl.CostEstimate(flops=10**9, bytes_accessed=10**7, transcendentals=0),
+        cost_estimate=pl.CostEstimate(flops=100 * cost, bytes_accessed=cost, transcendentals=0),
         compiler_params=pltpu.CompilerParams(vmem_limit_bytes=24 * 2**20),
         name=name,
     )(jnp.stack(scalars).astype(jnp.int32), *operands)
@@ -166,44 +166,33 @@
     return pl.ds(0, half), pl.ds(half, half)
 
 
-def spread(block, x, core, rights, tokens_ref, got_ref, kept_ref):
+def partials(block, x, core, rights, tokens_ref, leave, out_ref):
     width = rights[0].shape[0] // 2
-    depth = got_ref.shape[2]
-    own_first = core == 0
-    for begin in range(0, depth, 256):
-        size = min(256, depth - begin)
-        out = pl.ds(begin, size)
-
-        def products(place):
+    depth = out_ref.shape[2]
+    here, there = pl.ds(0, width), pl.ds(width, width)
+    by_core = core == 0 if leave else core != 0
+    place_fixed, place_by_core = 1 - x if leave else x, jnp.where(by_core, x, 1 - x)
+    fixed = [right[there if leave else here, :] for right in rights]
+    chosen = [jnp.where(by_core, right[there, :], right[here, :]) for right in rights]
+    order = (0, 1) if leave else (1, 0)
+    for i, place, lefts in ((order[0], place_fixed, fixed), (order[1], place_by_core, chosen)):
+        for begin in range(0, depth, 256):
+            size = min(256, depth - begin)
             at = pl.ds(pl.multiple_of((2 * block + place) * depth, 128) + begin, size)
-            return sum(
-                dot(right[...], tokens_ref[rows, at])
-                for right, rows in zip(rights, halves(tokens_ref))
+            total = sum(
+                dot(left, tokens_ref[rows, at]) for left, rows in zip(lefts, halves(tokens_ref))
             )
-
-        near, far = products(x), products(1 - x)
-        second = jnp.where(own_first, near[width:], far[:width])
-        first = jnp.where(own_first, far[:width], near[width:])
-        got_ref[0, :, out] = far[width:].astype(jnp.bfloat16)
-        got_ref[1, :, out] = second.astype(jnp.bfloat16)
-        kept_ref[0, :, out] = first
-        kept_ref[1, :, out] = near[:width]
-
-
-def spread_shapes(width, depth):
-    return [
-        jax.ShapeDtypeStruct((2, width, depth), jnp.bfloat16),
-        jax.ShapeDtypeStruct((2, width, depth), jnp.float32),
-    ]
-
-
-def contract(scalars, depth, tokens, right_a, right_b):
-    def kernel(at_ref, tokens_ref, right_a, right_b, got_ref, kept_ref):
+            out_ref[i, :, pl.ds(begin, size)] = total.astype(out_ref.dtype)
+
+
+def contract(scalars, depth, leave, tokens, right_a, right_b):
+    def kernel(at_ref, tokens_ref, right_a, right_b, out_ref):
         place = at_ref[0], at_ref[1], at_ref[2]
-        spread(*place, (right_a, right_b), tokens_ref, got_ref, kept_ref)
-
-    shapes = spread_shapes(right_a.shape[0] // 2, depth)
-    return call(kernel, shapes, scalars, tokens, right_a, right_b, name="contract")
+        partials(*place, (right_a, right_b), tokens_ref, leave, out_ref)
+
+    dtype = jnp.bfloat16 if leave else jnp.float32
+    out = jax.ShapeDtypeStruct((2, right_a.shape[0] // 2, depth), dtype)
+    return call(kernel, out, scalars, tokens, right_a, right_b, name="contract", cost=10**7)
 
 
 def head_gradients(scalars, depth, tokens, sums, own_up, other_up, norm_gain):
@@ -213,7 +202,7 @@
 
     def kernel(
         at_ref, tokens_ref, own_ref, both_ref, first_ref, second_ref, up_a, up_b, gain_ref,
-        right_a, right_b, got_ref, kept_ref,
+        right_a, right_b, leaving_ref,
     ):
         gain = gain_ref[...]
         own_first = at_ref[2] == 0
@@ -236,11 +225,12 @@
                         features = pl.ds((2 * side + i) * head, head)
                         right[features, within] = value.T.astype(jnp.bfloat16)
         place = at_ref[0], at_ref[1], at_ref[2]
-        spread(*place, (right_a, right_b), tokens_ref, got_ref, kept_ref)
-
+        partials(*place, (right_a, right_b), tokens_ref, True, leaving_ref)
+
+    right = jax.ShapeDtypeStruct((2 * width, half), jnp.bfloat16)
     return call(
         kernel,
-        [jax.ShapeDtypeStruct((2 * width, half), jnp.bfloat16)] * 2 + spread_shapes(width, depth),
+        [right, right, jax.ShapeDtypeStruct((2, width, depth), jnp.bfloat16)],
         scalars,
         tokens,
         *sums,
@@ -251,27 +241,76 @@
     )
 
 
-def by_rows(kept, got, *terms):
+def by_rows(scalars, *terms):
     width, depth = terms[0].shape
-    terms = (kept, got, *terms)
-
-    def kernel(kept_ref, got_ref, *refs):
-        *term_refs, out_ref = refs
+    half = depth // 2
+
+    def kernel(at_ref, *refs):
+        *term_refs, kept_ref, given_ref = refs
+
+        def put(part, begin, value):
+            rows = pl.ds(begin, value.shape[0])
+
+            @pl.when(at_ref[2] == part)
+            def _():
+                kept_ref[rows, :] = value
+
+            @pl.when(at_ref[2] != part)
+            def _():
+                given_ref[rows, :] = value
+
         for begin in range(0, depth, 128):
             size = min(128, depth - begin)
-            at = pl.ds(begin, size)
-            total = kept_ref[1, :, at] + got_ref[1, :, at].astype(jnp.float32)
-            for ref in term_refs:
-                total += ref[:, at].astype(jnp.float32)
-            out_ref[at, :] = total.T
-
-    return pl.pallas_call(
-        kernel,
-        out_shape=jax.ShapeDtypeStruct((depth, width), jnp.float32),
-        in_specs=[VMEM] * len(terms),
-        out_specs=VMEM,
-        name="by_rows",
-    )(*terms)
+            total = sum(ref[:, pl.ds(begin, size)].astype(jnp.float32) for ref in term_refs).T
+            below = max(0, min(size, half - begin))
+            if below:
+                put(0, begin, total[:below])
+            if below < size:
+                put(1, begin + below - half, total[below:])
+
+    out = jax.ShapeDtypeStruct((half, width), jnp.float32)
+    return call(kernel, [out, out], scalars, *terms, name="by_rows")
+
+
+def finish(scalars, kept, taken, probe, momentum, curvature):
+    head = kept.shape[1] // 2
+    shares = momentum.shape[1] // head
+
+    def kernel(at_ref, kept_ref, taken_ref, probe_ref, momentum_ref, curvature_ref, *out_refs):
+        own_first = at_ref[0] == 0
+        for i in range(shares):
+            columns = pl.ds(i * head, head)
+            mine = own_first if i == 0 else jnp.logical_not(own_first)
+            share = jnp.where(mine, kept_ref[...], taken_ref[...])
+            at = pl.multiple_of(at_ref[1] * (shares * head), 128) + i * head
+            results = step_outputs(
+                momentum_ref[:, columns],
+                curvature_ref[:, columns],
+                probe_ref[:, pl.ds(at, head)].astype(jnp.float32),
+                share[:, :head],
+                share[:, head:],
+            )
+            for out_ref, value in zip(out_refs, results):
+                out_ref[:, columns] = value
+
+    out = jax.ShapeDtypeStruct(momentum.shape, jnp.float32)
+    return call(kernel, [out] * 3, scalars, kept, taken, probe, momentum, curvature, name="finish")
+
+
+def columns_by_core(scalars, head, *arrays):
+    rows = arrays[0].shape[0]
+
+    def kernel(at_ref, *refs):
+        *array_refs, leaving_ref, staying_ref = refs
+        y, c = at_ref[0], at_ref[1]
+        for out_ref, core in ((leaving_ref, 1 - c), (staying_ref, c)):
+            for i, side in enumerate((y, 1 - y)):
+                for j, ref in enumerate(array_refs):
+                    column = pl.ds(pl.multiple_of((2 * side + core) * head, 128), head)
+                    out_ref[:, pl.ds((i * len(array_refs) + j) * head, head)] = ref[:, column]
+
+    out = jax.ShapeDtypeStruct((rows, 2 * len(arrays) * head), arrays[0].dtype)
+    return call(kernel, [out, out], scalars, *arrays, name="columns_by_core")
 
 
 def by_links(acts, upstream, k_weight, probe, norm_gain, momentum, curvature):
@@ -281,21 +320,10 @@
     y, z, x, c = lax.axis_index("dp"), place // 4, (place // 2) % 2, place % 2
     own_first = c == 0
 
-    def column(value, number):
-        return lax.dynamic_slice_in_dim(value, number * head, head, 1)
-
-    def weights_for(core, side):
-        return [column(k_weight, 2 * side + core), column(probe, 2 * side + core)]
-
-    leaving = jnp.concatenate(weights_for(1 - c, y) + weights_for(1 - c, 1 - y), axis=1)
-    staying = jnp.concatenate(weights_for(c, y) + weights_for(c, 1 - y), axis=1)
+    leaving, staying = columns_by_core((y, c), head, k_weight, probe)
     coming = send(leaving, to_core, "coming")
-    def upstream_for(core):
-        return jnp.concatenate(
-            [column(upstream, 2 * y + core), column(upstream, 2 * (1 - y) + core)], axis=1
-        )
-
-    own_up, other_up = upstream_for(c), send(upstream_for(1 - c), to_core, "other_up")
+    up_leaving, own_up = columns_by_core((y, c), head, after(upstream, leaving))
+    other_up = send(up_leaving, to_core, "other_up")
     chip_rows = jnp.where(
         own_first,
         jnp.concatenate([staying, coming], axis=0),
@@ -363,13 +391,13 @@
     both_sum = add_product(both_sum, 3, 1, three_both)
 
     sums = (own_sum, both_sum, first_sum, second_sum)
-    right_a, right_b, leaving_3, kept_3 = head_gradients(
+    right_a, right_b, leaving_3 = head_gradients(
         (z ^ 3, x, c), 2 * rows, tokens, sums, own_up, other_up, norm_gain
     )
 
-    def partial(slot):
+    def partial(slot, leave):
         def product(*operands):
-            return contract((z ^ slot, x, c), 2 * rows, *operands)
+            return contract((z ^ slot, x, c), 2 * rows, leave, *operands)
 
         return order.run(product, tokens, right_a, right_b)
 
@@ -382,37 +410,40 @@
 
         return order.run(total, kept, got, *more)
 
+    def sum_of(*terms):
+        return order.run(lambda *t: total_of(*t).astype(jnp.bfloat16), *terms)
+
     seconds_3 = send(leaving_3, to_second, "seconds_3")
-    leaving_2, kept_2 = partial(2)
-    seconds_2 = send(leaving_2, to_second, "seconds_2")
-    leaving_1, kept_1 = partial(1)
-    seconds_1 = send(leaving_1, to_second, "seconds_1")
-    leaving_0, kept_0 = partial(0)
-    seconds_0 = send(leaving_0, to_second, "seconds_0")
+    raw_1 = send(partial(1, True), Z_ONE, "raw_1")
+    seconds_2 = send(partial(2, True), to_second, "seconds_2")
+    kept_3 = partial(3, False)
     first_3 = send(rounded(0, kept_3, seconds_3), to_first, "first_3")
-    first_2 = send(rounded(0, kept_2, seconds_2), to_first, "first_2")
+    leaving_0 = partial(0, True)
+    kept_2 = partial(2, False)
+    kept_1 = partial(1, False)
+    kept_0 = partial(0, False)
+    leaving_0 = sum_of(leaving_0, raw_1)
     sum_3 = rounded(1, kept_3, seconds_3, first_3)
     three_in = send(sum_3, Z_IN, "three_in")
-    first_1 = send(rounded(0, kept_1, seconds_1), to_first, "first_1")
+    first_2 = send(rounded(0, kept_2, seconds_2), to_first, "first_2")
+    leaving_0 = order.wait(leaving_0)
+    seconds_0 = send(leaving_0, to_second, "seconds_0")
     sum_2 = rounded(1, kept_2, seconds_2, first_2, three_in)
     two_in = send(sum_2, Z_IN, "two_in")
     two = send(sum_2, Z_MIDDLE, "two")
-    sum_3 = order.run(lambda *t: total_of(*t).astype(jnp.bfloat16), sum_3, two_in)
-    three = send(sum_3, Z_MIDDLE, "three")
-    two = order.wait(two)
-    one = send(rounded(1, kept_1, seconds_1, first_1, two), Z_ONE, "one")
+    first_1 = send(order.run(lambda kept: kept[0].astype(jnp.bfloat16), kept_1), to_first, "first_1")
+    own_1 = order.run(lambda kept, got: total_of(kept[1], got), kept_1, first_1)
     first_0 = send(rounded(0, kept_0, seconds_0), to_first, "first_0")
-    owned = order.run(by_rows, kept_0, seconds_0, three, first_0, one)
-
-    kept = lax.dynamic_slice_in_dim(owned, c * rows, rows, 0)
-    given = lax.dynamic_slice_in_dim(owned, (1 - c) * rows, rows, 0)
+    three = send(sum_of(sum_3, two_in), Z_MIDDLE, "three")
+    one = send(sum_of(own_1, two), Z_ONE, "one")
+    own_0 = order.run(lambda kept, got: total_of(kept[1], got[1]), kept_0, seconds_0)
+
+    def turned(*terms):
+        return by_rows((y, x, c), *terms)
+
+    kept, given = order.run(turned, own_0, first_0, three, one)
     taken = send(given, to_core, "taken")
-    left = jnp.where(own_first, kept, taken)
-    right = jnp.where(own_first, taken, kept)
-    grad_share = jnp.concatenate([left[:, :head], right[:, :head]], axis=1)
-    hvp_share = jnp.concatenate([left[:, head:], right[:, head:]], axis=1)
-    probe_cols = lax.dynamic_slice_in_dim(probe, y * 2 * head, 2 * head, 1).astype(jnp.float32)
-    return step_outputs(order.token, curvature, probe_cols, grad_share, hvp_share)
+    return tuple(finish((c, y), kept, taken, probe, order.token, curvature))
 
 
 def solution(mesh):

time: 170 us -> 156 us (0.918)
  waiting for transfers between devices: 82.5 us -> 72.8 us
  Pallas kernels: 16.7 us -> 20.7 us
  other arithmetic: 11.8 us -> 9.07 us
  local copies, waits for them, and re-layouts: 4.44 us -> 2.17 us
    ppermute x33, waiting for transfers between devices: 82.5 us -> 72.8 us  [send(): return lax.ppermute(value, AXES, pairs_of(move))]
    pallas_call x4 -> x12, Pallas kernels: 13.4 us -> 20.7 us  [call(): pl.pallas_call(kernel, out_shape=outs, in_specs=[SMEM] + [VMEM] * len(ope...]
    dynamic_slice x3 -> x0, local copies, waits for them, and re-layouts: 3.52 us -> none  [the longest x2 2.47 us: column(): return lax.dynamic_slice_in_dim(value, number * head, head, 1)]
    pallas_call x1 -> x0, Pallas kernels: 3.36 us -> none  [by_rows(): pl.pallas_call(kernel, out_shape=jax.ShapeDtypeStruct((depth, width), jnp...]
  transfers between devices with their start and end apart: 33 -> 33, of which waited for: 19 -> 23; matrix products, arithmetic and copies ran while one was open for 11% -> 12% of each run, Pallas kernels for 5% -> 9%
where the time goes in v3:
time: 156 us; the launch traced here: 155 us
  waiting for transfers between devices  72.8 us (47%)
  starting transfers between devices  38.6 us (25%)
  Pallas kernels  20.7 us (13%)
  matrix products  10.4 us (7%)
  other arithmetic  9.07 us (6%)
  local copies, waits for them, and re-layouts  2.17 us (1%)
    ppermute x33, waiting for transfers between devices, send(): return lax.ppermute(value, AXES, pairs_of(move))  72.8 us
    ppermute x33, starting transfers between devices, send(): return lax.ppermute(value, AXES, pairs_of(move))  38.6 us
    pallas_call x12, Pallas kernels, call(): pl.pallas_call(kernel, out_shape=outs, in_specs=[SMEM] + [VMEM] * len(ope...  20.7 us
    dot_general x16, matrix products, product(): jnp.dot(block_of(held, slot, flip_x), unit, preferred_element_type=jnp.fl...  10.4 us
    concatenate x1, other arithmetic, by_links(): jnp.concatenate([a, b], axis=0)  6.77 us
  transfers between devices with their start and end apart: 33, of which 23 were waited for; matrix products, arithmetic and copies ran while one was open for 12% of the time, Pallas kernels for 9%

profile of v3, /device:TPU:11, one launch (start us, length us, event | category | flops | bytes accessed | tf_op | source)
XLA Modules:
  0.0 154.8 jit_solution(15273255530841283393)
XLA Ops:
  4.2 1.4 collective-permute-done
  6.6 3.2 %collective-permute-start.3 = (bf16[896,256]{1,0:T(8,128)(2,1)S(1)}, bf16[896,256]{1,0:T(8,128)(2,1)S(1)}, u32[]{:S(2)}, u32[]{:S(2)}) collective-permute-start(bf16[896,256]{1,0:T(8,128)(2,1)S(1)} %get-tuple-element.273), channel_id=1, source_target_pairs={{4,8},{5,9},{6,10},{7,11},{8,4},{9,5},{10,6},{11,7},{20,24},{21,25... | collective-permute-start | bytes 1376264 | tf_op jit(solution)/shard_map/near/ppermute | solution.py:90
  11.7 5.1 %collective-permute-done.4.up_b = bf16[448,256]{1,0:T(8,128)(2,1)S(1)} collective-permute-done((bf16[448,256]{1,0:T(8,128)(2,1)S(1)}, bf16[448,256]{1,0:T(8,128)(2,1)S(1)}, u32[]{:S(2)}, u32[]{:S(2)}) %collective-permute-start.4) | collective-permute-done | bytes 229408 | tf_op jit(solution)/shard_map/other_up/ppermute | solution.py:90
  16.8 3.6 %collective-permute-done.3 = bf16[896,256]{1,0:T(8,128)(2,1)S(1)} collective-permute-done((bf16[896,256]{1,0:T(8,128)(2,1)S(1)}, bf16[896,256]{1,0:T(8,128)(2,1)S(1)}, u32[]{:S(2)}, u32[]{:S(2)}) %collective-permute-start.3) | collective-permute-done | bytes 458784 | tf_op jit(solution)/shard_map/near/ppermute | solution.py:90
  20.4 1.1 collective-permute-done.2
  21.5 2.1 %collective-permute-start.7 = (bf16[896,256]{1,0:T(8,128)(2,1)S(1)}, bf16[896,256]{1,0:T(8,128)(2,1)S(1)}, u32[]{:S(2)}, u32[]{:S(2)}) collective-permute-start(bf16[896,256]{1,0:T(8,128)(2,1)S(1)} %collective-permute-done.2), channel_id=1, source_target_pairs={{4,8},{5,9},{6,10},{7,11},{8,4},{9,5},{10,6},{11,7},{20,24},{21,25... | collective-permute-start | bytes 1376264 | tf_op jit(solution)/shard_map/two_in/ppermute | solution.py:90
  23.6 1.3 collective-permute-start.6
  25.3 1.2 collective-permute-start.10
  26.9 6.8 %pad_maximum_fusion.tokens_ref = bf16[896,7168]{1,0:T(8,128)(2,1)S(1)} fusion(bf16[448,7168]{1,0:T(8,128)(2,1)} %collective-permute-done.1, bf16[448,7168]{1,0:T(8,128)(2,1)} %param.7), kind=kLoop, calls=%fused_computation | loop fusion | flops 25690112 | bytes 25690112 | tf_op jit(solution)/shard_map/concatenate | solution.py:348
  35.8 1.3 collective-permute-start.12
  37.1 2.2 %collective-permute-start.8 = (bf16[896,256]{1,0:T(8,128)(2,1)S(1)}, bf16[896,256]{1,0:T(8,128)(2,1)S(1)}, u32[]{:S(2)}, u32[]{:S(2)}) collective-permute-start(bf16[896,256]{1,0:T(8,128)(2,1)S(1)} %add.197), channel_id=1, source_target_pairs={{4,0},{5,1},{6,2},{7,3},{8,12},{9,13},{10,14},{11,15},{20,16},{21,... | collective-permute-start | bytes 1376264 | tf_op jit(solution)/shard_map/three_out/ppermute | solution.py:90
  39.9 2.8 %collective-permute-done.9 = bf16[896,256]{1,0:T(8,128)(2,1)S(1)} collective-permute-done((bf16[896,256]{1,0:T(8,128)(2,1)S(1)}, bf16[896,256]{1,0:T(8,128)(2,1)S(1)}, u32[]{:S(2)}, u32[]{:S(2)}) %collective-permute-start.9) | collective-permute-done | bytes 458784 | tf_op jit(solution)/shard_map/corner/ppermute | solution.py:90
  43.4 1.3 collective-permute-start.13
  48.3 1.2 collective-permute-start.14
  49.6 2.8 %collective-permute-done.13 = bf16[896,256]{1,0:T(8,128)(2,1)S(1)} collective-permute-done((bf16[896,256]{1,0:T(8,128)(2,1)S(1)}, bf16[896,256]{1,0:T(8,128)(2,1)S(1)}, u32[]{:S(2)}, u32[]{:S(2)}) %collective-permute-start.13) | collective-permute-done | bytes 458784 | tf_op jit(solution)/shard_map/one_both/ppermute | solution.py:90
  54.6 6.1 %collective-permute-done.15 = bf16[896,256]{1,0:T(8,128)(2,1)S(1)} collective-permute-done((bf16[896,256]{1,0:T(8,128)(2,1)S(1)}, bf16[896,256]{1,0:T(8,128)(2,1)S(1)}, u32[]{:S(2)}, u32[]{:S(2)}) %collective-permute-start.15) | collective-permute-done | bytes 458784 | tf_op jit(solution)/shard_map/two_second/ppermute | solution.py:90
  62.2 9.8 %collective-permute-done.17 = bf16[896,256]{1,0:T(8,128)(2,1)S(1)} collective-permute-done((bf16[896,256]{1,0:T(8,128)(2,1)S(1)}, bf16[896,256]{1,0:T(8,128)(2,1)S(1)}, u32[]{:S(2)}, u32[]{:S(2)}) %collective-permute-start.17) | collective-permute-done | bytes 458784 | tf_op jit(solution)/shard_map/two_both/ppermute | solution.py:90
  73.3 3.6 %collective-permute-done.16 = bf16[896,256]{1,0:T(8,128)(2,1)S(1)} collective-permute-done((bf16[896,256]{1,0:T(8,128)(2,1)S(1)}, bf16[896,256]{1,0:T(8,128)(2,1)S(1)}, u32[]{:S(2)}, u32[]{:S(2)}) %collective-permute-start.16) | collective-permute-done | bytes 458784 | tf_op jit(solution)/shard_map/three_both/ppermute | solution.py:90
  77.6 3.2 %head_gradients.1 = (bf16[512,448]{1,0:T(8,128)(2,1)S(1)}, bf16[512,448]{1,0:T(8,128)(2,1)S(1)}, bf16[2,256,896]{2,1,0:T(8,128)(2,1)S(1)}) custom-call(s32[3]{0:T(128)S(1)} %get-tuple-element.505.at_ref, bf16[896,7168]{1,0:T(8,128)(2,1)S(1)} %pad_maximum_fusion.tokens_ref, f32[896,256]{1,0:T(8,128)S(1)} %fusion.50.own_ref, f32[896,256]{1,0:T(8,128)S(1)} %fusion.65.both_ref, ...), custom_call_target="tpu_custom_call" | custom-call | flops 1000000000 | bytes 10000000 | tf_op jit(solution)/shard_map/head_gradients/pallas_call | solution.py:149
  81.2 1.8 %contract.7 = bf16[2,256,896]{2,1,0:T(8,128)(2,1)S(1)} custom-call(s32[3]{0:T(128)S(1)} %get-tuple-element.506.at_ref, bf16[896,7168]{1,0:T(8,128)(2,1)S(1)} %pad_maximum_fusion.tokens_ref, bf16[512,448]{1,0:T(8,128)(2,1)S(1)} %get-tuple-element.426.right_a, bf16[512,448]{1,0:T(8,128)(2,1)S(1)} %get-tuple-element.427.right_b), custom_call_target="tpu_custom_call" | custom-call | flops 1000000000 | bytes 10000000 | tf_op jit(solution)/shard_map/contract/pallas_call | solution.py:149
  83.2 1.8 %contract.8 = bf16[2,256,896]{2,1,0:T(8,128)(2,1)S(1)} custom-call(s32[3]{0:T(128)S(1)} %add_add_fusion.4.at_ref, bf16[896,7168]{1,0:T(8,128)(2,1)S(1)} %pad_maximum_fusion.tokens_ref, bf16[512,448]{1,0:T(8,128)(2,1)S(1)} %get-tuple-element.426.right_a, bf16[512,448]{1,0:T(8,128)(2,1)S(1)} %get-tuple-element.427.right_b), custom_call_target="tpu_custom_call" | custom-call | flops 1000000000 | bytes 10000000 | tf_op jit(solution)/shard_map/contract/pallas_call | solution.py:149
  85.0 1.2 collective-permute-start.21
  86.3 2.1 %contract.9 = f32[2,256,896]{2,1,0:T(8,128)S(1)} custom-call(s32[3]{0:T(128)S(1)} %get-tuple-element.505.at_ref, bf16[896,7168]{1,0:T(8,128)(2,1)S(1)} %pad_maximum_fusion.tokens_ref, bf16[512,448]{1,0:T(8,128)(2,1)S(1)} %get-tuple-element.426.right_a, bf16[512,448]{1,0:T(8,128)(2,1)S(1)} %get-tuple-element.427.right_b), custom_call_target="tpu_custom_call" | custom-call | flops 1000000000 | bytes 10000000 | tf_op jit(solution)/shard_map/contract/pallas_call | solution.py:149
  88.3 5.0 %collective-permute-done.19 = bf16[2,256,896]{2,1,0:T(8,128)(2,1)S(1)} collective-permute-done((bf16[2,256,896]{2,1,0:T(8,128)(2,1)S(1)}, bf16[2,256,896]{2,1,0:T(8,128)(2,1)S(1)}, u32[]{:S(2)}, u32[]{:S(2)}) %collective-permute-start.19) | collective-permute-done | bytes 917536 | tf_op jit(solution)/shard_map/seconds_3/ppermute | solution.py:90
  93.4 1.3 collective-permute-start.22
  94.7 1.8 %contract.10 = bf16[2,256,896]{2,1,0:T(8,128)(2,1)S(1)} custom-call(s32[3]{0:T(128)S(1)} %get-tuple-element.504.at_ref, bf16[896,7168]{1,0:T(8,128)(2,1)S(1)} %pad_maximum_fusion.tokens_ref, bf16[512,448]{1,0:T(8,128)(2,1)S(1)} %get-tuple-element.426.right_a, bf16[512,448]{1,0:T(8,128)(2,1)S(1)} %get-tuple-element.427.right_b), custom_call_target="tpu_custom_call" | custom-call | flops 1000000000 | bytes 10000000 | tf_op jit(solution)/shard_map/contract/pallas_call | solution.py:149
  96.6 1.8 %contract.11 = f32[2,256,896]{2,1,0:T(8,128)S(1)} custom-call(s32[3]{0:T(128)S(1)} %add_add_fusion.4.at_ref, bf16[896,7168]{1,0:T(8,128)(2,1)S(1)} %pad_maximum_fusion.tokens_ref, bf16[512,448]{1,0:T(8,128)(2,1)S(1)} %get-tuple-element.426.right_a, bf16[512,448]{1,0:T(8,128)(2,1)S(1)} %get-tuple-element.427.right_b), custom_call_target="tpu_custom_call" | custom-call | flops 1000000000 | bytes 10000000 | tf_op jit(solution)/shard_map/contract/pallas_call | solution.py:149
  98.4 1.8 %contract.12 = f32[2,256,896]{2,1,0:T(8,128)S(1)} custom-call(s32[3]{0:T(128)S(1)} %get-tuple-element.506.at_ref, bf16[896,7168]{1,0:T(8,128)(2,1)S(1)} %pad_maximum_fusion.tokens_ref, bf16[512,448]{1,0:T(8,128)(2,1)S(1)} %get-tuple-element.426.right_a, bf16[512,448]{1,0:T(8,128)(2,1)S(1)} %get-tuple-element.427.right_b), custom_call_target="tpu_custom_call" | custom-call | flops 1000000000 | bytes 10000000 | tf_op jit(solution)/shard_map/contract/pallas_call | solution.py:149
  100.3 1.8 %contract.13 = f32[2,256,896]{2,1,0:T(8,128)S(1)} custom-call(s32[3]{0:T(128)S(1)} %get-tuple-element.504.at_ref, bf16[896,7168]{1,0:T(8,128)(2,1)S(1)} %pad_maximum_fusion.tokens_ref, bf16[512,448]{1,0:T(8,128)(2,1)S(1)} %get-tuple-element.426.right_a, bf16[512,448]{1,0:T(8,128)(2,1)S(1)} %get-tuple-element.427.right_b), custom_call_target="tpu_custom_call" | custom-call | flops 1000000000 | bytes 10000000 | tf_op jit(solution)/shard_map/contract/pallas_call | solution.py:149
  103.3 2.8 %collective-permute-done.22 = bf16[256,896]{1,0:T(8,128)(2,1)S(1)} collective-permute-done((bf16[256,896]{1,0:T(8,128)(2,1)S(1)}, bf16[256,896]{1,0:T(8,128)(2,1)S(1)}, u32[]{:S(2)}, u32[]{:S(2)}) %collective-permute-start.22) | collective-permute-done | bytes 458784 | tf_op jit(solution)/shard_map/first_3/ppermute | solution.py:90
  106.3 1.8 %collective-permute-done.21 = bf16[2,256,896]{2,1,0:T(8,128)(2,1)S(1)} collective-permute-done((bf16[2,256,896]{2,1,0:T(8,128)(2,1)S(1)}, bf16[2,256,896]{2,1,0:T(8,128)(2,1)S(1)}, u32[]{:S(2)}, u32[]{:S(2)}) %collective-permute-start.21) | collective-permute-done | bytes 917536 | tf_op jit(solution)/shard_map/seconds_2/ppermute | solution.py:90
  108.2 1.3 collective-permute-start.24
  109.5 1.3 collective-permute-start.25
  110.9 5.0 %collective-permute-done.24 = bf16[256,896]{1,0:T(8,128)(2,1)S(1)} collective-permute-done((bf16[256,896]{1,0:T(8,128)(2,1)S(1)}, bf16[256,896]{1,0:T(8,128)(2,1)S(1)}, u32[]{:S(2)}, u32[]{:S(2)}) %collective-permute-start.24) | collective-permute-done | bytes 458784 | tf_op jit(solution)/shard_map/first_2/ppermute | solution.py:90
  115.9 5.7 %collective-permute-done.25 = bf16[256,896]{1,0:T(8,128)(2,1)S(1)} collective-permute-done((bf16[256,896]{1,0:T(8,128)(2,1)S(1)}, bf16[256,896]{1,0:T(8,128)(2,1)S(1)}, u32[]{:S(2)}, u32[]{:S(2)}) %collective-permute-start.25) | collective-permute-done | bytes 458784 | tf_op jit(solution)/shard_map/three_in/ppermute | solution.py:90
  121.9 1.3 collective-permute-start.28
  123.2 3.1 %collective-permute-start.27 = (bf16[256,896]{1,0:T(8,128)(2,1)S(1)}, bf16[256,896]{1,0:T(8,128)(2,1)S(1)}, u32[]{:S(2)}, u32[]{:S(2)}) collective-permute-start(bf16[256,896]{1,0:T(8,128)(2,1)S(1)} %fusion.69), channel_id=1, source_target_pairs={{4,8},{5,9},{6,10},{7,11},{8,4},{9,5},{10,6},{11,7},{20,24},{21,25... | collective-permute-start | bytes 1376264 | tf_op jit(solution)/shard_map/two/ppermute | solution.py:90
  126.3 4.3 %collective-permute-done.26 = bf16[256,896]{1,0:T(8,128)(2,1)S(1)} collective-permute-done((bf16[256,896]{1,0:T(8,128)(2,1)S(1)}, bf16[256,896]{1,0:T(8,128)(2,1)S(1)}, u32[]{:S(2)}, u32[]{:S(2)}) %collective-permute-start.26) | collective-permute-done | bytes 458784 | tf_op jit(solution)/shard_map/first_1/ppermute | solution.py:90
  130.8 1.8 %collective-permute-done.28 = bf16[256,896]{1,0:T(8,128)(2,1)S(1)} collective-permute-done((bf16[256,896]{1,0:T(8,128)(2,1)S(1)}, bf16[256,896]{1,0:T(8,128)(2,1)S(1)}, u32[]{:S(2)}, u32[]{:S(2)}) %collective-permute-start.28) | collective-permute-done | bytes 458784 | tf_op jit(solution)/shard_map/two_in/ppermute | solution.py:90
  132.8 1.2 collective-permute-done.27
  134.1 3.1 %collective-permute-start.30 = (bf16[256,896]{1,0:T(8,128)(2,1)S(1)}, bf16[256,896]{1,0:T(8,128)(2,1)S(1)}, u32[]{:S(2)}, u32[]{:S(2)}) collective-permute-start(bf16[256,896]{1,0:T(8,128)(2,1)S(1)} %add_convert_fusion.2), channel_id=1, source_target_pairs={{4,8},{5,9},{6,10},{7,11},{8,4},{9,5},{10,6},{11,7},{20,24},{21,25... | collective-permute-start | bytes 1376264 | tf_op jit(solution)/shard_map/three/ppermute | solution.py:90
  137.2 1.6 %collective-permute-start.29 = (bf16[256,896]{1,0:T(8,128)(2,1)S(1)}, bf16[256,896]{1,0:T(8,128)(2,1)S(1)}, u32[]{:S(2)}, u32[]{:S(2)}) collective-permute-start(bf16[256,896]{1,0:T(8,128)(2,1)S(1)} %fusion.73), channel_id=1, source_target_pairs={{0,2},{1,17},{2,0},{3,19},{4,6},{5,21},{6,4},{7,23},{8,10},{9,25},... | collective-permute-start | bytes 1376264 | tf_op jit(solution)/shard_map/first_0/ppermute | solution.py:90
  138.9 3.1 %collective-permute-done.31.refs_3_ = bf16[256,896]{1,0:T(8,128)(2,1)S(1)} collective-permute-done((bf16[256,896]{1,0:T(8,128)(2,1)S(1)}, bf16[256,896]{1,0:T(8,128)(2,1)S(1)}, u32[]{:S(2)}, u32[]{:S(2)}) %collective-permute-start.31) | collective-permute-done | bytes 458784 | tf_op jit(solution)/shard_map/one/ppermute | solution.py:90
  142.1 1.9 %collective-permute-done.30.refs_2_ = bf16[256,896]{1,0:T(8,128)(2,1)S(1)} collective-permute-done((bf16[256,896]{1,0:T(8,128)(2,1)S(1)}, bf16[256,896]{1,0:T(8,128)(2,1)S(1)}, u32[]{:S(2)}, u32[]{:S(2)}) %collective-permute-start.30) | collective-permute-done | bytes 458784 | tf_op jit(solution)/shard_map/three/ppermute | solution.py:90
  145.0 1.3 by_rows.1
  146.3 5.2 %collective-permute-start.32 = (f32[448,256]{1,0:T(8,128)S(1)}, f32[448,256]{1,0:T(8,128)S(1)}, u32[]{:S(2)}, u32[]{:S(2)}) collective-permute-start(f32[448,256]{1,0:T(8,128)S(1)} %get-tuple-element.499), channel_id=1, source_target_pairs={{0,1},{1,0},{2,3},{3,2},{4,5},{5,4},{6,7},{7,6},{8,9},{9,8},{10,11... | collective-permute-start | bytes 1376264 | tf_op jit(solution)/shard_map/taken/ppermute | solution.py:90
  151.6 1.4 collective-permute-done.32.taken_ref
  153.0 1.8 %finish.1 = (f32[448,256]{1,0:T(8,128)}, f32[448,256]{1,0:T(8,128)}, f32[448,256]{1,0:T(8,128)}) custom-call(s32[2]{0:T(128)S(1)} %pad_add_fusion.at_ref, f32[448,256]{1,0:T(8,128)S(1)} %get-tuple-element.498.kept_ref, f32[448,256]{1,0:T(8,128)S(1)} %collective-permute-done.32.taken_ref, bf16[448,512]{1,0:T(8,128)(2,1)S(1)} %copy-done.4, ...), custom_call_target="tpu_custom_call" | custom-call | flops 1000000000 | bytes 10000000 | tf_op jit(solution)/shard_map/finish/pallas_call | solution.py:149
  (82 shorter events, 23.8 us)
Async XLA Ops:
  0.7 1.0 copy-start.1
  1.7 1.0 copy-start.3
  3.5 2.2 %collective-permute-start = (bf16[448,512]{1,0:T(8,128)(2,1)S(1)}, bf16[448,512]{1,0:T(8,128)(2,1)S(1)}, u32[]{:S(2)}, u32[]{:S(2)}) collective-permute-start(bf16[448,512]{1,0:T(8,128)(2,1)S(1)} %get-tuple-element.253), channel_id=1, source_target_pairs={{0,1},{1,0},{2,3},{3,2},{4,5},{5,4},{6,7},{7,6},{8,9},{9,8},{10,11... | collective-permute-start | bytes 1376264 | tf_op jit(solution)/shard_map/coming/ppermute | solution.py:90
  5.7 4.5 %copy-start.2 = (bf16[448,512]{1,0:T(8,128)(2,1)S(1)}, bf16[448,512]{1,0:T(8,128)(2,1)}, u32[]{:S(2)}) copy-start(bf16[448,512]{1,0:T(8,128)(2,1)} %refs_0_.2) | copy-start | bytes 1376260
  6.0 18.9 %collective-permute-start.1 = (bf16[448,7168]{1,0:T(8,128)(2,1)}, bf16[448,7168]{1,0:T(8,128)(2,1)}, u32[]{:S(2)}, u32[]{:S(2)}) collective-permute-start(bf16[448,7168]{1,0:T(8,128)(2,1)} %param.7), channel_id=1, source_target_pairs={{0,1},{1,0},{2,3},{3,2},{4,5},{5,4},{6,7},{7,6},{8,9},{9,8},{10,11... | collective-permute-start | bytes 19267592 | tf_op jit(solution)/shard_map/other_acts/ppermute | solution.py:90
  6.6 13.9 %collective-permute-start.3 = (bf16[896,256]{1,0:T(8,128)(2,1)S(1)}, bf16[896,256]{1,0:T(8,128)(2,1)S(1)}, u32[]{:S(2)}, u32[]{:S(2)}) collective-permute-start(bf16[896,256]{1,0:T(8,128)(2,1)S(1)} %get-tuple-element.273), channel_id=1, source_target_pairs={{4,8},{5,9},{6,10},{7,11},{8,4},{9,5},{10,6},{11,7},{20,24},{21,25... | collective-permute-start | bytes 1376264 | tf_op jit(solution)/shard_map/near/ppermute | solution.py:90
  9.8 11.7 %collective-permute-start.2 = (bf16[896,256]{1,0:T(8,128)(2,1)S(1)}, bf16[896,256]{1,0:T(8,128)(2,1)S(1)}, u32[]{:S(2)}, u32[]{:S(2)}) collective-permute-start(bf16[896,256]{1,0:T(8,128)(2,1)S(1)} %get-tuple-element.273), channel_id=1, source_target_pairs={{0,4},{1,5},{2,6},{3,7},{4,0},{5,1},{6,2},{7,3},{8,12},{9,13},{10,... | collective-permute-start | bytes 1376264 | tf_op jit(solution)/shard_map/one/ppermute | solution.py:90
  9.8 16.7 %collective-permute-start.5 = (bf16[896,256]{1,0:T(8,128)(2,1)S(1)}, bf16[896,256]{1,0:T(8,128)(2,1)S(1)}, u32[]{:S(2)}, u32[]{:S(2)}) collective-permute-start(bf16[896,256]{1,0:T(8,128)(2,1)S(1)} %get-tuple-element.273), channel_id=1, source_target_pairs={{0,2},{1,3},{2,0},{3,1},{4,6},{5,7},{6,4},{7,5},{8,10},{9,11},{10,... | collective-permute-start | bytes 1376264 | tf_op jit(solution)/shard_map/across/ppermute | solution.py:90
  10.8 6.0 %collective-permute-start.4 = (bf16[448,256]{1,0:T(8,128)(2,1)S(1)}, bf16[448,256]{1,0:T(8,128)(2,1)S(1)}, u32[]{:S(2)}, u32[]{:S(2)}) collective-permute-start(bf16[448,256]{1,0:T(8,128)(2,1)S(1)} %get-tuple-element.256), channel_id=1, source_target_pairs={{0,1},{1,0},{2,3},{3,2},{4,5},{5,4},{6,7},{7,6},{8,9},{9,8},{10,11... | collective-permute-start | bytes 688136 | tf_op jit(solution)/shard_map/other_up/ppermute | solution.py:90
  21.5 14.1 %collective-permute-start.7 = (bf16[896,256]{1,0:T(8,128)(2,1)S(1)}, bf16[896,256]{1,0:T(8,128)(2,1)S(1)}, u32[]{:S(2)}, u32[]{:S(2)}) collective-permute-start(bf16[896,256]{1,0:T(8,128)(2,1)S(1)} %collective-permute-done.2), channel_id=1, source_target_pairs={{4,8},{5,9},{6,10},{7,11},{8,4},{9,5},{10,6},{11,7},{20,24},{21,25... | collective-permute-start | bytes 1376264 | tf_op jit(solution)/shard_map/two_in/ppermute | solution.py:90
  23.6 12.0 %collective-permute-start.6 = (bf16[896,256]{1,0:T(8,128)(2,1)S(1)}, bf16[896,256]{1,0:T(8,128)(2,1)S(1)}, u32[]{:S(2)}, u32[]{:S(2)}) collective-permute-start(bf16[896,256]{1,0:T(8,128)(2,1)S(1)} %collective-permute-done.3), channel_id=1, source_target_pairs={{4,0},{5,1},{6,2},{7,3},{8,12},{9,13},{10,14},{11,15},{20,16},{21,... | collective-permute-start | bytes 1376264 | tf_op jit(solution)/shard_map/two_out/ppermute | solution.py:90
  25.0 20.6 %collective-permute-start.11 = (bf16[896,256]{1,0:T(8,128)(2,1)S(1)}, bf16[896,256]{1,0:T(8,128)(2,1)S(1)}, u32[]{:S(2)}, u32[]{:S(2)}) collective-permute-start(bf16[896,256]{1,0:T(8,128)(2,1)S(1)} %collective-permute-done.2), channel_id=1, source_target_pairs={{0,16},{1,3},{2,18},{3,1},{4,20},{5,7},{6,22},{7,5},{8,24},{9,11},... | collective-permute-start | bytes 1376264 | tf_op jit(solution)/shard_map/one_second/ppermute | solution.py:90
  25.3 14.6 %collective-permute-start.10 = (bf16[896,256]{1,0:T(8,128)(2,1)S(1)}, bf16[896,256]{1,0:T(8,128)(2,1)S(1)}, u32[]{:S(2)}, u32[]{:S(2)}) collective-permute-start(bf16[896,256]{1,0:T(8,128)(2,1)S(1)} %collective-permute-done.2), channel_id=1, source_target_pairs={{0,2},{1,17},{2,0},{3,19},{4,6},{5,21},{6,4},{7,23},{8,10},{9,25},... | collective-permute-start | bytes 1376264 | tf_op jit(solution)/shard_map/one_first/ppermute | solution.py:90
  26.6 16.2 %collective-permute-start.9 = (bf16[896,256]{1,0:T(8,128)(2,1)S(1)}, bf16[896,256]{1,0:T(8,128)(2,1)S(1)}, u32[]{:S(2)}, u32[]{:S(2)}) collective-permute-start(bf16[896,256]{1,0:T(8,128)(2,1)S(1)} %broadcast_select_fusion), channel_id=1, source_target_pairs={{0,2},{1,17},{2,0},{3,19},{4,6},{5,21},{6,4},{7,23},{8,10},{9,25},... | collective-permute-start | bytes 1376264 | tf_op jit(solution)/shard_map/corner/ppermute | solution.py:90
  35.8 17.2 %collective-permute-start.12 = (bf16[896,256]{1,0:T(8,128)(2,1)S(1)}, bf16[896,256]{1,0:T(8,128)(2,1)S(1)}, u32[]{:S(2)}, u32[]{:S(2)}) collective-permute-start(bf16[896,256]{1,0:T(8,128)(2,1)S(1)} %add.197), channel_id=1, source_target_pairs={{0,2},{1,17},{2,0},{3,19},{4,6},{5,21},{6,4},{7,23},{8,10},{9,25},... | collective-permute-start | bytes 1376264 | tf_op jit(solution)/shard_map/two_first/ppermute | solution.py:90
  37.1 10.1 %collective-permute-start.8 = (bf16[896,256]{1,0:T(8,128)(2,1)S(1)}, bf16[896,256]{1,0:T(8,128)(2,1)S(1)}, u32[]{:S(2)}, u32[]{:S(2)}) collective-permute-start(bf16[896,256]{1,0:T(8,128)(2,1)S(1)} %add.197), channel_id=1, source_target_pairs={{4,0},{5,1},{6,2},{7,3},{8,12},{9,13},{10,14},{11,15},{20,16},{21,... | collective-permute-start | bytes 1376264 | tf_op jit(solution)/shard_map/three_out/ppermute | solution.py:90
  43.4 8.9 %collective-permute-start.13 = (bf16[896,256]{1,0:T(8,128)(2,1)S(1)}, bf16[896,256]{1,0:T(8,128)(2,1)S(1)}, u32[]{:S(2)}, u32[]{:S(2)}) collective-permute-start(bf16[896,256]{1,0:T(8,128)(2,1)S(1)} %collective-permute-done.10), channel_id=1, source_target_pairs={{0,16},{1,3},{2,18},{3,1},{4,20},{5,7},{6,22},{7,5},{8,24},{9,11},... | collective-permute-start | bytes 1376264 | tf_op jit(solution)/shard_map/one_both/ppermute | solution.py:90
  44.7 16.1 %collective-permute-start.15 = (bf16[896,256]{1,0:T(8,128)(2,1)S(1)}, bf16[896,256]{1,0:T(8,128)(2,1)S(1)}, u32[]{:S(2)}, u32[]{:S(2)}) collective-permute-start(bf16[896,256]{1,0:T(8,128)(2,1)S(1)} %add.197), channel_id=1, source_target_pairs={{0,16},{1,3},{2,18},{3,1},{4,20},{5,7},{6,22},{7,5},{8,24},{9,11},... | collective-permute-start | bytes 1376264 | tf_op jit(solution)/shard_map/two_second/ppermute | solution.py:90
  47.3 25.3 %collective-permute-start.18 = (bf16[896,256]{1,0:T(8,128)(2,1)S(1)}, bf16[896,256]{1,0:T(8,128)(2,1)S(1)}, u32[]{:S(2)}, u32[]{:S(2)}) collective-permute-start(bf16[896,256]{1,0:T(8,128)(2,1)S(1)} %add.209), channel_id=1, source_target_pairs={{0,16},{1,3},{2,18},{3,1},{4,20},{5,7},{6,22},{7,5},{8,24},{9,11},... | collective-permute-start | bytes 1376264 | tf_op jit(solution)/shard_map/three_second/ppermute | solution.py:90
  48.3 13.1 %collective-permute-start.14 = (bf16[896,256]{1,0:T(8,128)(2,1)S(1)}, bf16[896,256]{1,0:T(8,128)(2,1)S(1)}, u32[]{:S(2)}, u32[]{:S(2)}) collective-permute-start(bf16[896,256]{1,0:T(8,128)(2,1)S(1)} %add.209), channel_id=1, source_target_pairs={{0,2},{1,17},{2,0},{3,19},{4,6},{5,21},{6,4},{7,23},{8,10},{9,25},... | collective-permute-start | bytes 1376264 | tf_op jit(solution)/shard_map/three_first/ppermute | solution.py:90
  53.0 19.0 %collective-permute-start.17 = (bf16[896,256]{1,0:T(8,128)(2,1)S(1)}, bf16[896,256]{1,0:T(8,128)(2,1)S(1)}, u32[]{:S(2)}, u32[]{:S(2)}) collective-permute-start(bf16[896,256]{1,0:T(8,128)(2,1)S(1)} %collective-permute-done.12), channel_id=1, source_target_pairs={{0,16},{1,3},{2,18},{3,1},{4,20},{5,7},{6,22},{7,5},{8,24},{9,11},... | collective-permute-start | bytes 1376264 | tf_op jit(solution)/shard_map/two_both/ppermute | solution.py:90
  61.4 15.5 %collective-permute-start.16 = (bf16[896,256]{1,0:T(8,128)(2,1)S(1)}, bf16[896,256]{1,0:T(8,128)(2,1)S(1)}, u32[]{:S(2)}, u32[]{:S(2)}) collective-permute-start(bf16[896,256]{1,0:T(8,128)(2,1)S(1)} %collective-permute-done.14), channel_id=1, source_target_pairs={{0,16},{1,3},{2,18},{3,1},{4,20},{5,7},{6,22},{7,5},{8,24},{9,11},... | collective-permute-start | bytes 1376264 | tf_op jit(solution)/shard_map/three_both/ppermute | solution.py:90
  73.3 4.3 %copy-start = (f32[128]{0:T(128)S(1)}, f32[128]{0:T(128)}, u32[]{:S(2)}) copy-start(f32[128]{0:T(128)} %param.11) | copy-start | bytes 1540
  80.7 12.6 %collective-permute-start.19 = (bf16[2,256,896]{2,1,0:T(8,128)(2,1)S(1)}, bf16[2,256,896]{2,1,0:T(8,128)(2,1)S(1)}, u32[]{:S(2)}, u32[]{:S(2)}) collective-permute-start(bf16[2,256,896]{2,1,0:T(8,128)(2,1)S(1)} %get-tuple-element.404), channel_id=1, source_target_pairs={{0,16},{1,3},{2,18},{3,1},{4,20},{5,7},{6,22},{7,5},{8,24},{9,11},... | collective-permute-start | bytes 2752520 | tf_op jit(solution)/shard_map/seconds_3/ppermute | solution.py:90
  83.0 20.0 %collective-permute-start.20 = (bf16[2,256,896]{2,1,0:T(8,128)(2,1)S(1)}, bf16[2,256,896]{2,1,0:T(8,128)(2,1)S(1)}, u32[]{:S(2)}, u32[]{:S(2)}) collective-permute-start(bf16[2,256,896]{2,1,0:T(8,128)(2,1)S(1)} %contract.7), channel_id=1, source_target_pairs={{0,4},{1,5},{2,6},{3,7},{4,0},{5,1},{6,2},{7,3},{8,12},{9,13},{10,... | collective-permute-start | bytes 2752520 | tf_op jit(solution)/shard_map/raw_1/ppermute | solution.py:90
  85.0 23.1 %collective-permute-start.21 = (bf16[2,256,896]{2,1,0:T(8,128)(2,1)S(1)}, bf16[2,256,896]{2,1,0:T(8,128)(2,1)S(1)}, u32[]{:S(2)}, u32[]{:S(2)}) collective-permute-start(bf16[2,256,896]{2,1,0:T(8,128)(2,1)S(1)} %contract.8), channel_id=1, source_target_pairs={{0,16},{1,3},{2,18},{3,1},{4,20},{5,7},{6,22},{7,5},{8,24},{9,11},... | collective-permute-start | bytes 2752520 | tf_op jit(solution)/shard_map/seconds_2/ppermute | solution.py:90
  93.4 12.7 %collective-permute-start.22 = (bf16[256,896]{1,0:T(8,128)(2,1)S(1)}, bf16[256,896]{1,0:T(8,128)(2,1)S(1)}, u32[]{:S(2)}, u32[]{:S(2)}) collective-permute-start(bf16[256,896]{1,0:T(8,128)(2,1)S(1)} %fusion.71), channel_id=1, source_target_pairs={{0,2},{1,17},{2,0},{3,19},{4,6},{5,21},{6,4},{7,23},{8,10},{9,25},... | collective-permute-start | bytes 1376264 | tf_op jit(solution)/shard_map/first_3/ppermute | solution.py:90
  108.2 7.7 %collective-permute-start.24 = (bf16[256,896]{1,0:T(8,128)(2,1)S(1)}, bf16[256,896]{1,0:T(8,128)(2,1)S(1)}, u32[]{:S(2)}, u32[]{:S(2)}) collective-permute-start(bf16[256,896]{1,0:T(8,128)(2,1)S(1)} %fusion.72), channel_id=1, source_target_pairs={{0,2},{1,17},{2,0},{3,19},{4,6},{5,21},{6,4},{7,23},{8,10},{9,25},... | collective-permute-start | bytes 1376264 | tf_op jit(solution)/shard_map/first_2/ppermute | solution.py:90
  109.5 12.0 %collective-permute-start.25 = (bf16[256,896]{1,0:T(8,128)(2,1)S(1)}, bf16[256,896]{1,0:T(8,128)(2,1)S(1)}, u32[]{:S(2)}, u32[]{:S(2)}) collective-permute-start(bf16[256,896]{1,0:T(8,128)(2,1)S(1)} %fusion.70), channel_id=1, source_target_pairs={{0,4},{1,5},{2,6},{3,7},{12,8},{13,9},{14,10},{15,11},{16,20},{17,... | collective-permute-start | bytes 1376264 | tf_op jit(solution)/shard_map/three_in/ppermute | solution.py:90
  110.8 19.9 %collective-permute-start.23 = (bf16[2,256,896]{2,1,0:T(8,128)(2,1)S(1)}, bf16[2,256,896]{2,1,0:T(8,128)(2,1)S(1)}, u32[]{:S(2)}, u32[]{:S(2)}) collective-permute-start(bf16[2,256,896]{2,1,0:T(8,128)(2,1)S(1)} %add_convert_fusion), channel_id=1, source_target_pairs={{0,16},{1,3},{2,18},{3,1},{4,20},{5,7},{6,22},{7,5},{8,24},{9,11},... | collective-permute-start | bytes 2752520 | tf_op jit(solution)/shard_map/seconds_0/ppermute | solution.py:90
  121.8 8.8 %collective-permute-start.26 = (bf16[256,896]{1,0:T(8,128)(2,1)S(1)}, bf16[256,896]{1,0:T(8,128)(2,1)S(1)}, u32[]{:S(2)}, u32[]{:S(2)}) collective-permute-start(bf16[256,896]{1,0:T(8,128)(2,1)S(1)} %fusion.74), channel_id=1, source_target_pairs={{0,2},{1,17},{2,0},{3,19},{4,6},{5,21},{6,4},{7,23},{8,10},{9,25},... | collective-permute-start | bytes 1376264 | tf_op jit(solution)/shard_map/first_1/ppermute | solution.py:90
  121.9 10.8 %collective-permute-start.28 = (bf16[256,896]{1,0:T(8,128)(2,1)S(1)}, bf16[256,896]{1,0:T(8,128)(2,1)S(1)}, u32[]{:S(2)}, u32[]{:S(2)}) collective-permute-start(bf16[256,896]{1,0:T(8,128)(2,1)S(1)} %fusion.69), channel_id=1, source_target_pairs={{0,4},{1,5},{2,6},{3,7},{12,8},{13,9},{14,10},{15,11},{16,20},{17,... | collective-permute-start | bytes 1376264 | tf_op jit(solution)/shard_map/two_in/ppermute | solution.py:90
  123.2 10.8 %collective-permute-start.27 = (bf16[256,896]{1,0:T(8,128)(2,1)S(1)}, bf16[256,896]{1,0:T(8,128)(2,1)S(1)}, u32[]{:S(2)}, u32[]{:S(2)}) collective-permute-start(bf16[256,896]{1,0:T(8,128)(2,1)S(1)} %fusion.69), channel_id=1, source_target_pairs={{4,8},{5,9},{6,10},{7,11},{8,4},{9,5},{10,6},{11,7},{20,24},{21,25... | collective-permute-start | bytes 1376264 | tf_op jit(solution)/shard_map/two/ppermute | solution.py:90
  134.0 8.0 %collective-permute-start.31 = (bf16[256,896]{1,0:T(8,128)(2,1)S(1)}, bf16[256,896]{1,0:T(8,128)(2,1)S(1)}, u32[]{:S(2)}, u32[]{:S(2)}) collective-permute-start(bf16[256,896]{1,0:T(8,128)(2,1)S(1)} %add_convert_fusion.1), channel_id=1, source_target_pairs={{0,4},{1,5},{2,6},{3,7},{4,0},{5,1},{6,2},{7,3},{8,12},{9,13},{10,... | collective-permute-start | bytes 1376264 | tf_op jit(solution)/shard_map/one/ppermute | solution.py:90
  134.1 9.8 %collective-permute-start.30 = (bf16[256,896]{1,0:T(8,128)(2,1)S(1)}, bf16[256,896]{1,0:T(8,128)(2,1)S(1)}, u32[]{:S(2)}, u32[]{:S(2)}) collective-permute-start(bf16[256,896]{1,0:T(8,128)(2,1)S(1)} %add_convert_fusion.2), channel_id=1, source_target_pairs={{4,8},{5,9},{6,10},{7,11},{8,4},{9,5},{10,6},{11,7},{20,24},{21,25... | collective-permute-start | bytes 1376264 | tf_op jit(solution)/shard_map/three/ppermute | solution.py:90
  137.2 7.8 %collective-permute-start.29 = (bf16[256,896]{1,0:T(8,128)(2,1)S(1)}, bf16[256,896]{1,0:T(8,128)(2,1)S(1)}, u32[]{:S(2)}, u32[]{:S(2)}) collective-permute-start(bf16[256,896]{1,0:T(8,128)(2,1)S(1)} %fusion.73), channel_id=1, source_target_pairs={{0,2},{1,17},{2,0},{3,19},{4,6},{5,21},{6,4},{7,23},{8,10},{9,25},... | collective-permute-start | bytes 1376264 | tf_op jit(solution)/shard_map/first_0/ppermute | solution.py:90
  145.0 8.0 %copy-start.4 = (bf16[448,512]{1,0:T(8,128)(2,1)S(1)}, bf16[448,512]{1,0:T(8,128)(2,1)}, u32[]{:S(2)}) copy-start(bf16[448,512]{1,0:T(8,128)(2,1)} %probe_ref.1) | copy-start | bytes 1376260
  145.0 8.0 %copy-start.5 = (f32[448,256]{1,0:T(8,128)S(1)}, f32[448,256]{1,0:T(8,128)}, u32[]{:S(2)}) copy-start(f32[448,256]{1,0:T(8,128)} %momentum_ref) | copy-start | bytes 1376260
  145.0 8.0 %copy-start.6 = (f32[448,256]{1,0:T(8,128)S(1)}, f32[448,256]{1,0:T(8,128)}, u32[]{:S(2)}) copy-start(f32[448,256]{1,0:T(8,128)} %curvature_ref.1) | copy-start | bytes 1376260
  146.3 6.6 %collective-permute-start.32 = (f32[448,256]{1,0:T(8,128)S(1)}, f32[448,256]{1,0:T(8,128)S(1)}, u32[]{:S(2)}, u32[]{:S(2)}) collective-permute-start(f32[448,256]{1,0:T(8,128)S(1)} %get-tuple-element.499), channel_id=1, source_target_pairs={{0,1},{1,0},{2,3},{3,2},{4,5},{5,4},{6,7},{7,6},{8,9},{9,8},{10,11... | collective-permute-start | bytes 1376264 | tf_op jit(solution)/shard_map/taken/ppermute | solution.py:90

commit v4 on v3

--- a/solution.py
+++ b/solution.py
@@ -145,12 +145,13 @@
 SMEM = pl.BlockSpec(memory_space=pltpu.SMEM)
 
 
-def call(kernel, outs, scalars, *operands, name, cost=10**7):
+def call(kernel, outs, scalars, *operands, name, cost=10**7, aliases=None):
     return pl.pallas_call(
         kernel,
         out_shape=outs,
         in_specs=[SMEM] + [VMEM] * len(operands),
         out_specs=jax.tree.map(lambda _: VMEM, outs),
+        input_output_aliases=aliases or {},
         cost_estimate=pl.CostEstimate(flops=100 * cost, bytes_accessed=cost, transcendentals=0),
         compiler_params=pltpu.CompilerParams(vmem_limit_bytes=24 * 2**20),
         name=name,
@@ -297,6 +298,22 @@
     return call(kernel, [out] * 3, scalars, kept, taken, probe, momentum, curvature, name="finish")
 
 
+def unit_rows(scalars, head, weight, probe, units=()):
+    rows = weight.shape[0]
+
+    def kernel(at_ref, weight_ref, probe_ref, *refs):
+        y, c = at_ref[0], at_ref[1]
+        place = pl.ds(pl.multiple_of(at_ref[2] * rows, 16), rows)
+        for side, out_ref in zip((y, 1 - y), refs[-2:]):
+            column = pl.ds(pl.multiple_of((2 * side + c) * head, 128), head)
+            for j, ref in enumerate((weight_ref, probe_ref)):
+                out_ref[place, pl.ds(j * head, head)] = ref[:, column]
+
+    out = jax.ShapeDtypeStruct((2 * rows, 2 * head), weight.dtype)
+    aliases = {3: 0, 4: 1} if units else {}
+    return call(kernel, [out, out], scalars, weight, probe, *units, name="unit_rows", aliases=aliases)
+
+
 def columns_by_core(scalars, head, *arrays):
     rows = arrays[0].shape[0]
 
@@ -320,19 +337,13 @@
     y, z, x, c = lax.axis_index("dp"), place // 4, (place // 2) % 2, place % 2
     own_first = c == 0
 
-    leaving, staying = columns_by_core((y, c), head, k_weight, probe)
-    coming = send(leaving, to_core, "coming")
-    up_leaving, own_up = columns_by_core((y, c), head, after(upstream, leaving))
+    other_weight, other_probe = send(k_weight, to_core, "other_weight"), send(probe, to_core, "other_probe")
+    own_rows = unit_rows((y, c, c), head, k_weight, probe)
+    mine, beside = unit_rows((y, c, 1 - c), head, other_weight, other_probe, own_rows)
+    up_leaving, own_up = columns_by_core((y, c), head, after(upstream, mine))
     other_up = send(up_leaving, to_core, "other_up")
-    chip_rows = jnp.where(
-        own_first,
-        jnp.concatenate([staying, coming], axis=0),
-        jnp.concatenate([coming, staying], axis=0),
-    )
-    mine, beside = chip_rows[:, : 2 * head], chip_rows[:, 2 * head :]
-
     order = Order(momentum)
-    other_acts = send(after(acts, chip_rows), to_core, "other_acts")
+    other_acts = send(after(acts, mine), to_core, "other_acts")
     one = send(mine, Z_ONE, "one")
     near = send(mine, Z_MIDDLE, "near")
     across = send(mine, to_x, "across")
@@ -342,7 +353,6 @@
     two_in = send(one, Z_MIDDLE, "two_in")
     other_acts, one = order.wait(other_acts, one)
     one_first = send(one, to_first, "one_first")
-    one_second = send(one, to_second, "one_second")
     corner = order.run(lambda a, b: jnp.where(own_first, a, b), beside, across)
     corner = send(corner, to_corner, "corner")
     tokens = order.run(lambda a, b: jnp.concatenate([a, b], axis=0), acts, other_acts)
@@ -372,21 +382,23 @@
     two_second = send(two, to_second, "two_second")
     both_sum = add_product(both_sum, 0, 1, corner)
     first_sum = add_product(None, 1, 1 - c, one_first)
-    second_sum = add_product(None, 1, c, one_second)
     own_sum = add_product(own_sum, 2, 0, two)
     three = order.run(jnp.add, near, three_out)
     three_first = send(three, to_first, "three_first")
+    flip = order.run(lambda a, b: jnp.where(own_first, a, b), beside, across)
+    one_second = send(flip, Z_ONE, "one_second")
     three_second = send(three, to_second, "three_second")
     both_sum = add_product(both_sum, 1, 1, one_both)
     two_first = order.wait(two_first)
     two_both = send(two_first, to_second, "two_both")
     first_sum = add_product(first_sum, 2, 1 - c, two_first)
     own_sum = add_product(own_sum, 3, 0, three)
-    second_sum = add_product(second_sum, 2, c, two_second)
+    second_sum = add_product(None, 2, c, two_second)
     three_first = order.wait(three_first)
     three_both = send(three_first, to_second, "three_both")
     first_sum = add_product(first_sum, 3, 1 - c, three_first)
     both_sum = add_product(both_sum, 2, 1, two_both)
+    second_sum = add_product(second_sum, 1, c, one_second)
     second_sum = add_product(second_sum, 3, c, three_second)
     both_sum = add_product(both_sum, 3, 1, three_both)
 
@@ -426,12 +438,12 @@
     sum_3 = rounded(1, kept_3, seconds_3, first_3)
     three_in = send(sum_3, Z_IN, "three_in")
     first_2 = send(rounded(0, kept_2, seconds_2), to_first, "first_2")
+    first_1 = send(order.run(lambda kept: kept[0].astype(jnp.bfloat16), kept_1), to_first, "first_1")
     leaving_0 = order.wait(leaving_0)
     seconds_0 = send(leaving_0, to_second, "seconds_0")
     sum_2 = rounded(1, kept_2, seconds_2, first_2, three_in)
     two_in = send(sum_2, Z_IN, "two_in")
     two = send(sum_2, Z_MIDDLE, "two")
-    first_1 = send(order.run(lambda kept: kept[0].astype(jnp.bfloat16), kept_1), to_first, "first_1")
     own_1 = order.run(lambda kept, got: total_of(kept[1], got), kept_1, first_1)
     first_0 = send(rounded(0, kept_0, seconds_0), to_first, "first_0")
     three = send(sum_of(sum_3, two_in), Z_MIDDLE, "three")

time: 156 us -> 152 us (0.974)
  waiting for transfers between devices: 72.8 us -> 69.6 us
    ppermute x33 -> x34, waiting for transfers between devices: 72.8 us -> 69.6 us  [send(): return lax.ppermute(value, AXES, pairs_of(move))]
    pallas_call x12 -> x13, Pallas kernels: 20.7 us -> 21.2 us  [call(): pl.pallas_call(kernel, out_shape=outs, in_specs=[SMEM] + [VMEM] * len(ope...]
    ppermute x33 -> x34, starting transfers between devices: 38.6 us -> 38.3 us  [send(): return lax.ppermute(value, AXES, pairs_of(move))]
  transfers between devices with their start and end apart: 33 -> 34, of which waited for: 23 -> 21; matrix products, arithmetic and copies ran while one was open for 12% -> 12% of each run, Pallas kernels for 9% -> 9%
where the time goes in v4:
time: 152 us
  waiting for transfers between devices  69.6 us (46%)
  starting transfers between devices  38.3 us (25%)
  Pallas kernels  21.2 us (14%)
  matrix products  10.4 us (7%)
  other arithmetic  8.81 us (6%)
  local copies, waits for them, and re-layouts  2.11 us (1%)
    ppermute x34, waiting for transfers between devices, send(): return lax.ppermute(value, AXES, pairs_of(move))  69.6 us
    ppermute x34, starting transfers between devices, send(): return lax.ppermute(value, AXES, pairs_of(move))  38.3 us
    pallas_call x13, Pallas kernels, call(): pl.pallas_call(kernel, out_shape=outs, in_specs=[SMEM] + [VMEM] * len(ope...  21.2 us
    dot_general x16, matrix products, product(): jnp.dot(block_of(held, slot, flip_x), unit, preferred_element_type=jnp.fl...  10.4 us
    concatenate x1, other arithmetic, by_links(): jnp.concatenate([a, b], axis=0)  6.77 us
  transfers between devices with their start and end apart: 34, of which 21 were waited for; matrix products, arithmetic and copies ran while one was open for 12% of the time, Pallas kernels for 9%

profile of v4, /device:TPU:11, one launch (start us, length us, event | category | flops | bytes accessed | tf_op | source)
XLA Modules:
  0.0 151.5 jit_solution(8163077474522333497)
XLA Ops:
  5.4 3.2 %collective-permute-start.4 = (bf16[896,256]{1,0:T(8,128)(2,1)S(1)}, bf16[896,256]{1,0:T(8,128)(2,1)S(1)}, u32[]{:S(2)}, u32[]{:S(2)}) collective-permute-start(bf16[896,256]{1,0:T(8,128)(2,1)S(1)} %get-tuple-element.282), channel_id=1, source_target_pairs={{4,8},{5,9},{6,10},{7,11},{8,4},{9,5},{10,6},{11,7},{20,24},{21,25... | collective-permute-start | bytes 1376264 | tf_op jit(solution)/shard_map/near/ppermute | solution.py:90
  10.5 5.2 %collective-permute-done.5.up_b = bf16[448,256]{1,0:T(8,128)(2,1)S(1)} collective-permute-done((bf16[448,256]{1,0:T(8,128)(2,1)S(1)}, bf16[448,256]{1,0:T(8,128)(2,1)S(1)}, u32[]{:S(2)}, u32[]{:S(2)}) %collective-permute-start.5) | collective-permute-done | bytes 229408 | tf_op jit(solution)/shard_map/other_up/ppermute | solution.py:90
  15.7 3.7 %collective-permute-done.4 = bf16[896,256]{1,0:T(8,128)(2,1)S(1)} collective-permute-done((bf16[896,256]{1,0:T(8,128)(2,1)S(1)}, bf16[896,256]{1,0:T(8,128)(2,1)S(1)}, u32[]{:S(2)}, u32[]{:S(2)}) %collective-permute-start.4) | collective-permute-done | bytes 458784 | tf_op jit(solution)/shard_map/near/ppermute | solution.py:90
  20.5 2.1 %collective-permute-start.8 = (bf16[896,256]{1,0:T(8,128)(2,1)S(1)}, bf16[896,256]{1,0:T(8,128)(2,1)S(1)}, u32[]{:S(2)}, u32[]{:S(2)}) collective-permute-start(bf16[896,256]{1,0:T(8,128)(2,1)S(1)} %collective-permute-done.3), channel_id=1, source_target_pairs={{4,8},{5,9},{6,10},{7,11},{8,4},{9,5},{10,6},{11,7},{20,24},{21,25... | collective-permute-start | bytes 1376264 | tf_op jit(solution)/shard_map/two_in/ppermute | solution.py:90
  22.6 1.3 collective-permute-start.7
  24.0 1.3 collective-permute-start.10
  25.6 6.8 %pad_maximum_fusion.tokens_ref = bf16[896,7168]{1,0:T(8,128)(2,1)S(1)} fusion(bf16[448,7168]{1,0:T(8,128)(2,1)} %collective-permute-done.2, bf16[448,7168]{1,0:T(8,128)(2,1)} %param.7), kind=kLoop, calls=%fused_computation | loop fusion | flops 25690112 | bytes 25690112 | tf_op jit(solution)/shard_map/concatenate | solution.py:358
  34.4 1.3 collective-permute-start.12
  35.7 2.6 %collective-permute-start.9 = (bf16[896,256]{1,0:T(8,128)(2,1)S(1)}, bf16[896,256]{1,0:T(8,128)(2,1)S(1)}, u32[]{:S(2)}, u32[]{:S(2)}) collective-permute-start(bf16[896,256]{1,0:T(8,128)(2,1)S(1)} %add.197), channel_id=1, source_target_pairs={{4,0},{5,1},{6,2},{7,3},{8,12},{9,13},{10,14},{11,15},{20,16},{21,... | collective-permute-start | bytes 1376264 | tf_op jit(solution)/shard_map/three_out/ppermute | solution.py:90
  40.0 1.2 collective-permute-start.15
  42.5 4.1 %collective-permute-done.9 = bf16[896,256]{1,0:T(8,128)(2,1)S(1)} collective-permute-done((bf16[896,256]{1,0:T(8,128)(2,1)S(1)}, bf16[896,256]{1,0:T(8,128)(2,1)S(1)}, u32[]{:S(2)}, u32[]{:S(2)}) %collective-permute-start.9) | collective-permute-done | bytes 458784 | tf_op jit(solution)/shard_map/three_out/ppermute | solution.py:90
  47.0 2.5 %collective-permute-done.13 = bf16[896,256]{1,0:T(8,128)(2,1)S(1)} collective-permute-done((bf16[896,256]{1,0:T(8,128)(2,1)S(1)}, bf16[896,256]{1,0:T(8,128)(2,1)S(1)}, u32[]{:S(2)}, u32[]{:S(2)}) %collective-permute-start.13) | collective-permute-done | bytes 458784 | tf_op jit(solution)/shard_map/one_both/ppermute | solution.py:90
  52.7 3.3 %collective-permute-done.15 = bf16[896,256]{1,0:T(8,128)(2,1)S(1)} collective-permute-done((bf16[896,256]{1,0:T(8,128)(2,1)S(1)}, bf16[896,256]{1,0:T(8,128)(2,1)S(1)}, u32[]{:S(2)}, u32[]{:S(2)}) %collective-permute-start.15) | collective-permute-done | bytes 458784 | tf_op jit(solution)/shard_map/two_second/ppermute | solution.py:90
  56.6 2.9 %collective-permute-done.14 = bf16[896,256]{1,0:T(8,128)(2,1)S(1)} collective-permute-done((bf16[896,256]{1,0:T(8,128)(2,1)S(1)}, bf16[896,256]{1,0:T(8,128)(2,1)S(1)}, u32[]{:S(2)}, u32[]{:S(2)}) %collective-permute-start.14) | collective-permute-done | bytes 458784 | tf_op jit(solution)/shard_map/three_first/ppermute | solution.py:90
  59.5 1.4 collective-permute-start.16
  61.5 7.6 %collective-permute-done.17 = bf16[896,256]{1,0:T(8,128)(2,1)S(1)} collective-permute-done((bf16[896,256]{1,0:T(8,128)(2,1)S(1)}, bf16[896,256]{1,0:T(8,128)(2,1)S(1)}, u32[]{:S(2)}, u32[]{:S(2)}) %collective-permute-start.17) | collective-permute-done | bytes 458784 | tf_op jit(solution)/shard_map/two_both/ppermute | solution.py:90
  71.1 2.9 %collective-permute-done.16 = bf16[896,256]{1,0:T(8,128)(2,1)S(1)} collective-permute-done((bf16[896,256]{1,0:T(8,128)(2,1)S(1)}, bf16[896,256]{1,0:T(8,128)(2,1)S(1)}, u32[]{:S(2)}, u32[]{:S(2)}) %collective-permute-start.16) | collective-permute-done | bytes 458784 | tf_op jit(solution)/shard_map/three_both/ppermute | solution.py:90
  74.7 3.2 %head_gradients.1 = (bf16[512,448]{1,0:T(8,128)(2,1)S(1)}, bf16[512,448]{1,0:T(8,128)(2,1)S(1)}, bf16[2,256,896]{2,1,0:T(8,128)(2,1)S(1)}) custom-call(s32[3]{0:T(128)S(1)} %get-tuple-element.518.at_ref, bf16[896,7168]{1,0:T(8,128)(2,1)S(1)} %pad_maximum_fusion.tokens_ref, f32[896,256]{1,0:T(8,128)S(1)} %fusion.50.own_ref, f32[896,256]{1,0:T(8,128)S(1)} %fusion.65.both_ref, ...), custom_call_target="tpu_custom_call" | custom-call | flops 1000000000 | bytes 10000000 | tf_op jit(solution)/shard_map/head_gradients/pallas_call | solution.py:149
  78.3 1.8 %contract.7 = bf16[2,256,896]{2,1,0:T(8,128)(2,1)S(1)} custom-call(s32[3]{0:T(128)S(1)} %get-tuple-element.519.at_ref, bf16[896,7168]{1,0:T(8,128)(2,1)S(1)} %pad_maximum_fusion.tokens_ref, bf16[512,448]{1,0:T(8,128)(2,1)S(1)} %get-tuple-element.440.right_a, bf16[512,448]{1,0:T(8,128)(2,1)S(1)} %get-tuple-element.441.right_b), custom_call_target="tpu_custom_call" | custom-call | flops 1000000000 | bytes 10000000 | tf_op jit(solution)/shard_map/contract/pallas_call | solution.py:149
  80.5 1.8 %contract.8 = bf16[2,256,896]{2,1,0:T(8,128)(2,1)S(1)} custom-call(s32[3]{0:T(128)S(1)} %get-tuple-element.520.at_ref, bf16[896,7168]{1,0:T(8,128)(2,1)S(1)} %pad_maximum_fusion.tokens_ref, bf16[512,448]{1,0:T(8,128)(2,1)S(1)} %get-tuple-element.440.right_a, bf16[512,448]{1,0:T(8,128)(2,1)S(1)} %get-tuple-element.441.right_b), custom_call_target="tpu_custom_call" | custom-call | flops 1000000000 | bytes 10000000 | tf_op jit(solution)/shard_map/contract/pallas_call | solution.py:149
  82.4 1.2 collective-permute-start.22
  83.6 2.1 %contract.9 = f32[2,256,896]{2,1,0:T(8,128)S(1)} custom-call(s32[3]{0:T(128)S(1)} %get-tuple-element.518.at_ref, bf16[896,7168]{1,0:T(8,128)(2,1)S(1)} %pad_maximum_fusion.tokens_ref, bf16[512,448]{1,0:T(8,128)(2,1)S(1)} %get-tuple-element.440.right_a, bf16[512,448]{1,0:T(8,128)(2,1)S(1)} %get-tuple-element.441.right_b), custom_call_target="tpu_custom_call" | custom-call | flops 1000000000 | bytes 10000000 | tf_op jit(solution)/shard_map/contract/pallas_call | solution.py:149
  85.7 4.8 %collective-permute-done.20 = bf16[2,256,896]{2,1,0:T(8,128)(2,1)S(1)} collective-permute-done((bf16[2,256,896]{2,1,0:T(8,128)(2,1)S(1)}, bf16[2,256,896]{2,1,0:T(8,128)(2,1)S(1)}, u32[]{:S(2)}, u32[]{:S(2)}) %collective-permute-start.20) | collective-permute-done | bytes 917536 | tf_op jit(solution)/shard_map/seconds_3/ppermute | solution.py:90
  90.5 1.3 collective-permute-start.23
  91.8 1.8 %contract.10 = bf16[2,256,896]{2,1,0:T(8,128)(2,1)S(1)} custom-call(s32[3]{0:T(128)S(1)} %get-tuple-element.517.at_ref, bf16[896,7168]{1,0:T(8,128)(2,1)S(1)} %pad_maximum_fusion.tokens_ref, bf16[512,448]{1,0:T(8,128)(2,1)S(1)} %get-tuple-element.440.right_a, bf16[512,448]{1,0:T(8,128)(2,1)S(1)} %get-tuple-element.441.right_b), custom_call_target="tpu_custom_call" | custom-call | flops 1000000000 | bytes 10000000 | tf_op jit(solution)/shard_map/contract/pallas_call | solution.py:149
  93.7 1.8 %contract.11 = f32[2,256,896]{2,1,0:T(8,128)S(1)} custom-call(s32[3]{0:T(128)S(1)} %get-tuple-element.520.at_ref, bf16[896,7168]{1,0:T(8,128)(2,1)S(1)} %pad_maximum_fusion.tokens_ref, bf16[512,448]{1,0:T(8,128)(2,1)S(1)} %get-tuple-element.440.right_a, bf16[512,448]{1,0:T(8,128)(2,1)S(1)} %get-tuple-element.441.right_b), custom_call_target="tpu_custom_call" | custom-call | flops 1000000000 | bytes 10000000 | tf_op jit(solution)/shard_map/contract/pallas_call | solution.py:149
  95.5 1.8 %contract.12 = f32[2,256,896]{2,1,0:T(8,128)S(1)} custom-call(s32[3]{0:T(128)S(1)} %get-tuple-element.519.at_ref, bf16[896,7168]{1,0:T(8,128)(2,1)S(1)} %pad_maximum_fusion.tokens_ref, bf16[512,448]{1,0:T(8,128)(2,1)S(1)} %get-tuple-element.440.right_a, bf16[512,448]{1,0:T(8,128)(2,1)S(1)} %get-tuple-element.441.right_b), custom_call_target="tpu_custom_call" | custom-call | flops 1000000000 | bytes 10000000 | tf_op jit(solution)/shard_map/contract/pallas_call | solution.py:149
  97.4 1.8 %contract.13 = f32[2,256,896]{2,1,0:T(8,128)S(1)} custom-call(s32[3]{0:T(128)S(1)} %get-tuple-element.517.at_ref, bf16[896,7168]{1,0:T(8,128)(2,1)S(1)} %pad_maximum_fusion.tokens_ref, bf16[512,448]{1,0:T(8,128)(2,1)S(1)} %get-tuple-element.440.right_a, bf16[512,448]{1,0:T(8,128)(2,1)S(1)} %get-tuple-element.441.right_b), custom_call_target="tpu_custom_call" | custom-call | flops 1000000000 | bytes 10000000 | tf_op jit(solution)/shard_map/contract/pallas_call | solution.py:149
  99.2 1.3 collective-permute-done.21
  100.7 2.5 %collective-permute-done.23 = bf16[256,896]{1,0:T(8,128)(2,1)S(1)} collective-permute-done((bf16[256,896]{1,0:T(8,128)(2,1)S(1)}, bf16[256,896]{1,0:T(8,128)(2,1)S(1)}, u32[]{:S(2)}, u32[]{:S(2)}) %collective-permute-start.23) | collective-permute-done | bytes 458784 | tf_op jit(solution)/shard_map/first_3/ppermute | solution.py:90
  103.4 1.8 %collective-permute-done.22 = bf16[2,256,896]{2,1,0:T(8,128)(2,1)S(1)} collective-permute-done((bf16[2,256,896]{2,1,0:T(8,128)(2,1)S(1)}, bf16[2,256,896]{2,1,0:T(8,128)(2,1)S(1)}, u32[]{:S(2)}, u32[]{:S(2)}) %collective-permute-start.22) | collective-permute-done | bytes 917536 | tf_op jit(solution)/shard_map/seconds_2/ppermute | solution.py:90
  105.3 1.3 collective-permute-start.26
  106.6 1.3 collective-permute-start.27
  108.3 4.9 %collective-permute-done.26 = bf16[256,896]{1,0:T(8,128)(2,1)S(1)} collective-permute-done((bf16[256,896]{1,0:T(8,128)(2,1)S(1)}, bf16[256,896]{1,0:T(8,128)(2,1)S(1)}, u32[]{:S(2)}, u32[]{:S(2)}) %collective-permute-start.26) | collective-permute-done | bytes 458784 | tf_op jit(solution)/shard_map/first_2/ppermute | solution.py:90
  113.2 5.8 %collective-permute-done.27 = bf16[256,896]{1,0:T(8,128)(2,1)S(1)} collective-permute-done((bf16[256,896]{1,0:T(8,128)(2,1)S(1)}, bf16[256,896]{1,0:T(8,128)(2,1)S(1)}, u32[]{:S(2)}, u32[]{:S(2)}) %collective-permute-start.27) | collective-permute-done | bytes 458784 | tf_op jit(solution)/shard_map/three_in/ppermute | solution.py:90
  119.1 1.3 collective-permute-start.29
  120.4 3.2 %collective-permute-start.28 = (bf16[256,896]{1,0:T(8,128)(2,1)S(1)}, bf16[256,896]{1,0:T(8,128)(2,1)S(1)}, u32[]{:S(2)}, u32[]{:S(2)}) collective-permute-start(bf16[256,896]{1,0:T(8,128)(2,1)S(1)} %fusion.69), channel_id=1, source_target_pairs={{4,8},{5,9},{6,10},{7,11},{8,4},{9,5},{10,6},{11,7},{20,24},{21,25... | collective-permute-start | bytes 1376264 | tf_op jit(solution)/shard_map/two/ppermute | solution.py:90
  123.7 5.7 %collective-permute-done.24 = bf16[2,256,896]{2,1,0:T(8,128)(2,1)S(1)} collective-permute-done((bf16[2,256,896]{2,1,0:T(8,128)(2,1)S(1)}, bf16[2,256,896]{2,1,0:T(8,128)(2,1)S(1)}, u32[]{:S(2)}, u32[]{:S(2)}) %collective-permute-start.24) | collective-permute-done | bytes 917536 | tf_op jit(solution)/shard_map/seconds_0/ppermute | solution.py:90
  129.5 1.1 collective-permute-start.30
  130.8 1.1 collective-permute-done.28
  132.0 3.2 %collective-permute-start.31 = (bf16[256,896]{1,0:T(8,128)(2,1)S(1)}, bf16[256,896]{1,0:T(8,128)(2,1)S(1)}, u32[]{:S(2)}, u32[]{:S(2)}) collective-permute-start(bf16[256,896]{1,0:T(8,128)(2,1)S(1)} %add_convert_fusion.2), channel_id=1, source_target_pairs={{4,8},{5,9},{6,10},{7,11},{8,4},{9,5},{10,6},{11,7},{20,24},{21,25... | collective-permute-start | bytes 1376264 | tf_op jit(solution)/shard_map/three/ppermute | solution.py:90
  135.4 1.9 %collective-permute-done.30.refs_1_ = bf16[256,896]{1,0:T(8,128)(2,1)S(1)} collective-permute-done((bf16[256,896]{1,0:T(8,128)(2,1)S(1)}, bf16[256,896]{1,0:T(8,128)(2,1)S(1)}, u32[]{:S(2)}, u32[]{:S(2)}) %collective-permute-start.30) | collective-permute-done | bytes 458784 | tf_op jit(solution)/shard_map/first_0/ppermute | solution.py:90
  137.2 3.4 %collective-permute-done.32.refs_3_ = bf16[256,896]{1,0:T(8,128)(2,1)S(1)} collective-permute-done((bf16[256,896]{1,0:T(8,128)(2,1)S(1)}, bf16[256,896]{1,0:T(8,128)(2,1)S(1)}, u32[]{:S(2)}, u32[]{:S(2)}) %collective-permute-start.32) | collective-permute-done | bytes 458784 | tf_op jit(solution)/shard_map/one/ppermute | solution.py:90
  140.6 1.9 %collective-permute-done.31.refs_2_ = bf16[256,896]{1,0:T(8,128)(2,1)S(1)} collective-permute-done((bf16[256,896]{1,0:T(8,128)(2,1)S(1)}, bf16[256,896]{1,0:T(8,128)(2,1)S(1)}, u32[]{:S(2)}, u32[]{:S(2)}) %collective-permute-start.31) | collective-permute-done | bytes 458784 | tf_op jit(solution)/shard_map/three/ppermute | solution.py:90
  142.6 1.3 by_rows.1
  143.9 4.4 %collective-permute-start.33 = (f32[448,256]{1,0:T(8,128)S(1)}, f32[448,256]{1,0:T(8,128)S(1)}, u32[]{:S(2)}, u32[]{:S(2)}) collective-permute-start(f32[448,256]{1,0:T(8,128)S(1)} %get-tuple-element.513), channel_id=1, source_target_pairs={{0,1},{1,0},{2,3},{3,2},{4,5},{5,4},{6,7},{7,6},{8,9},{9,8},{10,11... | collective-permute-start | bytes 1376264 | tf_op jit(solution)/shard_map/taken/ppermute | solution.py:90
  148.3 1.4 collective-permute-done.33.taken_ref
  149.7 1.8 %finish.1 = (f32[448,256]{1,0:T(8,128)}, f32[448,256]{1,0:T(8,128)}, f32[448,256]{1,0:T(8,128)}) custom-call(s32[2]{0:T(128)S(1)} %pad_add_fusion.at_ref, f32[448,256]{1,0:T(8,128)S(1)} %get-tuple-element.512.kept_ref, f32[448,256]{1,0:T(8,128)S(1)} %collective-permute-done.33.taken_ref, bf16[448,512]{1,0:T(8,128)(2,1)S(1)} %copy-done.4, ...), custom_call_target="tpu_custom_call" | custom-call | flops 1000000000 | bytes 10000000 | tf_op jit(solution)/shard_map/finish/pallas_call | solution.py:149
  (85 shorter events, 23.0 us)
Async XLA Ops:
  0.6 3.7 %collective-permute-start = (bf16[448,512]{1,0:T(8,128)(2,1)}, bf16[448,512]{1,0:T(8,128)(2,1)S(1)}, u32[]{:S(2)}, u32[]{:S(2)}) collective-permute-start(bf16[448,512]{1,0:T(8,128)(2,1)} %weight_ref.1), channel_id=1, source_target_pairs={{0,1},{1,0},{2,3},{3,2},{4,5},{5,4},{6,7},{7,6},{8,9},{9,8},{10,11... | collective-permute-start | bytes 1376264 | tf_op jit(solution)/shard_map/other_weight/ppermute | solution.py:90
  1.4 2.9 %collective-permute-start.1 = (bf16[448,512]{1,0:T(8,128)(2,1)}, bf16[448,512]{1,0:T(8,128)(2,1)S(1)}, u32[]{:S(2)}, u32[]{:S(2)}) collective-permute-start(bf16[448,512]{1,0:T(8,128)(2,1)} %probe_ref.3), channel_id=1, source_target_pairs={{0,1},{1,0},{2,3},{3,2},{4,5},{5,4},{6,7},{7,6},{8,9},{9,8},{10,11... | collective-permute-start | bytes 1376264 | tf_op jit(solution)/shard_map/other_probe/ppermute | solution.py:90
  1.5 1.0 copy-start.1
  2.5 1.0 copy-start.3
  4.3 4.8 %copy-start.2 = (bf16[448,512]{1,0:T(8,128)(2,1)S(1)}, bf16[448,512]{1,0:T(8,128)(2,1)}, u32[]{:S(2)}) copy-start(bf16[448,512]{1,0:T(8,128)(2,1)} %refs_0_) | copy-start | bytes 1376260
  4.9 19.0 %collective-permute-start.2 = (bf16[448,7168]{1,0:T(8,128)(2,1)}, bf16[448,7168]{1,0:T(8,128)(2,1)}, u32[]{:S(2)}, u32[]{:S(2)}) collective-permute-start(bf16[448,7168]{1,0:T(8,128)(2,1)} %param.7), channel_id=1, source_target_pairs={{0,1},{1,0},{2,3},{3,2},{4,5},{5,4},{6,7},{7,6},{8,9},{9,8},{10,11... | collective-permute-start | bytes 19267592 | tf_op jit(solution)/shard_map/other_acts/ppermute | solution.py:90
  5.4 14.0 %collective-permute-start.4 = (bf16[896,256]{1,0:T(8,128)(2,1)S(1)}, bf16[896,256]{1,0:T(8,128)(2,1)S(1)}, u32[]{:S(2)}, u32[]{:S(2)}) collective-permute-start(bf16[896,256]{1,0:T(8,128)(2,1)S(1)} %get-tuple-element.282), channel_id=1, source_target_pairs={{4,8},{5,9},{6,10},{7,11},{8,4},{9,5},{10,6},{11,7},{20,24},{21,25... | collective-permute-start | bytes 1376264 | tf_op jit(solution)/shard_map/near/ppermute | solution.py:90
  8.6 11.8 %collective-permute-start.3 = (bf16[896,256]{1,0:T(8,128)(2,1)S(1)}, bf16[896,256]{1,0:T(8,128)(2,1)S(1)}, u32[]{:S(2)}, u32[]{:S(2)}) collective-permute-start(bf16[896,256]{1,0:T(8,128)(2,1)S(1)} %get-tuple-element.282), channel_id=1, source_target_pairs={{0,4},{1,5},{2,6},{3,7},{4,0},{5,1},{6,2},{7,3},{8,12},{9,13},{10,... | collective-permute-start | bytes 1376264 | tf_op jit(solution)/shard_map/one/ppermute | solution.py:90
  8.7 15.2 %collective-permute-start.6 = (bf16[896,256]{1,0:T(8,128)(2,1)S(1)}, bf16[896,256]{1,0:T(8,128)(2,1)S(1)}, u32[]{:S(2)}, u32[]{:S(2)}) collective-permute-start(bf16[896,256]{1,0:T(8,128)(2,1)S(1)} %get-tuple-element.282), channel_id=1, source_target_pairs={{0,2},{1,3},{2,0},{3,1},{4,6},{5,7},{6,4},{7,5},{8,10},{9,11},{10,... | collective-permute-start | bytes 1376264 | tf_op jit(solution)/shard_map/across/ppermute | solution.py:90
  9.8 6.0 %collective-permute-start.5 = (bf16[448,256]{1,0:T(8,128)(2,1)S(1)}, bf16[448,256]{1,0:T(8,128)(2,1)S(1)}, u32[]{:S(2)}, u32[]{:S(2)}) collective-permute-start(bf16[448,256]{1,0:T(8,128)(2,1)S(1)} %get-tuple-element.264), channel_id=1, source_target_pairs={{0,1},{1,0},{2,3},{3,2},{4,5},{5,4},{6,7},{7,6},{8,9},{9,8},{10,11... | collective-permute-start | bytes 688136 | tf_op jit(solution)/shard_map/other_up/ppermute | solution.py:90
  20.5 13.8 %collective-permute-start.8 = (bf16[896,256]{1,0:T(8,128)(2,1)S(1)}, bf16[896,256]{1,0:T(8,128)(2,1)S(1)}, u32[]{:S(2)}, u32[]{:S(2)}) collective-permute-start(bf16[896,256]{1,0:T(8,128)(2,1)S(1)} %collective-permute-done.3), channel_id=1, source_target_pairs={{4,8},{5,9},{6,10},{7,11},{8,4},{9,5},{10,6},{11,7},{20,24},{21,25... | collective-permute-start | bytes 1376264 | tf_op jit(solution)/shard_map/two_in/ppermute | solution.py:90
  22.6 11.7 %collective-permute-start.7 = (bf16[896,256]{1,0:T(8,128)(2,1)S(1)}, bf16[896,256]{1,0:T(8,128)(2,1)S(1)}, u32[]{:S(2)}, u32[]{:S(2)}) collective-permute-start(bf16[896,256]{1,0:T(8,128)(2,1)S(1)} %collective-permute-done.4), channel_id=1, source_target_pairs={{4,0},{5,1},{6,2},{7,3},{8,12},{9,13},{10,14},{11,15},{20,16},{21,... | collective-permute-start | bytes 1376264 | tf_op jit(solution)/shard_map/two_out/ppermute | solution.py:90
  24.0 15.0 %collective-permute-start.10 = (bf16[896,256]{1,0:T(8,128)(2,1)S(1)}, bf16[896,256]{1,0:T(8,128)(2,1)S(1)}, u32[]{:S(2)}, u32[]{:S(2)}) collective-permute-start(bf16[896,256]{1,0:T(8,128)(2,1)S(1)} %broadcast_select_fusion.1), channel_id=1, source_target_pairs={{0,2},{1,17},{2,0},{3,19},{4,6},{5,21},{6,4},{7,23},{8,10},{9,25},... | collective-permute-start | bytes 1376264 | tf_op jit(solution)/shard_map/corner/ppermute | solution.py:90
  25.3 13.7 %collective-permute-start.11 = (bf16[896,256]{1,0:T(8,128)(2,1)S(1)}, bf16[896,256]{1,0:T(8,128)(2,1)S(1)}, u32[]{:S(2)}, u32[]{:S(2)}) collective-permute-start(bf16[896,256]{1,0:T(8,128)(2,1)S(1)} %collective-permute-done.3), channel_id=1, source_target_pairs={{0,2},{1,17},{2,0},{3,19},{4,6},{5,21},{6,4},{7,23},{8,10},{9,25},... | collective-permute-start | bytes 1376264 | tf_op jit(solution)/shard_map/one_first/ppermute | solution.py:90
  34.4 16.2 %collective-permute-start.12 = (bf16[896,256]{1,0:T(8,128)(2,1)S(1)}, bf16[896,256]{1,0:T(8,128)(2,1)S(1)}, u32[]{:S(2)}, u32[]{:S(2)}) collective-permute-start(bf16[896,256]{1,0:T(8,128)(2,1)S(1)} %add.197), channel_id=1, source_target_pairs={{0,2},{1,17},{2,0},{3,19},{4,6},{5,21},{6,4},{7,23},{8,10},{9,25},... | collective-permute-start | bytes 1376264 | tf_op jit(solution)/shard_map/two_first/ppermute | solution.py:90
  35.7 10.9 %collective-permute-start.9 = (bf16[896,256]{1,0:T(8,128)(2,1)S(1)}, bf16[896,256]{1,0:T(8,128)(2,1)S(1)}, u32[]{:S(2)}, u32[]{:S(2)}) collective-permute-start(bf16[896,256]{1,0:T(8,128)(2,1)S(1)} %add.197), channel_id=1, source_target_pairs={{4,0},{5,1},{6,2},{7,3},{8,12},{9,13},{10,14},{11,15},{20,16},{21,... | collective-permute-start | bytes 1376264 | tf_op jit(solution)/shard_map/three_out/ppermute | solution.py:90
  39.7 9.8 %collective-permute-start.13 = (bf16[896,256]{1,0:T(8,128)(2,1)S(1)}, bf16[896,256]{1,0:T(8,128)(2,1)S(1)}, u32[]{:S(2)}, u32[]{:S(2)}) collective-permute-start(bf16[896,256]{1,0:T(8,128)(2,1)S(1)} %collective-permute-done.11), channel_id=1, source_target_pairs={{0,16},{1,3},{2,18},{3,1},{4,20},{5,7},{6,22},{7,5},{8,24},{9,11},... | collective-permute-start | bytes 1376264 | tf_op jit(solution)/shard_map/one_both/ppermute | solution.py:90
  40.0 16.0 %collective-permute-start.15 = (bf16[896,256]{1,0:T(8,128)(2,1)S(1)}, bf16[896,256]{1,0:T(8,128)(2,1)S(1)}, u32[]{:S(2)}, u32[]{:S(2)}) collective-permute-start(bf16[896,256]{1,0:T(8,128)(2,1)S(1)} %add.197), channel_id=1, source_target_pairs={{0,16},{1,3},{2,18},{3,1},{4,20},{5,7},{6,22},{7,5},{8,24},{9,11},... | collective-permute-start | bytes 1376264 | tf_op jit(solution)/shard_map/two_second/ppermute | solution.py:90
  46.7 23.7 %collective-permute-start.18 = (bf16[896,256]{1,0:T(8,128)(2,1)S(1)}, bf16[896,256]{1,0:T(8,128)(2,1)S(1)}, u32[]{:S(2)}, u32[]{:S(2)}) collective-permute-start(bf16[896,256]{1,0:T(8,128)(2,1)S(1)} %add.207), channel_id=1, source_target_pairs={{0,16},{1,3},{2,18},{3,1},{4,20},{5,7},{6,22},{7,5},{8,24},{9,11},... | collective-permute-start | bytes 1376264 | tf_op jit(solution)/shard_map/three_second/ppermute | solution.py:90
  46.8 12.7 %collective-permute-start.14 = (bf16[896,256]{1,0:T(8,128)(2,1)S(1)}, bf16[896,256]{1,0:T(8,128)(2,1)S(1)}, u32[]{:S(2)}, u32[]{:S(2)}) collective-permute-start(bf16[896,256]{1,0:T(8,128)(2,1)S(1)} %add.207), channel_id=1, source_target_pairs={{0,2},{1,17},{2,0},{3,19},{4,6},{5,21},{6,4},{7,23},{8,10},{9,25},... | collective-permute-start | bytes 1376264 | tf_op jit(solution)/shard_map/three_first/ppermute | solution.py:90
  49.5 20.3 %collective-permute-start.19 = (bf16[896,256]{1,0:T(8,128)(2,1)S(1)}, bf16[896,256]{1,0:T(8,128)(2,1)S(1)}, u32[]{:S(2)}, u32[]{:S(2)}) collective-permute-start(bf16[896,256]{1,0:T(8,128)(2,1)S(1)} %broadcast_select_fusion), channel_id=1, source_target_pairs={{0,4},{1,5},{2,6},{3,7},{4,0},{5,1},{6,2},{7,3},{8,12},{9,13},{10,... | collective-permute-start | bytes 1376264 | tf_op jit(solution)/shard_map/one_second/ppermute | solution.py:90
  50.7 18.4 %collective-permute-start.17 = (bf16[896,256]{1,0:T(8,128)(2,1)S(1)}, bf16[896,256]{1,0:T(8,128)(2,1)S(1)}, u32[]{:S(2)}, u32[]{:S(2)}) collective-permute-start(bf16[896,256]{1,0:T(8,128)(2,1)S(1)} %collective-permute-done.12), channel_id=1, source_target_pairs={{0,16},{1,3},{2,18},{3,1},{4,20},{5,7},{6,22},{7,5},{8,24},{9,11},... | collective-permute-start | bytes 1376264 | tf_op jit(solution)/shard_map/two_both/ppermute | solution.py:90
  59.5 14.5 %collective-permute-start.16 = (bf16[896,256]{1,0:T(8,128)(2,1)S(1)}, bf16[896,256]{1,0:T(8,128)(2,1)S(1)}, u32[]{:S(2)}, u32[]{:S(2)}) collective-permute-start(bf16[896,256]{1,0:T(8,128)(2,1)S(1)} %collective-permute-done.14), channel_id=1, source_target_pairs={{0,16},{1,3},{2,18},{3,1},{4,20},{5,7},{6,22},{7,5},{8,24},{9,11},... | collective-permute-start | bytes 1376264 | tf_op jit(solution)/shard_map/three_both/ppermute | solution.py:90
  71.1 3.6 %copy-start = (f32[128]{0:T(128)S(1)}, f32[128]{0:T(128)}, u32[]{:S(2)}) copy-start(f32[128]{0:T(128)} %param.11) | copy-start | bytes 1540
  77.9 12.6 %collective-permute-start.20 = (bf16[2,256,896]{2,1,0:T(8,128)(2,1)S(1)}, bf16[2,256,896]{2,1,0:T(8,128)(2,1)S(1)}, u32[]{:S(2)}, u32[]{:S(2)}) collective-permute-start(bf16[2,256,896]{2,1,0:T(8,128)(2,1)S(1)} %get-tuple-element.418), channel_id=1, source_target_pairs={{0,16},{1,3},{2,18},{3,1},{4,20},{5,7},{6,22},{7,5},{8,24},{9,11},... | collective-permute-start | bytes 2752520 | tf_op jit(solution)/shard_map/seconds_3/ppermute | solution.py:90
  80.2 20.3 %collective-permute-start.21 = (bf16[2,256,896]{2,1,0:T(8,128)(2,1)S(1)}, bf16[2,256,896]{2,1,0:T(8,128)(2,1)S(1)}, u32[]{:S(2)}, u32[]{:S(2)}) collective-permute-start(bf16[2,256,896]{2,1,0:T(8,128)(2,1)S(1)} %contract.7), channel_id=1, source_target_pairs={{0,4},{1,5},{2,6},{3,7},{4,0},{5,1},{6,2},{7,3},{8,12},{9,13},{10,... | collective-permute-start | bytes 2752520 | tf_op jit(solution)/shard_map/raw_1/ppermute | solution.py:90
  82.4 22.9 %collective-permute-start.22 = (bf16[2,256,896]{2,1,0:T(8,128)(2,1)S(1)}, bf16[2,256,896]{2,1,0:T(8,128)(2,1)S(1)}, u32[]{:S(2)}, u32[]{:S(2)}) collective-permute-start(bf16[2,256,896]{2,1,0:T(8,128)(2,1)S(1)} %contract.8), channel_id=1, source_target_pairs={{0,16},{1,3},{2,18},{3,1},{4,20},{5,7},{6,22},{7,5},{8,24},{9,11},... | collective-permute-start | bytes 2752520 | tf_op jit(solution)/shard_map/seconds_2/ppermute | solution.py:90
  90.5 12.7 %collective-permute-start.23 = (bf16[256,896]{1,0:T(8,128)(2,1)S(1)}, bf16[256,896]{1,0:T(8,128)(2,1)S(1)}, u32[]{:S(2)}, u32[]{:S(2)}) collective-permute-start(bf16[256,896]{1,0:T(8,128)(2,1)S(1)} %fusion.71), channel_id=1, source_target_pairs={{0,2},{1,17},{2,0},{3,19},{4,6},{5,21},{6,4},{7,23},{8,10},{9,25},... | collective-permute-start | bytes 1376264 | tf_op jit(solution)/shard_map/first_3/ppermute | solution.py:90
  105.3 7.9 %collective-permute-start.26 = (bf16[256,896]{1,0:T(8,128)(2,1)S(1)}, bf16[256,896]{1,0:T(8,128)(2,1)S(1)}, u32[]{:S(2)}, u32[]{:S(2)}) collective-permute-start(bf16[256,896]{1,0:T(8,128)(2,1)S(1)} %fusion.72), channel_id=1, source_target_pairs={{0,2},{1,17},{2,0},{3,19},{4,6},{5,21},{6,4},{7,23},{8,10},{9,25},... | collective-permute-start | bytes 1376264 | tf_op jit(solution)/shard_map/first_2/ppermute | solution.py:90
  106.6 12.3 %collective-permute-start.27 = (bf16[256,896]{1,0:T(8,128)(2,1)S(1)}, bf16[256,896]{1,0:T(8,128)(2,1)S(1)}, u32[]{:S(2)}, u32[]{:S(2)}) collective-permute-start(bf16[256,896]{1,0:T(8,128)(2,1)S(1)} %fusion.70), channel_id=1, source_target_pairs={{0,4},{1,5},{2,6},{3,7},{12,8},{13,9},{14,10},{15,11},{16,20},{17,... | collective-permute-start | bytes 1376264 | tf_op jit(solution)/shard_map/three_in/ppermute | solution.py:90
  107.9 21.5 %collective-permute-start.24 = (bf16[2,256,896]{2,1,0:T(8,128)(2,1)S(1)}, bf16[2,256,896]{2,1,0:T(8,128)(2,1)S(1)}, u32[]{:S(2)}, u32[]{:S(2)}) collective-permute-start(bf16[2,256,896]{2,1,0:T(8,128)(2,1)S(1)} %add_convert_fusion), channel_id=1, source_target_pairs={{0,16},{1,3},{2,18},{3,1},{4,20},{5,7},{6,22},{7,5},{8,24},{9,11},... | collective-permute-start | bytes 2752520 | tf_op jit(solution)/shard_map/seconds_0/ppermute | solution.py:90
  108.0 15.6 %collective-permute-start.25 = (bf16[256,896]{1,0:T(8,128)(2,1)S(1)}, bf16[256,896]{1,0:T(8,128)(2,1)S(1)}, u32[]{:S(2)}, u32[]{:S(2)}) collective-permute-start(bf16[256,896]{1,0:T(8,128)(2,1)S(1)} %fusion.74), channel_id=1, source_target_pairs={{0,2},{1,17},{2,0},{3,19},{4,6},{5,21},{6,4},{7,23},{8,10},{9,25},... | collective-permute-start | bytes 1376264 | tf_op jit(solution)/shard_map/first_1/ppermute | solution.py:90
  119.1 11.5 %collective-permute-start.29 = (bf16[256,896]{1,0:T(8,128)(2,1)S(1)}, bf16[256,896]{1,0:T(8,128)(2,1)S(1)}, u32[]{:S(2)}, u32[]{:S(2)}) collective-permute-start(bf16[256,896]{1,0:T(8,128)(2,1)S(1)} %fusion.69), channel_id=1, source_target_pairs={{0,4},{1,5},{2,6},{3,7},{12,8},{13,9},{14,10},{15,11},{16,20},{17,... | collective-permute-start | bytes 1376264 | tf_op jit(solution)/shard_map/two_in/ppermute | solution.py:90
  120.4 11.4 %collective-permute-start.28 = (bf16[256,896]{1,0:T(8,128)(2,1)S(1)}, bf16[256,896]{1,0:T(8,128)(2,1)S(1)}, u32[]{:S(2)}, u32[]{:S(2)}) collective-permute-start(bf16[256,896]{1,0:T(8,128)(2,1)S(1)} %fusion.69), channel_id=1, source_target_pairs={{4,8},{5,9},{6,10},{7,11},{8,4},{9,5},{10,6},{11,7},{20,24},{21,25... | collective-permute-start | bytes 1376264 | tf_op jit(solution)/shard_map/two/ppermute | solution.py:90
  129.5 7.7 %collective-permute-start.30 = (bf16[256,896]{1,0:T(8,128)(2,1)S(1)}, bf16[256,896]{1,0:T(8,128)(2,1)S(1)}, u32[]{:S(2)}, u32[]{:S(2)}) collective-permute-start(bf16[256,896]{1,0:T(8,128)(2,1)S(1)} %fusion.73), channel_id=1, source_target_pairs={{0,2},{1,17},{2,0},{3,19},{4,6},{5,21},{6,4},{7,23},{8,10},{9,25},... | collective-permute-start | bytes 1376264 | tf_op jit(solution)/shard_map/first_0/ppermute | solution.py:90
  132.0 8.7 %collective-permute-start.32 = (bf16[256,896]{1,0:T(8,128)(2,1)S(1)}, bf16[256,896]{1,0:T(8,128)(2,1)S(1)}, u32[]{:S(2)}, u32[]{:S(2)}) collective-permute-start(bf16[256,896]{1,0:T(8,128)(2,1)S(1)} %add_convert_fusion.1), channel_id=1, source_target_pairs={{0,4},{1,5},{2,6},{3,7},{4,0},{5,1},{6,2},{7,3},{8,12},{9,13},{10,... | collective-permute-start | bytes 1376264 | tf_op jit(solution)/shard_map/one/ppermute | solution.py:90
  132.0 10.5 %collective-permute-start.31 = (bf16[256,896]{1,0:T(8,128)(2,1)S(1)}, bf16[256,896]{1,0:T(8,128)(2,1)S(1)}, u32[]{:S(2)}, u32[]{:S(2)}) collective-permute-start(bf16[256,896]{1,0:T(8,128)(2,1)S(1)} %add_convert_fusion.2), channel_id=1, source_target_pairs={{4,8},{5,9},{6,10},{7,11},{8,4},{9,5},{10,6},{11,7},{20,24},{21,25... | collective-permute-start | bytes 1376264 | tf_op jit(solution)/shard_map/three/ppermute | solution.py:90
  142.6 7.2 %copy-start.4 = (bf16[448,512]{1,0:T(8,128)(2,1)S(1)}, bf16[448,512]{1,0:T(8,128)(2,1)}, u32[]{:S(2)}) copy-start(bf16[448,512]{1,0:T(8,128)(2,1)} %probe_ref.3) | copy-start | bytes 1376260
  142.6 7.2 %copy-start.5 = (f32[448,256]{1,0:T(8,128)S(1)}, f32[448,256]{1,0:T(8,128)}, u32[]{:S(2)}) copy-start(f32[448,256]{1,0:T(8,128)} %momentum_ref) | copy-start | bytes 1376260
  142.6 7.2 %copy-start.6 = (f32[448,256]{1,0:T(8,128)S(1)}, f32[448,256]{1,0:T(8,128)}, u32[]{:S(2)}) copy-start(f32[448,256]{1,0:T(8,128)} %curvature_ref.1) | copy-start | bytes 1376260
  143.9 5.8 %collective-permute-start.33 = (f32[448,256]{1,0:T(8,128)S(1)}, f32[448,256]{1,0:T(8,128)S(1)}, u32[]{:S(2)}, u32[]{:S(2)}) collective-permute-start(f32[448,256]{1,0:T(8,128)S(1)} %get-tuple-element.513), channel_id=1, source_target_pairs={{0,1},{1,0},{2,3},{3,2},{4,5},{5,4},{6,7},{7,6},{8,9},{9,8},{10,11... | collective-permute-start | bytes 1376264 | tf_op jit(solution)/shard_map/taken/ppermute | solution.py:90

commit v5 on v4

--- a/solution.py
+++ b/solution.py
@@ -104,7 +104,8 @@
 
     def run(self, operation, *values):
         *values, self.token = lax.optimization_barrier((*values, self.token))
-        return self.wait(operation(*values))
+        found = operation(*values)
+        return self.wait(*found) if isinstance(found, (list, tuple)) else self.wait(found)
 
 
 def to_core(y, z, x, c):
@@ -167,14 +168,12 @@
     return pl.ds(0, half), pl.ds(half, half)
 
 
-def partials(block, x, core, rights, tokens_ref, leave, out_ref):
-    width = rights[0].shape[0] // 2
+def partials(block, x, core, heres, theres, tokens_ref, leave, out_ref):
     depth = out_ref.shape[2]
-    here, there = pl.ds(0, width), pl.ds(width, width)
     by_core = core == 0 if leave else core != 0
     place_fixed, place_by_core = 1 - x if leave else x, jnp.where(by_core, x, 1 - x)
-    fixed = [right[there if leave else here, :] for right in rights]
-    chosen = [jnp.where(by_core, right[there, :], right[here, :]) for right in rights]
+    fixed = [ref[...] for ref in (theres if leave else heres)]
+    chosen = [jnp.where(by_core, there[...], here[...]) for here, there in zip(heres, theres)]
     order = (0, 1) if leave else (1, 0)
     for i, place, lefts in ((order[0], place_fixed, fixed), (order[1], place_by_core, chosen)):
         for begin in range(0, depth, 256):
@@ -186,60 +185,81 @@
             out_ref[i, :, pl.ds(begin, size)] = total.astype(out_ref.dtype)
 
 
-def contract(scalars, depth, leave, tokens, right_a, right_b):
-    def kernel(at_ref, tokens_ref, right_a, right_b, out_ref):
+def contract(scalars, depth, leave, tokens, *rights):
+    def kernel(at_ref, tokens_ref, here_a, here_b, there_a, there_b, out_ref):
         place = at_ref[0], at_ref[1], at_ref[2]
-        partials(*place, (right_a, right_b), tokens_ref, leave, out_ref)
+        partials(*place, (here_a, here_b), (there_a, there_b), tokens_ref, leave, out_ref)
 
     dtype = jnp.bfloat16 if leave else jnp.float32
-    out = jax.ShapeDtypeStruct((2, right_a.shape[0] // 2, depth), dtype)
-    return call(kernel, out, scalars, tokens, right_a, right_b, name="contract", cost=10**7)
-
-
-def head_gradients(scalars, depth, tokens, sums, own_up, other_up, norm_gain):
-    half = tokens.shape[0] // 2
-    width = sums[0].shape[1]
+    out = jax.ShapeDtypeStruct((2, rights[0].shape[0], depth), dtype)
+    return call(kernel, out, scalars, tokens, *rights, name="contract")
+
+
+def turned_gradients(product_of, up_refs, column, gain, out_refs):
+    head = gain.shape[1]
+    for part, (up_ref, out_ref) in enumerate(zip(up_refs, out_refs)):
+        half = up_ref.shape[0]
+        for begin in range(0, half, 128):
+            size = min(128, half - begin)
+            within = pl.ds(begin, size)
+            product = product_of(part, begin, size)
+            weighted = up_ref[within, column].astype(jnp.float32) * gain
+            pair = head_terms(product[:, :head], product[:, head:], weighted)
+            for i, value in enumerate(pair):
+                out_ref[pl.ds(i * head, head), within] = value.T.astype(jnp.bfloat16)
+
+
+def side_column(at_ref, side, head):
+    return pl.ds(pl.multiple_of((2 * side + at_ref[2]) * head, 128), head)
+
+
+def gradients_here(scalars, own, first, second, upstream, other_up, norm_gain):
+    half, width = own.shape[0] // 2, own.shape[1]
     head = norm_gain.shape[0]
 
+    def kernel(at_ref, own_ref, first_ref, second_ref, up_a, up_b, gain_ref, *out_refs):
+        own_first = at_ref[2] == 0
+
+        def product_of(part, begin, size):
+            at = pl.ds(part * half + begin, size)
+            return own_ref[at, :] + jnp.where(own_first, first_ref[at, :], second_ref[at, :])
+
+        column = side_column(at_ref, at_ref[3], head)
+        turned_gradients(product_of, (up_a, up_b), column, gain_ref[...], out_refs)
+
+    out = jax.ShapeDtypeStruct((width, half), jnp.bfloat16)
+    operands = (own, first, second, upstream, other_up, norm_gain.reshape(1, head))
+    return call(kernel, [out, out], scalars, *operands, name="gradients_here")
+
+
+def gradients_there(scalars, tokens, heres, both, first, second, last, upstream, other_up, norm_gain):
+    half, width = both.shape[0] // 2, both.shape[1]
+    depth = last.shape[0]
+    head = norm_gain.shape[0]
+
     def kernel(
-        at_ref, tokens_ref, own_ref, both_ref, first_ref, second_ref, up_a, up_b, gain_ref,
-        right_a, right_b, leaving_ref,
+        at_ref, tokens_ref, here_a, here_b, both_ref, first_ref, second_ref, last_ref, up_a, up_b, gain_ref,
+        there_a, there_b, leaving_ref,
     ):
-        gain = gain_ref[...]
-        own_first = at_ref[2] == 0
-        for part, (up, right) in enumerate(((up_a, right_a), (up_b, right_b))):
-            for begin in range(0, half, 128):
-                size = min(128, half - begin)
-                within = pl.ds(begin, size)
-                at = pl.ds(part * half + begin, size)
-                weighted = up[within, :].astype(jnp.float32)
-                first, second = first_ref[at, :], second_ref[at, :]
-                here = own_ref[at, :] + jnp.where(own_first, first, second)
-                there = both_ref[at, :] + jnp.where(own_first, second, first)
-                for side, product in enumerate((here, there)):
-                    pair = head_terms(
-                        product[:, :head],
-                        product[:, head:],
-                        weighted[:, side * head : (side + 1) * head] * gain,
-                    )
-                    for i, value in enumerate(pair):
-                        features = pl.ds((2 * side + i) * head, head)
-                        right[features, within] = value.T.astype(jnp.bfloat16)
-        place = at_ref[0], at_ref[1], at_ref[2]
-        partials(*place, (right_a, right_b), tokens_ref, True, leaving_ref)
-
-    right = jax.ShapeDtypeStruct((2 * width, half), jnp.bfloat16)
-    return call(
-        kernel,
-        [right, right, jax.ShapeDtypeStruct((2, width, depth), jnp.bfloat16)],
-        scalars,
-        tokens,
-        *sums,
-        own_up,
-        other_up,
-        norm_gain.reshape(1, head),
-        name="head_gradients",
-    )
+        block, x, core = at_ref[0], at_ref[1], at_ref[2]
+        far = pl.ds(pl.multiple_of((2 * block + 1 - x) * depth, 128), depth)
+        products = [dot(tokens_ref[rows, far], last_ref[...]) for rows in halves(tokens)]
+
+        def product_of(part, begin, size):
+            at = pl.ds(part * half + begin, size)
+            by_core = jnp.where(core == 0, second_ref[at, :], first_ref[at, :])
+            return both_ref[at, :] + by_core + products[part][begin : begin + size]
+
+        column = side_column(at_ref, 1 - at_ref[3], head)
+        turned_gradients(product_of, (up_a, up_b), column, gain_ref[...], (there_a, there_b))
+        partials(
+            block, x, core, (here_a, here_b), (there_a, there_b), tokens_ref, True, leaving_ref
+        )
+
+    out = jax.ShapeDtypeStruct((width, half), jnp.bfloat16)
+    leaving = jax.ShapeDtypeStruct((2, width, depth), jnp.bfloat16)
+    operands = (*heres, both, first, second, last, upstream, other_up, norm_gain.reshape(1, head))
+    return call(kernel, [out, out, leaving], scalars, tokens, *operands, name="gradients_there")
 
 
 def by_rows(scalars, *terms):
@@ -314,22 +334,6 @@
     return call(kernel, [out, out], scalars, weight, probe, *units, name="unit_rows", aliases=aliases)
 
 
-def columns_by_core(scalars, head, *arrays):
-    rows = arrays[0].shape[0]
-
-    def kernel(at_ref, *refs):
-        *array_refs, leaving_ref, staying_ref = refs
-        y, c = at_ref[0], at_ref[1]
-        for out_ref, core in ((leaving_ref, 1 - c), (staying_ref, c)):
-            for i, side in enumerate((y, 1 - y)):
-                for j, ref in enumerate(array_refs):
-                    column = pl.ds(pl.multiple_of((2 * side + core) * head, 128), head)
-                    out_ref[:, pl.ds((i * len(array_refs) + j) * head, head)] = ref[:, column]
-
-    out = jax.ShapeDtypeStruct((rows, 2 * len(arrays) * head), arrays[0].dtype)
-    return call(kernel, [out, out], scalars, *arrays, name="columns_by_core")
-
-
 def by_links(acts, upstream, k_weight, probe, norm_gain, momentum, curvature):
     head = norm_gain.shape[0]
     rows = k_weight.shape[0]
@@ -340,8 +344,7 @@
     other_weight, other_probe = send(k_weight, to_core, "other_weight"), send(probe, to_core, "other_probe")
     own_rows = unit_rows((y, c, c), head, k_weight, probe)
     mine, beside = unit_rows((y, c, 1 - c), head, other_weight, other_probe, own_rows)
-    up_leaving, own_up = columns_by_core((y, c), head, after(upstream, mine))
-    other_up = send(up_leaving, to_core, "other_up")
+    other_up = send(upstream, to_core, "other_up")
     order = Order(momentum)
     other_acts = send(after(acts, mine), to_core, "other_acts")
     one = send(mine, Z_ONE, "one")
@@ -374,11 +377,11 @@
     two_out, two_in = order.wait(two_out, two_in)
     two = order.run(jnp.add, two_out, two_in)
     three_out = send(two, Z_OUT, "three_out")
-    two_first = send(two, to_first, "two_first")
     own_sum = add_product(own_sum, 1, 0, one)
     one_first = order.wait(one_first)
     one_both = send(one_first, to_second, "one_both")
     corner, two = order.wait(corner, two)
+    two_first = send(two, to_first, "two_first")
     two_second = send(two, to_second, "two_second")
     both_sum = add_product(both_sum, 0, 1, corner)
     first_sum = add_product(None, 1, 1 - c, one_first)
@@ -388,9 +391,9 @@
     flip = order.run(lambda a, b: jnp.where(own_first, a, b), beside, across)
     one_second = send(flip, Z_ONE, "one_second")
     three_second = send(three, to_second, "three_second")
-    both_sum = add_product(both_sum, 1, 1, one_both)
     two_first = order.wait(two_first)
     two_both = send(two_first, to_second, "two_both")
+    both_sum = add_product(both_sum, 1, 1, one_both)
     first_sum = add_product(first_sum, 2, 1 - c, two_first)
     own_sum = add_product(own_sum, 3, 0, three)
     second_sum = add_product(None, 2, c, two_second)
@@ -400,18 +403,20 @@
     both_sum = add_product(both_sum, 2, 1, two_both)
     second_sum = add_product(second_sum, 1, c, one_second)
     second_sum = add_product(second_sum, 3, c, three_second)
-    both_sum = add_product(both_sum, 3, 1, three_both)
-
-    sums = (own_sum, both_sum, first_sum, second_sum)
-    right_a, right_b, leaving_3 = head_gradients(
-        (z ^ 3, x, c), 2 * rows, tokens, sums, own_up, other_up, norm_gain
+    place = (z ^ 3, x, c, y)
+    ups = (upstream, other_up, norm_gain)
+    heres = order.run(
+        lambda *sums: gradients_here(place, *sums, *ups), own_sum, first_sum, second_sum
+    )
+    *theres, leaving_3 = gradients_there(
+        place, tokens, heres, both_sum, first_sum, second_sum, order.wait(three_both), *ups
     )
 
     def partial(slot, leave):
         def product(*operands):
             return contract((z ^ slot, x, c), 2 * rows, leave, *operands)
 
-        return order.run(product, tokens, right_a, right_b)
+        return order.run(product, tokens, *heres, *theres)
 
     def total_of(*terms):
         return sum((t.astype(jnp.float32) for t in terms[1:]), terms[0].astype(jnp.float32))

time: 152 us -> 152 us (level)
    dot_general x16 -> x15, matrix products: 10.4 us -> 9.72 us  [product(): jnp.dot(block_of(held, slot, flip_x), unit, preferred_element_type=jnp.fl...]
  transfers between devices with their start and end apart: 34 -> 34, of which waited for: 21 -> 20; matrix products, arithmetic and copies ran while one was open for 12% -> 12% of each run, Pallas kernels for 9% -> 10%
where the time goes in v5:
time: 152 us; the launch traced here: 151 us
  waiting for transfers between devices  68.7 us (45%)
  starting transfers between devices  38.5 us (25%)
  Pallas kernels  22.1 us (15%)
  matrix products  9.72 us (6%)
  other arithmetic  8.99 us (6%)
  local copies, waits for them, and re-layouts  2.11 us (1%)
    ppermute x34, waiting for transfers between devices, send(): return lax.ppermute(value, AXES, pairs_of(move))  68.7 us
    ppermute x34, starting transfers between devices, send(): return lax.ppermute(value, AXES, pairs_of(move))  38.5 us
    pallas_call x13, Pallas kernels, call(): pl.pallas_call(kernel, out_shape=outs, in_specs=[SMEM] + [VMEM] * len(ope...  22.1 us
    dot_general x15, matrix products, product(): jnp.dot(block_of(held, slot, flip_x), unit, preferred_element_type=jnp.fl...  9.72 us
    concatenate x1, other arithmetic, by_links(): jnp.concatenate([a, b], axis=0)  6.77 us
  transfers between devices with their start and end apart: 34, of which 20 were waited for; matrix products, arithmetic and copies ran while one was open for 12% of the time, Pallas kernels for 10%

profile of v5, /device:TPU:11, one launch (start us, length us, event | category | flops | bytes accessed | tf_op | source)
XLA Modules:
  0.0 151.2 jit_solution(9886312629979791438)
XLA Ops:
  1.5 1.0 copy-done.2
  5.7 3.2 %collective-permute-start.4 = (bf16[896,256]{1,0:T(8,128)(2,1)S(1)}, bf16[896,256]{1,0:T(8,128)(2,1)S(1)}, u32[]{:S(2)}, u32[]{:S(2)}) collective-permute-start(bf16[896,256]{1,0:T(8,128)(2,1)S(1)} %get-tuple-element.296), channel_id=1, source_target_pairs={{4,8},{5,9},{6,10},{7,11},{8,4},{9,5},{10,6},{11,7},{20,24},{21,25... | collective-permute-start | bytes 1376264 | tf_op jit(solution)/shard_map/near/ppermute | solution.py:90
  9.4 2.4 %collective-permute-done.5.up_b = bf16[448,512]{1,0:T(8,128)(2,1)S(1)} collective-permute-done((bf16[448,512]{1,0:T(8,128)(2,1)S(1)}, bf16[448,512]{1,0:T(8,128)(2,1)S(1)}, u32[]{:S(2)}, u32[]{:S(2)}) %collective-permute-start.5) | collective-permute-done | bytes 458784 | tf_op jit(solution)/shard_map/other_up/ppermute | solution.py:90
  11.8 7.7 %collective-permute-done.4 = bf16[896,256]{1,0:T(8,128)(2,1)S(1)} collective-permute-done((bf16[896,256]{1,0:T(8,128)(2,1)S(1)}, bf16[896,256]{1,0:T(8,128)(2,1)S(1)}, u32[]{:S(2)}, u32[]{:S(2)}) %collective-permute-start.4) | collective-permute-done | bytes 458784 | tf_op jit(solution)/shard_map/near/ppermute | solution.py:90
  19.5 1.1 collective-permute-done.3
  20.6 2.1 %collective-permute-start.8 = (bf16[896,256]{1,0:T(8,128)(2,1)S(1)}, bf16[896,256]{1,0:T(8,128)(2,1)S(1)}, u32[]{:S(2)}, u32[]{:S(2)}) collective-permute-start(bf16[896,256]{1,0:T(8,128)(2,1)S(1)} %collective-permute-done.3), channel_id=1, source_target_pairs={{4,8},{5,9},{6,10},{7,11},{8,4},{9,5},{10,6},{11,7},{20,24},{21,25... | collective-permute-start | bytes 1376264 | tf_op jit(solution)/shard_map/two_in/ppermute | solution.py:90
  22.8 1.3 collective-permute-start.7
  24.2 1.3 collective-permute-start.10
  25.7 6.8 %pad_maximum_fusion.tokens_ref = bf16[896,7168]{1,0:T(8,128)(2,1)S(1)} fusion(bf16[448,7168]{1,0:T(8,128)(2,1)} %collective-permute-done.2, bf16[448,7168]{1,0:T(8,128)(2,1)} %param.7), kind=kLoop, calls=%fused_computation | loop fusion | flops 25690112 | bytes 25690112 | tf_op jit(solution)/shard_map/concatenate | solution.py:361
  35.3 2.4 %collective-permute-start.9 = (bf16[896,256]{1,0:T(8,128)(2,1)S(1)}, bf16[896,256]{1,0:T(8,128)(2,1)S(1)}, u32[]{:S(2)}, u32[]{:S(2)}) collective-permute-start(bf16[896,256]{1,0:T(8,128)(2,1)S(1)} %add.188), channel_id=1, source_target_pairs={{4,0},{5,1},{6,2},{7,3},{8,12},{9,13},{10,14},{11,15},{20,16},{21,... | collective-permute-start | bytes 1376264 | tf_op jit(solution)/shard_map/three_out/ppermute | solution.py:90
  38.0 1.2 collective-permute-start.12
  39.9 1.2 collective-permute-start.13
  42.5 2.6 %collective-permute-done.9 = bf16[896,256]{1,0:T(8,128)(2,1)S(1)} collective-permute-done((bf16[896,256]{1,0:T(8,128)(2,1)S(1)}, bf16[896,256]{1,0:T(8,128)(2,1)S(1)}, u32[]{:S(2)}, u32[]{:S(2)}) %collective-permute-start.9) | collective-permute-done | bytes 458784 | tf_op jit(solution)/shard_map/three_out/ppermute | solution.py:90
  45.6 1.2 collective-permute-start.14
  47.8 1.3 collective-permute-start.17
  49.1 6.5 %collective-permute-done.13 = bf16[896,256]{1,0:T(8,128)(2,1)S(1)} collective-permute-done((bf16[896,256]{1,0:T(8,128)(2,1)S(1)}, bf16[896,256]{1,0:T(8,128)(2,1)S(1)}, u32[]{:S(2)}, u32[]{:S(2)}) %collective-permute-start.13) | collective-permute-done | bytes 458784 | tf_op jit(solution)/shard_map/one_both/ppermute | solution.py:90
  58.6 1.3 collective-permute-start.19
  60.5 9.5 %collective-permute-done.18 = bf16[896,256]{1,0:T(8,128)(2,1)S(1)} collective-permute-done((bf16[896,256]{1,0:T(8,128)(2,1)S(1)}, bf16[896,256]{1,0:T(8,128)(2,1)S(1)}, u32[]{:S(2)}, u32[]{:S(2)}) %collective-permute-start.18) | collective-permute-done | bytes 458784 | tf_op jit(solution)/shard_map/two_both/ppermute | solution.py:90
  72.0 1.5 gradients_here.1
  73.5 1.4 collective-permute-done.19.last_ref
  74.9 3.1 %gradients_there.1 = (bf16[256,448]{1,0:T(8,128)(2,1)S(1)}, bf16[256,448]{1,0:T(8,128)(2,1)S(1)}, bf16[2,256,896]{2,1,0:T(8,128)(2,1)S(1)}) custom-call(s32[4]{0:T(128)S(1)} %pad_add_fusion.3.at_ref, bf16[896,7168]{1,0:T(8,128)(2,1)S(1)} %pad_maximum_fusion.tokens_ref, bf16[256,448]{1,0:T(8,128)(2,1)S(1)} %get-tuple-element.470.here_a, ...), custom_call_target="tpu_custom_call" | custom-call | flops 1000000000 | bytes 10000000 | tf_op jit(solution)/shard_map/gradients_there/pallas_call | solution.py:150
  78.5 1.8 %contract.7 = bf16[2,256,896]{2,1,0:T(8,128)(2,1)S(1)} custom-call(s32[3]{0:T(128)S(1)} %get-tuple-element.550.at_ref, bf16[896,7168]{1,0:T(8,128)(2,1)S(1)} %pad_maximum_fusion.tokens_ref, bf16[256,448]{1,0:T(8,128)(2,1)S(1)} %get-tuple-element.470.here_a, bf16[256,448]{1,0:T(8,128)(2,1)S(1)} %get-tuple-element.471.here_b, ...), custom_call_target="tpu_custom_call" | custom-call | flops 1000000000 | bytes 10000000 | tf_op jit(solution)/shard_map/contract/pallas_call | solution.py:150
  80.5 1.8 %contract.8 = bf16[2,256,896]{2,1,0:T(8,128)(2,1)S(1)} custom-call(s32[3]{0:T(128)S(1)} %get-tuple-element.551.at_ref, bf16[896,7168]{1,0:T(8,128)(2,1)S(1)} %pad_maximum_fusion.tokens_ref, bf16[256,448]{1,0:T(8,128)(2,1)S(1)} %get-tuple-element.470.here_a, bf16[256,448]{1,0:T(8,128)(2,1)S(1)} %get-tuple-element.471.here_b, ...), custom_call_target="tpu_custom_call" | custom-call | flops 1000000000 | bytes 10000000 | tf_op jit(solution)/shard_map/contract/pallas_call | solution.py:150
  82.3 1.3 collective-permute-start.22
  83.6 2.1 %contract.9 = f32[2,256,896]{2,1,0:T(8,128)S(1)} custom-call(s32[3]{0:T(128)S(1)} %get-tuple-element.552.at_ref, bf16[896,7168]{1,0:T(8,128)(2,1)S(1)} %pad_maximum_fusion.tokens_ref, bf16[256,448]{1,0:T(8,128)(2,1)S(1)} %get-tuple-element.470.here_a, bf16[256,448]{1,0:T(8,128)(2,1)S(1)} %get-tuple-element.471.here_b, ...), custom_call_target="tpu_custom_call" | custom-call | flops 1000000000 | bytes 10000000 | tf_op jit(solution)/shard_map/contract/pallas_call | solution.py:150
  85.6 5.0 %collective-permute-done.20 = bf16[2,256,896]{2,1,0:T(8,128)(2,1)S(1)} collective-permute-done((bf16[2,256,896]{2,1,0:T(8,128)(2,1)S(1)}, bf16[2,256,896]{2,1,0:T(8,128)(2,1)S(1)}, u32[]{:S(2)}, u32[]{:S(2)}) %collective-permute-start.20) | collective-permute-done | bytes 917536 | tf_op jit(solution)/shard_map/seconds_3/ppermute | solution.py:90
  90.8 1.3 collective-permute-start.23
  92.0 1.8 %contract.10 = bf16[2,256,896]{2,1,0:T(8,128)(2,1)S(1)} custom-call(s32[3]{0:T(128)S(1)} %get-tuple-element.549.at_ref, bf16[896,7168]{1,0:T(8,128)(2,1)S(1)} %pad_maximum_fusion.tokens_ref, bf16[256,448]{1,0:T(8,128)(2,1)S(1)} %get-tuple-element.470.here_a, bf16[256,448]{1,0:T(8,128)(2,1)S(1)} %get-tuple-element.471.here_b, ...), custom_call_target="tpu_custom_call" | custom-call | flops 1000000000 | bytes 10000000 | tf_op jit(solution)/shard_map/contract/pallas_call | solution.py:150
  93.9 1.8 %contract.11 = f32[2,256,896]{2,1,0:T(8,128)S(1)} custom-call(s32[3]{0:T(128)S(1)} %get-tuple-element.551.at_ref, bf16[896,7168]{1,0:T(8,128)(2,1)S(1)} %pad_maximum_fusion.tokens_ref, bf16[256,448]{1,0:T(8,128)(2,1)S(1)} %get-tuple-element.470.here_a, bf16[256,448]{1,0:T(8,128)(2,1)S(1)} %get-tuple-element.471.here_b, ...), custom_call_target="tpu_custom_call" | custom-call | flops 1000000000 | bytes 10000000 | tf_op jit(solution)/shard_map/contract/pallas_call | solution.py:150
  95.7 1.8 %contract.12 = f32[2,256,896]{2,1,0:T(8,128)S(1)} custom-call(s32[3]{0:T(128)S(1)} %get-tuple-element.550.at_ref, bf16[896,7168]{1,0:T(8,128)(2,1)S(1)} %pad_maximum_fusion.tokens_ref, bf16[256,448]{1,0:T(8,128)(2,1)S(1)} %get-tuple-element.470.here_a, bf16[256,448]{1,0:T(8,128)(2,1)S(1)} %get-tuple-element.471.here_b, ...), custom_call_target="tpu_custom_call" | custom-call | flops 1000000000 | bytes 10000000 | tf_op jit(solution)/shard_map/contract/pallas_call | solution.py:150
  97.6 1.8 %contract.13 = f32[2,256,896]{2,1,0:T(8,128)S(1)} custom-call(s32[3]{0:T(128)S(1)} %get-tuple-element.549.at_ref, bf16[896,7168]{1,0:T(8,128)(2,1)S(1)} %pad_maximum_fusion.tokens_ref, bf16[256,448]{1,0:T(8,128)(2,1)S(1)} %get-tuple-element.470.here_a, bf16[256,448]{1,0:T(8,128)(2,1)S(1)} %get-tuple-element.471.here_b, ...), custom_call_target="tpu_custom_call" | custom-call | flops 1000000000 | bytes 10000000 | tf_op jit(solution)/shard_map/contract/pallas_call | solution.py:150
  100.5 2.9 %collective-permute-done.23 = bf16[256,896]{1,0:T(8,128)(2,1)S(1)} collective-permute-done((bf16[256,896]{1,0:T(8,128)(2,1)S(1)}, bf16[256,896]{1,0:T(8,128)(2,1)S(1)}, u32[]{:S(2)}, u32[]{:S(2)}) %collective-permute-start.23) | collective-permute-done | bytes 458784 | tf_op jit(solution)/shard_map/first_3/ppermute | solution.py:90
  103.6 1.8 %collective-permute-done.22 = bf16[2,256,896]{2,1,0:T(8,128)(2,1)S(1)} collective-permute-done((bf16[2,256,896]{2,1,0:T(8,128)(2,1)S(1)}, bf16[2,256,896]{2,1,0:T(8,128)(2,1)S(1)}, u32[]{:S(2)}, u32[]{:S(2)}) %collective-permute-start.22) | collective-permute-done | bytes 917536 | tf_op jit(solution)/shard_map/seconds_2/ppermute | solution.py:90
  105.5 1.3 collective-permute-start.26
  106.8 1.3 collective-permute-start.27
  108.5 4.7 %collective-permute-done.26 = bf16[256,896]{1,0:T(8,128)(2,1)S(1)} collective-permute-done((bf16[256,896]{1,0:T(8,128)(2,1)S(1)}, bf16[256,896]{1,0:T(8,128)(2,1)S(1)}, u32[]{:S(2)}, u32[]{:S(2)}) %collective-permute-start.26) | collective-permute-done | bytes 458784 | tf_op jit(solution)/shard_map/first_2/ppermute | solution.py:90
  113.2 5.7 %collective-permute-done.27 = bf16[256,896]{1,0:T(8,128)(2,1)S(1)} collective-permute-done((bf16[256,896]{1,0:T(8,128)(2,1)S(1)}, bf16[256,896]{1,0:T(8,128)(2,1)S(1)}, u32[]{:S(2)}, u32[]{:S(2)}) %collective-permute-start.27) | collective-permute-done | bytes 458784 | tf_op jit(solution)/shard_map/three_in/ppermute | solution.py:90
  119.1 1.3 collective-permute-start.29
  120.4 3.0 %collective-permute-start.28 = (bf16[256,896]{1,0:T(8,128)(2,1)S(1)}, bf16[256,896]{1,0:T(8,128)(2,1)S(1)}, u32[]{:S(2)}, u32[]{:S(2)}) collective-permute-start(bf16[256,896]{1,0:T(8,128)(2,1)S(1)} %fusion.64), channel_id=1, source_target_pairs={{4,8},{5,9},{6,10},{7,11},{8,4},{9,5},{10,6},{11,7},{20,24},{21,25... | collective-permute-start | bytes 1376264 | tf_op jit(solution)/shard_map/two/ppermute | solution.py:90
  123.5 6.4 %collective-permute-done.24 = bf16[2,256,896]{2,1,0:T(8,128)(2,1)S(1)} collective-permute-done((bf16[2,256,896]{2,1,0:T(8,128)(2,1)S(1)}, bf16[2,256,896]{2,1,0:T(8,128)(2,1)S(1)}, u32[]{:S(2)}, u32[]{:S(2)}) %collective-permute-start.24) | collective-permute-done | bytes 917536 | tf_op jit(solution)/shard_map/seconds_0/ppermute | solution.py:90
  131.7 3.0 %collective-permute-start.31 = (bf16[256,896]{1,0:T(8,128)(2,1)S(1)}, bf16[256,896]{1,0:T(8,128)(2,1)S(1)}, u32[]{:S(2)}, u32[]{:S(2)}) collective-permute-start(bf16[256,896]{1,0:T(8,128)(2,1)S(1)} %add_convert_fusion.2), channel_id=1, source_target_pairs={{4,8},{5,9},{6,10},{7,11},{8,4},{9,5},{10,6},{11,7},{20,24},{21,25... | collective-permute-start | bytes 1376264 | tf_op jit(solution)/shard_map/three/ppermute | solution.py:90
  134.8 3.0 %collective-permute-done.30.refs_1_ = bf16[256,896]{1,0:T(8,128)(2,1)S(1)} collective-permute-done((bf16[256,896]{1,0:T(8,128)(2,1)S(1)}, bf16[256,896]{1,0:T(8,128)(2,1)S(1)}, u32[]{:S(2)}, u32[]{:S(2)}) %collective-permute-start.30) | collective-permute-done | bytes 458784 | tf_op jit(solution)/shard_map/first_0/ppermute | solution.py:90
  137.7 2.3 %collective-permute-done.32.refs_3_ = bf16[256,896]{1,0:T(8,128)(2,1)S(1)} collective-permute-done((bf16[256,896]{1,0:T(8,128)(2,1)S(1)}, bf16[256,896]{1,0:T(8,128)(2,1)S(1)}, u32[]{:S(2)}, u32[]{:S(2)}) %collective-permute-start.32) | collective-permute-done | bytes 458784 | tf_op jit(solution)/shard_map/one/ppermute | solution.py:90
  140.0 1.9 %collective-permute-done.31.refs_2_ = bf16[256,896]{1,0:T(8,128)(2,1)S(1)} collective-permute-done((bf16[256,896]{1,0:T(8,128)(2,1)S(1)}, bf16[256,896]{1,0:T(8,128)(2,1)S(1)}, u32[]{:S(2)}, u32[]{:S(2)}) %collective-permute-start.31) | collective-permute-done | bytes 458784 | tf_op jit(solution)/shard_map/three/ppermute | solution.py:90
  141.9 1.3 by_rows.1
  143.2 4.7 %collective-permute-start.33 = (f32[448,256]{1,0:T(8,128)S(1)}, f32[448,256]{1,0:T(8,128)S(1)}, u32[]{:S(2)}, u32[]{:S(2)}) collective-permute-start(f32[448,256]{1,0:T(8,128)S(1)} %get-tuple-element.545), channel_id=1, source_target_pairs={{0,1},{1,0},{2,3},{3,2},{4,5},{5,4},{6,7},{7,6},{8,9},{9,8},{10,11... | collective-permute-start | bytes 1376264 | tf_op jit(solution)/shard_map/taken/ppermute | solution.py:90
  148.0 1.4 collective-permute-done.33.taken_ref
  149.4 1.8 %finish.1 = (f32[448,256]{1,0:T(8,128)}, f32[448,256]{1,0:T(8,128)}, f32[448,256]{1,0:T(8,128)}) custom-call(s32[2]{0:T(128)S(1)} %pad_add_fusion.at_ref, f32[448,256]{1,0:T(8,128)S(1)} %get-tuple-element.544.kept_ref, f32[448,256]{1,0:T(8,128)S(1)} %collective-permute-done.33.taken_ref, bf16[448,512]{1,0:T(8,128)(2,1)S(1)} %copy-done.4, ...), custom_call_target="tpu_custom_call" | custom-call | flops 1000000000 | bytes 10000000 | tf_op jit(solution)/shard_map/finish/pallas_call | solution.py:150
  (84 shorter events, 21.7 us)
Async XLA Ops:
  0.6 3.7 %collective-permute-start = (bf16[448,512]{1,0:T(8,128)(2,1)}, bf16[448,512]{1,0:T(8,128)(2,1)S(1)}, u32[]{:S(2)}, u32[]{:S(2)}) collective-permute-start(bf16[448,512]{1,0:T(8,128)(2,1)} %weight_ref.1), channel_id=1, source_target_pairs={{0,1},{1,0},{2,3},{3,2},{4,5},{5,4},{6,7},{7,6},{8,9},{9,8},{10,11... | collective-permute-start | bytes 1376264 | tf_op jit(solution)/shard_map/other_weight/ppermute | solution.py:90
  1.4 2.9 %collective-permute-start.1 = (bf16[448,512]{1,0:T(8,128)(2,1)}, bf16[448,512]{1,0:T(8,128)(2,1)S(1)}, u32[]{:S(2)}, u32[]{:S(2)}) collective-permute-start(bf16[448,512]{1,0:T(8,128)(2,1)} %probe_ref.3), channel_id=1, source_target_pairs={{0,1},{1,0},{2,3},{3,2},{4,5},{5,4},{6,7},{7,6},{8,9},{9,8},{10,11... | collective-permute-start | bytes 1376264 | tf_op jit(solution)/shard_map/other_probe/ppermute | solution.py:90
  1.5 1.0 copy-start.2
  2.5 1.0 copy-start.3
  4.3 1.1 copy-start
  4.9 19.1 %collective-permute-start.2 = (bf16[448,7168]{1,0:T(8,128)(2,1)}, bf16[448,7168]{1,0:T(8,128)(2,1)}, u32[]{:S(2)}, u32[]{:S(2)}) collective-permute-start(bf16[448,7168]{1,0:T(8,128)(2,1)} %param.7), channel_id=1, source_target_pairs={{0,1},{1,0},{2,3},{3,2},{4,5},{5,4},{6,7},{7,6},{8,9},{9,8},{10,11... | collective-permute-start | bytes 19267592 | tf_op jit(solution)/shard_map/other_acts/ppermute | solution.py:90
  5.4 6.4 %collective-permute-start.5 = (bf16[448,512]{1,0:T(8,128)(2,1)S(1)}, bf16[448,512]{1,0:T(8,128)(2,1)S(1)}, u32[]{:S(2)}, u32[]{:S(2)}) collective-permute-start(bf16[448,512]{1,0:T(8,128)(2,1)S(1)} %copy-done), channel_id=1, source_target_pairs={{0,1},{1,0},{2,3},{3,2},{4,5},{5,4},{6,7},{7,6},{8,9},{9,8},{10,11... | collective-permute-start | bytes 1376264 | tf_op jit(solution)/shard_map/other_up/ppermute | solution.py:90
  5.7 13.8 %collective-permute-start.4 = (bf16[896,256]{1,0:T(8,128)(2,1)S(1)}, bf16[896,256]{1,0:T(8,128)(2,1)S(1)}, u32[]{:S(2)}, u32[]{:S(2)}) collective-permute-start(bf16[896,256]{1,0:T(8,128)(2,1)S(1)} %get-tuple-element.296), channel_id=1, source_target_pairs={{4,8},{5,9},{6,10},{7,11},{8,4},{9,5},{10,6},{11,7},{20,24},{21,25... | collective-permute-start | bytes 1376264 | tf_op jit(solution)/shard_map/near/ppermute | solution.py:90
  8.9 11.7 %collective-permute-start.3 = (bf16[896,256]{1,0:T(8,128)(2,1)S(1)}, bf16[896,256]{1,0:T(8,128)(2,1)S(1)}, u32[]{:S(2)}, u32[]{:S(2)}) collective-permute-start(bf16[896,256]{1,0:T(8,128)(2,1)S(1)} %get-tuple-element.296), channel_id=1, source_target_pairs={{0,4},{1,5},{2,6},{3,7},{4,0},{5,1},{6,2},{7,3},{8,12},{9,13},{10,... | collective-permute-start | bytes 1376264 | tf_op jit(solution)/shard_map/one/ppermute | solution.py:90
  9.0 15.1 %collective-permute-start.6 = (bf16[896,256]{1,0:T(8,128)(2,1)S(1)}, bf16[896,256]{1,0:T(8,128)(2,1)S(1)}, u32[]{:S(2)}, u32[]{:S(2)}) collective-permute-start(bf16[896,256]{1,0:T(8,128)(2,1)S(1)} %get-tuple-element.296), channel_id=1, source_target_pairs={{0,2},{1,3},{2,0},{3,1},{4,6},{5,7},{6,4},{7,5},{8,10},{9,11},{10,... | collective-permute-start | bytes 1376264 | tf_op jit(solution)/shard_map/across/ppermute | solution.py:90
  20.6 13.8 %collective-permute-start.8 = (bf16[896,256]{1,0:T(8,128)(2,1)S(1)}, bf16[896,256]{1,0:T(8,128)(2,1)S(1)}, u32[]{:S(2)}, u32[]{:S(2)}) collective-permute-start(bf16[896,256]{1,0:T(8,128)(2,1)S(1)} %collective-permute-done.3), channel_id=1, source_target_pairs={{4,8},{5,9},{6,10},{7,11},{8,4},{9,5},{10,6},{11,7},{20,24},{21,25... | collective-permute-start | bytes 1376264 | tf_op jit(solution)/shard_map/two_in/ppermute | solution.py:90
  22.8 11.7 %collective-permute-start.7 = (bf16[896,256]{1,0:T(8,128)(2,1)S(1)}, bf16[896,256]{1,0:T(8,128)(2,1)S(1)}, u32[]{:S(2)}, u32[]{:S(2)}) collective-permute-start(bf16[896,256]{1,0:T(8,128)(2,1)S(1)} %collective-permute-done.4), channel_id=1, source_target_pairs={{4,0},{5,1},{6,2},{7,3},{8,12},{9,13},{10,14},{11,15},{20,16},{21,... | collective-permute-start | bytes 1376264 | tf_op jit(solution)/shard_map/two_out/ppermute | solution.py:90
  24.2 13.5 %collective-permute-start.10 = (bf16[896,256]{1,0:T(8,128)(2,1)S(1)}, bf16[896,256]{1,0:T(8,128)(2,1)S(1)}, u32[]{:S(2)}, u32[]{:S(2)}) collective-permute-start(bf16[896,256]{1,0:T(8,128)(2,1)S(1)} %broadcast_select_fusion.1), channel_id=1, source_target_pairs={{0,2},{1,17},{2,0},{3,19},{4,6},{5,21},{6,4},{7,23},{8,10},{9,25},... | collective-permute-start | bytes 1376264 | tf_op jit(solution)/shard_map/corner/ppermute | solution.py:90
  25.5 12.2 %collective-permute-start.11 = (bf16[896,256]{1,0:T(8,128)(2,1)S(1)}, bf16[896,256]{1,0:T(8,128)(2,1)S(1)}, u32[]{:S(2)}, u32[]{:S(2)}) collective-permute-start(bf16[896,256]{1,0:T(8,128)(2,1)S(1)} %collective-permute-done.3), channel_id=1, source_target_pairs={{0,2},{1,17},{2,0},{3,19},{4,6},{5,21},{6,4},{7,23},{8,10},{9,25},... | collective-permute-start | bytes 1376264 | tf_op jit(solution)/shard_map/one_first/ppermute | solution.py:90
  35.3 9.8 %collective-permute-start.9 = (bf16[896,256]{1,0:T(8,128)(2,1)S(1)}, bf16[896,256]{1,0:T(8,128)(2,1)S(1)}, u32[]{:S(2)}, u32[]{:S(2)}) collective-permute-start(bf16[896,256]{1,0:T(8,128)(2,1)S(1)} %add.188), channel_id=1, source_target_pairs={{4,0},{5,1},{6,2},{7,3},{8,12},{9,13},{10,14},{11,15},{20,16},{21,... | collective-permute-start | bytes 1376264 | tf_op jit(solution)/shard_map/three_out/ppermute | solution.py:90
  37.7 20.2 %collective-permute-start.15 = (bf16[896,256]{1,0:T(8,128)(2,1)S(1)}, bf16[896,256]{1,0:T(8,128)(2,1)S(1)}, u32[]{:S(2)}, u32[]{:S(2)}) collective-permute-start(bf16[896,256]{1,0:T(8,128)(2,1)S(1)} %add.188), channel_id=1, source_target_pairs={{0,16},{1,3},{2,18},{3,1},{4,20},{5,7},{6,22},{7,5},{8,24},{9,11},... | collective-permute-start | bytes 1376264 | tf_op jit(solution)/shard_map/two_second/ppermute | solution.py:90
  38.0 9.8 %collective-permute-start.12 = (bf16[896,256]{1,0:T(8,128)(2,1)S(1)}, bf16[896,256]{1,0:T(8,128)(2,1)S(1)}, u32[]{:S(2)}, u32[]{:S(2)}) collective-permute-start(bf16[896,256]{1,0:T(8,128)(2,1)S(1)} %add.188), channel_id=1, source_target_pairs={{0,2},{1,17},{2,0},{3,19},{4,6},{5,21},{6,4},{7,23},{8,10},{9,25},... | collective-permute-start | bytes 1376264 | tf_op jit(solution)/shard_map/two_first/ppermute | solution.py:90
  39.9 15.7 %collective-permute-start.13 = (bf16[896,256]{1,0:T(8,128)(2,1)S(1)}, bf16[896,256]{1,0:T(8,128)(2,1)S(1)}, u32[]{:S(2)}, u32[]{:S(2)}) collective-permute-start(bf16[896,256]{1,0:T(8,128)(2,1)S(1)} %collective-permute-done.11), channel_id=1, source_target_pairs={{0,16},{1,3},{2,18},{3,1},{4,20},{5,7},{6,22},{7,5},{8,24},{9,11},... | collective-permute-start | bytes 1376264 | tf_op jit(solution)/shard_map/one_both/ppermute | solution.py:90
  45.2 26.1 %collective-permute-start.16 = (bf16[896,256]{1,0:T(8,128)(2,1)S(1)}, bf16[896,256]{1,0:T(8,128)(2,1)S(1)}, u32[]{:S(2)}, u32[]{:S(2)}) collective-permute-start(bf16[896,256]{1,0:T(8,128)(2,1)S(1)} %add.198), channel_id=1, source_target_pairs={{0,16},{1,3},{2,18},{3,1},{4,20},{5,7},{6,22},{7,5},{8,24},{9,11},... | collective-permute-start | bytes 1376264 | tf_op jit(solution)/shard_map/three_second/ppermute | solution.py:90
  45.6 13.0 %collective-permute-start.14 = (bf16[896,256]{1,0:T(8,128)(2,1)S(1)}, bf16[896,256]{1,0:T(8,128)(2,1)S(1)}, u32[]{:S(2)}, u32[]{:S(2)}) collective-permute-start(bf16[896,256]{1,0:T(8,128)(2,1)S(1)} %add.198), channel_id=1, source_target_pairs={{0,2},{1,17},{2,0},{3,19},{4,6},{5,21},{6,4},{7,23},{8,10},{9,25},... | collective-permute-start | bytes 1376264 | tf_op jit(solution)/shard_map/three_first/ppermute | solution.py:90
  47.8 22.8 %collective-permute-start.17 = (bf16[896,256]{1,0:T(8,128)(2,1)S(1)}, bf16[896,256]{1,0:T(8,128)(2,1)S(1)}, u32[]{:S(2)}, u32[]{:S(2)}) collective-permute-start(bf16[896,256]{1,0:T(8,128)(2,1)S(1)} %broadcast_select_fusion), channel_id=1, source_target_pairs={{0,4},{1,5},{2,6},{3,7},{4,0},{5,1},{6,2},{7,3},{8,12},{9,13},{10,... | collective-permute-start | bytes 1376264 | tf_op jit(solution)/shard_map/one_second/ppermute | solution.py:90
  56.3 13.7 %collective-permute-start.18 = (bf16[896,256]{1,0:T(8,128)(2,1)S(1)}, bf16[896,256]{1,0:T(8,128)(2,1)S(1)}, u32[]{:S(2)}, u32[]{:S(2)}) collective-permute-start(bf16[896,256]{1,0:T(8,128)(2,1)S(1)} %collective-permute-done.12), channel_id=1, source_target_pairs={{0,16},{1,3},{2,18},{3,1},{4,20},{5,7},{6,22},{7,5},{8,24},{9,11},... | collective-permute-start | bytes 1376264 | tf_op jit(solution)/shard_map/two_both/ppermute | solution.py:90
  58.6 16.3 %collective-permute-start.19 = (bf16[896,256]{1,0:T(8,128)(2,1)S(1)}, bf16[896,256]{1,0:T(8,128)(2,1)S(1)}, u32[]{:S(2)}, u32[]{:S(2)}) collective-permute-start(bf16[896,256]{1,0:T(8,128)(2,1)S(1)} %collective-permute-done.14), channel_id=1, source_target_pairs={{0,16},{1,3},{2,18},{3,1},{4,20},{5,7},{6,22},{7,5},{8,24},{9,11},... | collective-permute-start | bytes 1376264 | tf_op jit(solution)/shard_map/three_both/ppermute | solution.py:90
  71.3 0.7 copy-start.1
  78.0 12.6 %collective-permute-start.20 = (bf16[2,256,896]{2,1,0:T(8,128)(2,1)S(1)}, bf16[2,256,896]{2,1,0:T(8,128)(2,1)S(1)}, u32[]{:S(2)}, u32[]{:S(2)}) collective-permute-start(bf16[2,256,896]{2,1,0:T(8,128)(2,1)S(1)} %get-tuple-element.442), channel_id=1, source_target_pairs={{0,16},{1,3},{2,18},{3,1},{4,20},{5,7},{6,22},{7,5},{8,24},{9,11},... | collective-permute-start | bytes 2752520 | tf_op jit(solution)/shard_map/seconds_3/ppermute | solution.py:90
  80.3 20.0 %collective-permute-start.21 = (bf16[2,256,896]{2,1,0:T(8,128)(2,1)S(1)}, bf16[2,256,896]{2,1,0:T(8,128)(2,1)S(1)}, u32[]{:S(2)}, u32[]{:S(2)}) collective-permute-start(bf16[2,256,896]{2,1,0:T(8,128)(2,1)S(1)} %contract.7), channel_id=1, source_target_pairs={{0,4},{1,5},{2,6},{3,7},{4,0},{5,1},{6,2},{7,3},{8,12},{9,13},{10,... | collective-permute-start | bytes 2752520 | tf_op jit(solution)/shard_map/raw_1/ppermute | solution.py:90
  82.3 23.1 %collective-permute-start.22 = (bf16[2,256,896]{2,1,0:T(8,128)(2,1)S(1)}, bf16[2,256,896]{2,1,0:T(8,128)(2,1)S(1)}, u32[]{:S(2)}, u32[]{:S(2)}) collective-permute-start(bf16[2,256,896]{2,1,0:T(8,128)(2,1)S(1)} %contract.8), channel_id=1, source_target_pairs={{0,16},{1,3},{2,18},{3,1},{4,20},{5,7},{6,22},{7,5},{8,24},{9,11},... | collective-permute-start | bytes 2752520 | tf_op jit(solution)/shard_map/seconds_2/ppermute | solution.py:90
  90.8 12.7 %collective-permute-start.23 = (bf16[256,896]{1,0:T(8,128)(2,1)S(1)}, bf16[256,896]{1,0:T(8,128)(2,1)S(1)}, u32[]{:S(2)}, u32[]{:S(2)}) collective-permute-start(bf16[256,896]{1,0:T(8,128)(2,1)S(1)} %fusion.66), channel_id=1, source_target_pairs={{0,2},{1,17},{2,0},{3,19},{4,6},{5,21},{6,4},{7,23},{8,10},{9,25},... | collective-permute-start | bytes 1376264 | tf_op jit(solution)/shard_map/first_3/ppermute | solution.py:90
  105.5 7.7 %collective-permute-start.26 = (bf16[256,896]{1,0:T(8,128)(2,1)S(1)}, bf16[256,896]{1,0:T(8,128)(2,1)S(1)}, u32[]{:S(2)}, u32[]{:S(2)}) collective-permute-start(bf16[256,896]{1,0:T(8,128)(2,1)S(1)} %fusion.67), channel_id=1, source_target_pairs={{0,2},{1,17},{2,0},{3,19},{4,6},{5,21},{6,4},{7,23},{8,10},{9,25},... | collective-permute-start | bytes 1376264 | tf_op jit(solution)/shard_map/first_2/ppermute | solution.py:90
  106.8 12.1 %collective-permute-start.27 = (bf16[256,896]{1,0:T(8,128)(2,1)S(1)}, bf16[256,896]{1,0:T(8,128)(2,1)S(1)}, u32[]{:S(2)}, u32[]{:S(2)}) collective-permute-start(bf16[256,896]{1,0:T(8,128)(2,1)S(1)} %fusion.65), channel_id=1, source_target_pairs={{0,4},{1,5},{2,6},{3,7},{12,8},{13,9},{14,10},{15,11},{16,20},{17,... | collective-permute-start | bytes 1376264 | tf_op jit(solution)/shard_map/three_in/ppermute | solution.py:90
  108.1 21.8 %collective-permute-start.24 = (bf16[2,256,896]{2,1,0:T(8,128)(2,1)S(1)}, bf16[2,256,896]{2,1,0:T(8,128)(2,1)S(1)}, u32[]{:S(2)}, u32[]{:S(2)}) collective-permute-start(bf16[2,256,896]{2,1,0:T(8,128)(2,1)S(1)} %add_convert_fusion), channel_id=1, source_target_pairs={{0,16},{1,3},{2,18},{3,1},{4,20},{5,7},{6,22},{7,5},{8,24},{9,11},... | collective-permute-start | bytes 2752520 | tf_op jit(solution)/shard_map/seconds_0/ppermute | solution.py:90
  108.2 15.2 %collective-permute-start.25 = (bf16[256,896]{1,0:T(8,128)(2,1)S(1)}, bf16[256,896]{1,0:T(8,128)(2,1)S(1)}, u32[]{:S(2)}, u32[]{:S(2)}) collective-permute-start(bf16[256,896]{1,0:T(8,128)(2,1)S(1)} %fusion.69), channel_id=1, source_target_pairs={{0,2},{1,17},{2,0},{3,19},{4,6},{5,21},{6,4},{7,23},{8,10},{9,25},... | collective-permute-start | bytes 1376264 | tf_op jit(solution)/shard_map/first_1/ppermute | solution.py:90
  119.1 11.7 %collective-permute-start.29 = (bf16[256,896]{1,0:T(8,128)(2,1)S(1)}, bf16[256,896]{1,0:T(8,128)(2,1)S(1)}, u32[]{:S(2)}, u32[]{:S(2)}) collective-permute-start(bf16[256,896]{1,0:T(8,128)(2,1)S(1)} %fusion.64), channel_id=1, source_target_pairs={{0,4},{1,5},{2,6},{3,7},{12,8},{13,9},{14,10},{15,11},{16,20},{17,... | collective-permute-start | bytes 1376264 | tf_op jit(solution)/shard_map/two_in/ppermute | solution.py:90
  120.4 11.2 %collective-permute-start.28 = (bf16[256,896]{1,0:T(8,128)(2,1)S(1)}, bf16[256,896]{1,0:T(8,128)(2,1)S(1)}, u32[]{:S(2)}, u32[]{:S(2)}) collective-permute-start(bf16[256,896]{1,0:T(8,128)(2,1)S(1)} %fusion.64), channel_id=1, source_target_pairs={{4,8},{5,9},{6,10},{7,11},{8,4},{9,5},{10,6},{11,7},{20,24},{21,25... | collective-permute-start | bytes 1376264 | tf_op jit(solution)/shard_map/two/ppermute | solution.py:90
  130.0 7.7 %collective-permute-start.30 = (bf16[256,896]{1,0:T(8,128)(2,1)S(1)}, bf16[256,896]{1,0:T(8,128)(2,1)S(1)}, u32[]{:S(2)}, u32[]{:S(2)}) collective-permute-start(bf16[256,896]{1,0:T(8,128)(2,1)S(1)} %fusion.68), channel_id=1, source_target_pairs={{0,2},{1,17},{2,0},{3,19},{4,6},{5,21},{6,4},{7,23},{8,10},{9,25},... | collective-permute-start | bytes 1376264 | tf_op jit(solution)/shard_map/first_0/ppermute | solution.py:90
  131.6 8.4 %collective-permute-start.32 = (bf16[256,896]{1,0:T(8,128)(2,1)S(1)}, bf16[256,896]{1,0:T(8,128)(2,1)S(1)}, u32[]{:S(2)}, u32[]{:S(2)}) collective-permute-start(bf16[256,896]{1,0:T(8,128)(2,1)S(1)} %add_convert_fusion.1), channel_id=1, source_target_pairs={{0,4},{1,5},{2,6},{3,7},{4,0},{5,1},{6,2},{7,3},{8,12},{9,13},{10,... | collective-permute-start | bytes 1376264 | tf_op jit(solution)/shard_map/one/ppermute | solution.py:90
  131.7 10.2 %collective-permute-start.31 = (bf16[256,896]{1,0:T(8,128)(2,1)S(1)}, bf16[256,896]{1,0:T(8,128)(2,1)S(1)}, u32[]{:S(2)}, u32[]{:S(2)}) collective-permute-start(bf16[256,896]{1,0:T(8,128)(2,1)S(1)} %add_convert_fusion.2), channel_id=1, source_target_pairs={{4,8},{5,9},{6,10},{7,11},{8,4},{9,5},{10,6},{11,7},{20,24},{21,25... | collective-permute-start | bytes 1376264 | tf_op jit(solution)/shard_map/three/ppermute | solution.py:90
  141.9 7.4 %copy-start.4 = (bf16[448,512]{1,0:T(8,128)(2,1)S(1)}, bf16[448,512]{1,0:T(8,128)(2,1)}, u32[]{:S(2)}) copy-start(bf16[448,512]{1,0:T(8,128)(2,1)} %probe_ref.3) | copy-start | bytes 1376260
  141.9 7.4 %copy-start.5 = (f32[448,256]{1,0:T(8,128)S(1)}, f32[448,256]{1,0:T(8,128)}, u32[]{:S(2)}) copy-start(f32[448,256]{1,0:T(8,128)} %momentum_ref) | copy-start | bytes 1376260
  141.9 7.4 %copy-start.6 = (f32[448,256]{1,0:T(8,128)S(1)}, f32[448,256]{1,0:T(8,128)}, u32[]{:S(2)}) copy-start(f32[448,256]{1,0:T(8,128)} %curvature_ref.1) | copy-start | bytes 1376260
  143.2 6.1 %collective-permute-start.33 = (f32[448,256]{1,0:T(8,128)S(1)}, f32[448,256]{1,0:T(8,128)S(1)}, u32[]{:S(2)}, u32[]{:S(2)}) collective-permute-start(f32[448,256]{1,0:T(8,128)S(1)} %get-tuple-element.545), channel_id=1, source_target_pairs={{0,1},{1,0},{2,3},{3,2},{4,5},{5,4},{6,7},{7,6},{8,9},{9,8},{10,11... | collective-permute-start | bytes 1376264 | tf_op jit(solution)/shard_map/taken/ppermute | solution.py:90

commit v6 on v5

--- a/solution.py
+++ b/solution.py
@@ -146,7 +146,7 @@
 SMEM = pl.BlockSpec(memory_space=pltpu.SMEM)
 
 
-def call(kernel, outs, scalars, *operands, name, cost=10**7, aliases=None):
+def call(kernel, outs, scalars, *operands, name, cost=3 * 10**6, aliases=None):
     return pl.pallas_call(
         kernel,
         out_shape=outs,
@@ -278,7 +278,7 @@
 
             @pl.when(at_ref[2] != part)
             def _():
-                given_ref[rows, :] = value
+                given_ref[rows, :] = value.astype(given_ref.dtype)
 
         for begin in range(0, depth, 128):
             size = min(128, depth - begin)
@@ -289,8 +289,8 @@
             if below < size:
                 put(1, begin + below - half, total[below:])
 
-    out = jax.ShapeDtypeStruct((half, width), jnp.float32)
-    return call(kernel, [out, out], scalars, *terms, name="by_rows")
+    outs = [jax.ShapeDtypeStruct((half, width), dtype) for dtype in (jnp.float32, jnp.bfloat16)]
+    return call(kernel, outs, scalars, *terms, name="by_rows")
 
 
 def finish(scalars, kept, taken, probe, momentum, curvature):
@@ -302,7 +302,7 @@
         for i in range(shares):
             columns = pl.ds(i * head, head)
             mine = own_first if i == 0 else jnp.logical_not(own_first)
-            share = jnp.where(mine, kept_ref[...], taken_ref[...])
+            share = jnp.where(mine, kept_ref[...], taken_ref[...].astype(jnp.float32))
             at = pl.multiple_of(at_ref[1] * (shares * head), 128) + i * head
             results = step_outputs(
                 momentum_ref[:, columns],

time: 152 us -> 151 us (level)
  no operation moved by 1% of the time
where the time goes in v6:
time: 151 us; the launch traced here: 150 us
  waiting for transfers between devices  68.1 us (45%)
  starting transfers between devices  38.2 us (25%)
  Pallas kernels  22.1 us (15%)
  matrix products  9.72 us (6%)
  other arithmetic  8.96 us (6%)
  local copies, waits for them, and re-layouts  2.12 us (1%)
    ppermute x34, waiting for transfers between devices, send(): return lax.ppermute(value, AXES, pairs_of(move))  68.1 us
    ppermute x34, starting transfers between devices, send(): return lax.ppermute(value, AXES, pairs_of(move))  38.2 us
    pallas_call x13, Pallas kernels, call(): pl.pallas_call(kernel, out_shape=outs, in_specs=[SMEM] + [VMEM] * len(ope...  22.1 us
    dot_general x15, matrix products, product(): jnp.dot(block_of(held, slot, flip_x), unit, preferred_element_type=jnp.fl...  9.72 us
    concatenate x1, other arithmetic, by_links(): jnp.concatenate([a, b], axis=0)  6.77 us
  transfers between devices with their start and end apart: 34, of which 20 were waited for; matrix products, arithmetic and copies ran while one was open for 12% of the time, Pallas kernels for 10%

profile of v6, /device:TPU:11, one launch (start us, length us, event | category | flops | bytes accessed | tf_op | source)
XLA Modules:
  0.0 150.3 jit_solution(10499061101411671595)
XLA Ops:
  1.5 1.0 copy-done.1
  5.5 3.2 %collective-permute-start.4 = (bf16[896,256]{1,0:T(8,128)(2,1)S(1)}, bf16[896,256]{1,0:T(8,128)(2,1)S(1)}, u32[]{:S(2)}, u32[]{:S(2)}) collective-permute-start(bf16[896,256]{1,0:T(8,128)(2,1)S(1)} %get-tuple-element.296), channel_id=1, source_target_pairs={{4,8},{5,9},{6,10},{7,11},{8,4},{9,5},{10,6},{11,7},{20,24},{21,25... | collective-permute-start | bytes 1376264 | tf_op jit(solution)/shard_map/near/ppermute | solution.py:90
  9.2 2.6 %collective-permute-done.5.up_b = bf16[448,512]{1,0:T(8,128)(2,1)S(1)} collective-permute-done((bf16[448,512]{1,0:T(8,128)(2,1)S(1)}, bf16[448,512]{1,0:T(8,128)(2,1)S(1)}, u32[]{:S(2)}, u32[]{:S(2)}) %collective-permute-start.5) | collective-permute-done | bytes 458784 | tf_op jit(solution)/shard_map/other_up/ppermute | solution.py:90
  11.8 7.3 %collective-permute-done.4 = bf16[896,256]{1,0:T(8,128)(2,1)S(1)} collective-permute-done((bf16[896,256]{1,0:T(8,128)(2,1)S(1)}, bf16[896,256]{1,0:T(8,128)(2,1)S(1)}, u32[]{:S(2)}, u32[]{:S(2)}) %collective-permute-start.4) | collective-permute-done | bytes 458784 | tf_op jit(solution)/shard_map/near/ppermute | solution.py:90
  19.1 1.1 collective-permute-done.3
  20.1 2.1 %collective-permute-start.8 = (bf16[896,256]{1,0:T(8,128)(2,1)S(1)}, bf16[896,256]{1,0:T(8,128)(2,1)S(1)}, u32[]{:S(2)}, u32[]{:S(2)}) collective-permute-start(bf16[896,256]{1,0:T(8,128)(2,1)S(1)} %collective-permute-done.3), channel_id=1, source_target_pairs={{4,8},{5,9},{6,10},{7,11},{8,4},{9,5},{10,6},{11,7},{20,24},{21,25... | collective-permute-start | bytes 1376264 | tf_op jit(solution)/shard_map/two_in/ppermute | solution.py:90
  22.3 1.3 collective-permute-start.7
  23.7 1.3 collective-permute-start.10
  25.2 6.8 %pad_maximum_fusion.tokens_ref = bf16[896,7168]{1,0:T(8,128)(2,1)S(1)} fusion(bf16[448,7168]{1,0:T(8,128)(2,1)} %collective-permute-done.2, bf16[448,7168]{1,0:T(8,128)(2,1)} %param.7), kind=kLoop, calls=%fused_computation | loop fusion | flops 25690112 | bytes 25690112 | tf_op jit(solution)/shard_map/concatenate | solution.py:361
  34.8 2.2 %collective-permute-start.9 = (bf16[896,256]{1,0:T(8,128)(2,1)S(1)}, bf16[896,256]{1,0:T(8,128)(2,1)S(1)}, u32[]{:S(2)}, u32[]{:S(2)}) collective-permute-start(bf16[896,256]{1,0:T(8,128)(2,1)S(1)} %add.188), channel_id=1, source_target_pairs={{4,0},{5,1},{6,2},{7,3},{8,12},{9,13},{10,14},{11,15},{20,16},{21,... | collective-permute-start | bytes 1376264 | tf_op jit(solution)/shard_map/three_out/ppermute | solution.py:90
  37.3 1.2 collective-permute-start.12
  39.2 1.3 collective-permute-start.13
  41.8 2.3 %collective-permute-done.9 = bf16[896,256]{1,0:T(8,128)(2,1)S(1)} collective-permute-done((bf16[896,256]{1,0:T(8,128)(2,1)S(1)}, bf16[896,256]{1,0:T(8,128)(2,1)S(1)}, u32[]{:S(2)}, u32[]{:S(2)}) %collective-permute-start.9) | collective-permute-done | bytes 458784 | tf_op jit(solution)/shard_map/three_out/ppermute | solution.py:90
  44.6 1.2 collective-permute-start.14
  46.9 1.3 collective-permute-start.17
  48.1 6.5 %collective-permute-done.13 = bf16[896,256]{1,0:T(8,128)(2,1)S(1)} collective-permute-done((bf16[896,256]{1,0:T(8,128)(2,1)S(1)}, bf16[896,256]{1,0:T(8,128)(2,1)S(1)}, u32[]{:S(2)}, u32[]{:S(2)}) %collective-permute-start.13) | collective-permute-done | bytes 458784 | tf_op jit(solution)/shard_map/one_both/ppermute | solution.py:90
  57.6 1.3 collective-permute-start.19
  59.6 9.7 %collective-permute-done.18 = bf16[896,256]{1,0:T(8,128)(2,1)S(1)} collective-permute-done((bf16[896,256]{1,0:T(8,128)(2,1)S(1)}, bf16[896,256]{1,0:T(8,128)(2,1)S(1)}, u32[]{:S(2)}, u32[]{:S(2)}) %collective-permute-start.18) | collective-permute-done | bytes 458784 | tf_op jit(solution)/shard_map/two_both/ppermute | solution.py:90
  71.2 1.5 gradients_here.1
  72.8 1.4 collective-permute-done.19.last_ref
  74.2 3.1 %gradients_there.1 = (bf16[256,448]{1,0:T(8,128)(2,1)S(1)}, bf16[256,448]{1,0:T(8,128)(2,1)S(1)}, bf16[2,256,896]{2,1,0:T(8,128)(2,1)S(1)}) custom-call(s32[4]{0:T(128)S(1)} %pad_add_fusion.3.at_ref, bf16[896,7168]{1,0:T(8,128)(2,1)S(1)} %pad_maximum_fusion.tokens_ref, bf16[256,448]{1,0:T(8,128)(2,1)S(1)} %get-tuple-element.470.here_a, ...), custom_call_target="tpu_custom_call" | custom-call | flops 300000000 | bytes 3000000 | tf_op jit(solution)/shard_map/gradients_there/pallas_call | solution.py:150
  77.7 1.8 %contract.7 = bf16[2,256,896]{2,1,0:T(8,128)(2,1)S(1)} custom-call(s32[3]{0:T(128)S(1)} %get-tuple-element.550.at_ref, bf16[896,7168]{1,0:T(8,128)(2,1)S(1)} %pad_maximum_fusion.tokens_ref, bf16[256,448]{1,0:T(8,128)(2,1)S(1)} %get-tuple-element.470.here_a, bf16[256,448]{1,0:T(8,128)(2,1)S(1)} %get-tuple-element.471.here_b, ...), custom_call_target="tpu_custom_call" | custom-call | flops 300000000 | bytes 3000000 | tf_op jit(solution)/shard_map/contract/pallas_call | solution.py:150
  79.7 1.8 %contract.8 = bf16[2,256,896]{2,1,0:T(8,128)(2,1)S(1)} custom-call(s32[3]{0:T(128)S(1)} %get-tuple-element.551.at_ref, bf16[896,7168]{1,0:T(8,128)(2,1)S(1)} %pad_maximum_fusion.tokens_ref, bf16[256,448]{1,0:T(8,128)(2,1)S(1)} %get-tuple-element.470.here_a, bf16[256,448]{1,0:T(8,128)(2,1)S(1)} %get-tuple-element.471.here_b, ...), custom_call_target="tpu_custom_call" | custom-call | flops 300000000 | bytes 3000000 | tf_op jit(solution)/shard_map/contract/pallas_call | solution.py:150
  81.6 1.3 collective-permute-start.22
  82.8 2.1 %contract.9 = f32[2,256,896]{2,1,0:T(8,128)S(1)} custom-call(s32[3]{0:T(128)S(1)} %get-tuple-element.552.at_ref, bf16[896,7168]{1,0:T(8,128)(2,1)S(1)} %pad_maximum_fusion.tokens_ref, bf16[256,448]{1,0:T(8,128)(2,1)S(1)} %get-tuple-element.470.here_a, bf16[256,448]{1,0:T(8,128)(2,1)S(1)} %get-tuple-element.471.here_b, ...), custom_call_target="tpu_custom_call" | custom-call | flops 300000000 | bytes 3000000 | tf_op jit(solution)/shard_map/contract/pallas_call | solution.py:150
  84.9 5.0 %collective-permute-done.20 = bf16[2,256,896]{2,1,0:T(8,128)(2,1)S(1)} collective-permute-done((bf16[2,256,896]{2,1,0:T(8,128)(2,1)S(1)}, bf16[2,256,896]{2,1,0:T(8,128)(2,1)S(1)}, u32[]{:S(2)}, u32[]{:S(2)}) %collective-permute-start.20) | collective-permute-done | bytes 917536 | tf_op jit(solution)/shard_map/seconds_3/ppermute | solution.py:90
  90.0 1.3 collective-permute-start.23
  91.3 1.8 %contract.10 = bf16[2,256,896]{2,1,0:T(8,128)(2,1)S(1)} custom-call(s32[3]{0:T(128)S(1)} %get-tuple-element.549.at_ref, bf16[896,7168]{1,0:T(8,128)(2,1)S(1)} %pad_maximum_fusion.tokens_ref, bf16[256,448]{1,0:T(8,128)(2,1)S(1)} %get-tuple-element.470.here_a, bf16[256,448]{1,0:T(8,128)(2,1)S(1)} %get-tuple-element.471.here_b, ...), custom_call_target="tpu_custom_call" | custom-call | flops 300000000 | bytes 3000000 | tf_op jit(solution)/shard_map/contract/pallas_call | solution.py:150
  93.1 1.8 %contract.11 = f32[2,256,896]{2,1,0:T(8,128)S(1)} custom-call(s32[3]{0:T(128)S(1)} %get-tuple-element.551.at_ref, bf16[896,7168]{1,0:T(8,128)(2,1)S(1)} %pad_maximum_fusion.tokens_ref, bf16[256,448]{1,0:T(8,128)(2,1)S(1)} %get-tuple-element.470.here_a, bf16[256,448]{1,0:T(8,128)(2,1)S(1)} %get-tuple-element.471.here_b, ...), custom_call_target="tpu_custom_call" | custom-call | flops 300000000 | bytes 3000000 | tf_op jit(solution)/shard_map/contract/pallas_call | solution.py:150
  95.0 1.8 %contract.12 = f32[2,256,896]{2,1,0:T(8,128)S(1)} custom-call(s32[3]{0:T(128)S(1)} %get-tuple-element.550.at_ref, bf16[896,7168]{1,0:T(8,128)(2,1)S(1)} %pad_maximum_fusion.tokens_ref, bf16[256,448]{1,0:T(8,128)(2,1)S(1)} %get-tuple-element.470.here_a, bf16[256,448]{1,0:T(8,128)(2,1)S(1)} %get-tuple-element.471.here_b, ...), custom_call_target="tpu_custom_call" | custom-call | flops 300000000 | bytes 3000000 | tf_op jit(solution)/shard_map/contract/pallas_call | solution.py:150
  96.8 1.8 %contract.13 = f32[2,256,896]{2,1,0:T(8,128)S(1)} custom-call(s32[3]{0:T(128)S(1)} %get-tuple-element.549.at_ref, bf16[896,7168]{1,0:T(8,128)(2,1)S(1)} %pad_maximum_fusion.tokens_ref, bf16[256,448]{1,0:T(8,128)(2,1)S(1)} %get-tuple-element.470.here_a, bf16[256,448]{1,0:T(8,128)(2,1)S(1)} %get-tuple-element.471.here_b, ...), custom_call_target="tpu_custom_call" | custom-call | flops 300000000 | bytes 3000000 | tf_op jit(solution)/shard_map/contract/pallas_call | solution.py:150
  99.8 2.9 %collective-permute-done.23 = bf16[256,896]{1,0:T(8,128)(2,1)S(1)} collective-permute-done((bf16[256,896]{1,0:T(8,128)(2,1)S(1)}, bf16[256,896]{1,0:T(8,128)(2,1)S(1)}, u32[]{:S(2)}, u32[]{:S(2)}) %collective-permute-start.23) | collective-permute-done | bytes 458784 | tf_op jit(solution)/shard_map/first_3/ppermute | solution.py:90
  102.9 1.8 %collective-permute-done.22 = bf16[2,256,896]{2,1,0:T(8,128)(2,1)S(1)} collective-permute-done((bf16[2,256,896]{2,1,0:T(8,128)(2,1)S(1)}, bf16[2,256,896]{2,1,0:T(8,128)(2,1)S(1)}, u32[]{:S(2)}, u32[]{:S(2)}) %collective-permute-start.22) | collective-permute-done | bytes 917536 | tf_op jit(solution)/shard_map/seconds_2/ppermute | solution.py:90
  104.8 1.3 collective-permute-start.26
  106.1 1.3 collective-permute-start.27
  107.8 4.7 %collective-permute-done.26 = bf16[256,896]{1,0:T(8,128)(2,1)S(1)} collective-permute-done((bf16[256,896]{1,0:T(8,128)(2,1)S(1)}, bf16[256,896]{1,0:T(8,128)(2,1)S(1)}, u32[]{:S(2)}, u32[]{:S(2)}) %collective-permute-start.26) | collective-permute-done | bytes 458784 | tf_op jit(solution)/shard_map/first_2/ppermute | solution.py:90
  112.5 5.7 %collective-permute-done.27 = bf16[256,896]{1,0:T(8,128)(2,1)S(1)} collective-permute-done((bf16[256,896]{1,0:T(8,128)(2,1)S(1)}, bf16[256,896]{1,0:T(8,128)(2,1)S(1)}, u32[]{:S(2)}, u32[]{:S(2)}) %collective-permute-start.27) | collective-permute-done | bytes 458784 | tf_op jit(solution)/shard_map/three_in/ppermute | solution.py:90
  118.3 1.3 collective-permute-start.29
  119.6 3.1 %collective-permute-start.28 = (bf16[256,896]{1,0:T(8,128)(2,1)S(1)}, bf16[256,896]{1,0:T(8,128)(2,1)S(1)}, u32[]{:S(2)}, u32[]{:S(2)}) collective-permute-start(bf16[256,896]{1,0:T(8,128)(2,1)S(1)} %fusion.64), channel_id=1, source_target_pairs={{4,8},{5,9},{6,10},{7,11},{8,4},{9,5},{10,6},{11,7},{20,24},{21,25... | collective-permute-start | bytes 1376264 | tf_op jit(solution)/shard_map/two/ppermute | solution.py:90
  122.8 6.4 %collective-permute-done.24 = bf16[2,256,896]{2,1,0:T(8,128)(2,1)S(1)} collective-permute-done((bf16[2,256,896]{2,1,0:T(8,128)(2,1)S(1)}, bf16[2,256,896]{2,1,0:T(8,128)(2,1)S(1)}, u32[]{:S(2)}, u32[]{:S(2)}) %collective-permute-start.24) | collective-permute-done | bytes 917536 | tf_op jit(solution)/shard_map/seconds_0/ppermute | solution.py:90
  131.0 3.2 %collective-permute-start.31 = (bf16[256,896]{1,0:T(8,128)(2,1)S(1)}, bf16[256,896]{1,0:T(8,128)(2,1)S(1)}, u32[]{:S(2)}, u32[]{:S(2)}) collective-permute-start(bf16[256,896]{1,0:T(8,128)(2,1)S(1)} %add_convert_fusion.2), channel_id=1, source_target_pairs={{4,8},{5,9},{6,10},{7,11},{8,4},{9,5},{10,6},{11,7},{20,24},{21,25... | collective-permute-start | bytes 1376264 | tf_op jit(solution)/shard_map/three/ppermute | solution.py:90
  134.3 2.7 %collective-permute-done.30.refs_1_ = bf16[256,896]{1,0:T(8,128)(2,1)S(1)} collective-permute-done((bf16[256,896]{1,0:T(8,128)(2,1)S(1)}, bf16[256,896]{1,0:T(8,128)(2,1)S(1)}, u32[]{:S(2)}, u32[]{:S(2)}) %collective-permute-start.30) | collective-permute-done | bytes 458784 | tf_op jit(solution)/shard_map/first_0/ppermute | solution.py:90
  137.0 2.4 %collective-permute-done.32.refs_3_ = bf16[256,896]{1,0:T(8,128)(2,1)S(1)} collective-permute-done((bf16[256,896]{1,0:T(8,128)(2,1)S(1)}, bf16[256,896]{1,0:T(8,128)(2,1)S(1)}, u32[]{:S(2)}, u32[]{:S(2)}) %collective-permute-start.32) | collective-permute-done | bytes 458784 | tf_op jit(solution)/shard_map/one/ppermute | solution.py:90
  139.3 2.0 %collective-permute-done.31.refs_2_ = bf16[256,896]{1,0:T(8,128)(2,1)S(1)} collective-permute-done((bf16[256,896]{1,0:T(8,128)(2,1)S(1)}, bf16[256,896]{1,0:T(8,128)(2,1)S(1)}, u32[]{:S(2)}, u32[]{:S(2)}) %collective-permute-start.31) | collective-permute-done | bytes 458784 | tf_op jit(solution)/shard_map/three/ppermute | solution.py:90
  141.4 1.3 by_rows.1
  142.7 4.7 %collective-permute-start.33 = (bf16[448,256]{1,0:T(8,128)(2,1)S(1)}, bf16[448,256]{1,0:T(8,128)(2,1)S(1)}, u32[]{:S(2)}, u32[]{:S(2)}) collective-permute-start(bf16[448,256]{1,0:T(8,128)(2,1)S(1)} %get-tuple-element.545), channel_id=1, source_target_pairs={{0,1},{1,0},{2,3},{3,2},{4,5},{5,4},{6,7},{7,6},{8,9},{9,8},{10,11... | collective-permute-start | bytes 688136 | tf_op jit(solution)/shard_map/taken/ppermute | solution.py:90
  147.4 1.0 collective-permute-done.33.taken_ref
  148.5 1.8 %finish.1 = (f32[448,256]{1,0:T(8,128)}, f32[448,256]{1,0:T(8,128)}, f32[448,256]{1,0:T(8,128)}) custom-call(s32[2]{0:T(128)S(1)} %pad_add_fusion.at_ref, f32[448,256]{1,0:T(8,128)S(1)} %get-tuple-element.544.kept_ref, bf16[448,256]{1,0:T(8,128)(2,1)S(1)} %collective-permute-done.33.taken_ref, bf16[448,512]{1,0:T(8,128)(2,1)S(1)} %copy-done.2, ...), custom_call_target="tpu_custom_call" | custom-call | flops 300000000 | bytes 3000000 | tf_op jit(solution)/shard_map/finish/pallas_call | solution.py:150
  (84 shorter events, 21.5 us)
Async XLA Ops:
  0.6 4.8 %copy-start = (bf16[448,512]{1,0:T(8,128)(2,1)S(1)}, bf16[448,512]{1,0:T(8,128)(2,1)}, u32[]{:S(2)}) copy-start(bf16[448,512]{1,0:T(8,128)(2,1)} %up_a.3) | copy-start | bytes 1376260
  0.6 3.7 %collective-permute-start = (bf16[448,512]{1,0:T(8,128)(2,1)}, bf16[448,512]{1,0:T(8,128)(2,1)S(1)}, u32[]{:S(2)}, u32[]{:S(2)}) collective-permute-start(bf16[448,512]{1,0:T(8,128)(2,1)} %weight_ref.1), channel_id=1, source_target_pairs={{0,1},{1,0},{2,3},{3,2},{4,5},{5,4},{6,7},{7,6},{8,9},{9,8},{10,11... | collective-permute-start | bytes 1376264 | tf_op jit(solution)/shard_map/other_weight/ppermute | solution.py:90
  1.4 2.9 %collective-permute-start.1 = (bf16[448,512]{1,0:T(8,128)(2,1)}, bf16[448,512]{1,0:T(8,128)(2,1)S(1)}, u32[]{:S(2)}, u32[]{:S(2)}) collective-permute-start(bf16[448,512]{1,0:T(8,128)(2,1)} %probe_ref.3), channel_id=1, source_target_pairs={{0,1},{1,0},{2,3},{3,2},{4,5},{5,4},{6,7},{7,6},{8,9},{9,8},{10,11... | collective-permute-start | bytes 1376264 | tf_op jit(solution)/shard_map/other_probe/ppermute | solution.py:90
  1.5 1.0 copy-start.1
  2.6 1.0 copy-start.6
  4.9 18.7 %collective-permute-start.2 = (bf16[448,7168]{1,0:T(8,128)(2,1)}, bf16[448,7168]{1,0:T(8,128)(2,1)}, u32[]{:S(2)}, u32[]{:S(2)}) collective-permute-start(bf16[448,7168]{1,0:T(8,128)(2,1)} %param.7), channel_id=1, source_target_pairs={{0,1},{1,0},{2,3},{3,2},{4,5},{5,4},{6,7},{7,6},{8,9},{9,8},{10,11... | collective-permute-start | bytes 19267592 | tf_op jit(solution)/shard_map/other_acts/ppermute | solution.py:90
  5.4 6.4 %collective-permute-start.5 = (bf16[448,512]{1,0:T(8,128)(2,1)S(1)}, bf16[448,512]{1,0:T(8,128)(2,1)S(1)}, u32[]{:S(2)}, u32[]{:S(2)}) collective-permute-start(bf16[448,512]{1,0:T(8,128)(2,1)S(1)} %copy-done), channel_id=1, source_target_pairs={{0,1},{1,0},{2,3},{3,2},{4,5},{5,4},{6,7},{7,6},{8,9},{9,8},{10,11... | collective-permute-start | bytes 1376264 | tf_op jit(solution)/shard_map/other_up/ppermute | solution.py:90
  5.5 13.6 %collective-permute-start.4 = (bf16[896,256]{1,0:T(8,128)(2,1)S(1)}, bf16[896,256]{1,0:T(8,128)(2,1)S(1)}, u32[]{:S(2)}, u32[]{:S(2)}) collective-permute-start(bf16[896,256]{1,0:T(8,128)(2,1)S(1)} %get-tuple-element.296), channel_id=1, source_target_pairs={{4,8},{5,9},{6,10},{7,11},{8,4},{9,5},{10,6},{11,7},{20,24},{21,25... | collective-permute-start | bytes 1376264 | tf_op jit(solution)/shard_map/near/ppermute | solution.py:90
  8.7 11.4 %collective-permute-start.3 = (bf16[896,256]{1,0:T(8,128)(2,1)S(1)}, bf16[896,256]{1,0:T(8,128)(2,1)S(1)}, u32[]{:S(2)}, u32[]{:S(2)}) collective-permute-start(bf16[896,256]{1,0:T(8,128)(2,1)S(1)} %get-tuple-element.296), channel_id=1, source_target_pairs={{0,4},{1,5},{2,6},{3,7},{4,0},{5,1},{6,2},{7,3},{8,12},{9,13},{10,... | collective-permute-start | bytes 1376264 | tf_op jit(solution)/shard_map/one/ppermute | solution.py:90
  8.8 14.8 %collective-permute-start.6 = (bf16[896,256]{1,0:T(8,128)(2,1)S(1)}, bf16[896,256]{1,0:T(8,128)(2,1)S(1)}, u32[]{:S(2)}, u32[]{:S(2)}) collective-permute-start(bf16[896,256]{1,0:T(8,128)(2,1)S(1)} %get-tuple-element.296), channel_id=1, source_target_pairs={{0,2},{1,3},{2,0},{3,1},{4,6},{5,7},{6,4},{7,5},{8,10},{9,11},{10,... | collective-permute-start | bytes 1376264 | tf_op jit(solution)/shard_map/across/ppermute | solution.py:90
  20.1 13.8 %collective-permute-start.8 = (bf16[896,256]{1,0:T(8,128)(2,1)S(1)}, bf16[896,256]{1,0:T(8,128)(2,1)S(1)}, u32[]{:S(2)}, u32[]{:S(2)}) collective-permute-start(bf16[896,256]{1,0:T(8,128)(2,1)S(1)} %collective-permute-done.3), channel_id=1, source_target_pairs={{4,8},{5,9},{6,10},{7,11},{8,4},{9,5},{10,6},{11,7},{20,24},{21,25... | collective-permute-start | bytes 1376264 | tf_op jit(solution)/shard_map/two_in/ppermute | solution.py:90
  22.3 11.7 %collective-permute-start.7 = (bf16[896,256]{1,0:T(8,128)(2,1)S(1)}, bf16[896,256]{1,0:T(8,128)(2,1)S(1)}, u32[]{:S(2)}, u32[]{:S(2)}) collective-permute-start(bf16[896,256]{1,0:T(8,128)(2,1)S(1)} %collective-permute-done.4), channel_id=1, source_target_pairs={{4,0},{5,1},{6,2},{7,3},{8,12},{9,13},{10,14},{11,15},{20,16},{21,... | collective-permute-start | bytes 1376264 | tf_op jit(solution)/shard_map/two_out/ppermute | solution.py:90
  23.7 13.3 %collective-permute-start.10 = (bf16[896,256]{1,0:T(8,128)(2,1)S(1)}, bf16[896,256]{1,0:T(8,128)(2,1)S(1)}, u32[]{:S(2)}, u32[]{:S(2)}) collective-permute-start(bf16[896,256]{1,0:T(8,128)(2,1)S(1)} %broadcast_select_fusion.1), channel_id=1, source_target_pairs={{0,2},{1,17},{2,0},{3,19},{4,6},{5,21},{6,4},{7,23},{8,10},{9,25},... | collective-permute-start | bytes 1376264 | tf_op jit(solution)/shard_map/corner/ppermute | solution.py:90
  25.0 12.0 %collective-permute-start.11 = (bf16[896,256]{1,0:T(8,128)(2,1)S(1)}, bf16[896,256]{1,0:T(8,128)(2,1)S(1)}, u32[]{:S(2)}, u32[]{:S(2)}) collective-permute-start(bf16[896,256]{1,0:T(8,128)(2,1)S(1)} %collective-permute-done.3), channel_id=1, source_target_pairs={{0,2},{1,17},{2,0},{3,19},{4,6},{5,21},{6,4},{7,23},{8,10},{9,25},... | collective-permute-start | bytes 1376264 | tf_op jit(solution)/shard_map/one_first/ppermute | solution.py:90
  34.8 9.3 %collective-permute-start.9 = (bf16[896,256]{1,0:T(8,128)(2,1)S(1)}, bf16[896,256]{1,0:T(8,128)(2,1)S(1)}, u32[]{:S(2)}, u32[]{:S(2)}) collective-permute-start(bf16[896,256]{1,0:T(8,128)(2,1)S(1)} %add.188), channel_id=1, source_target_pairs={{4,0},{5,1},{6,2},{7,3},{8,12},{9,13},{10,14},{11,15},{20,16},{21,... | collective-permute-start | bytes 1376264 | tf_op jit(solution)/shard_map/three_out/ppermute | solution.py:90
  37.0 20.0 %collective-permute-start.15 = (bf16[896,256]{1,0:T(8,128)(2,1)S(1)}, bf16[896,256]{1,0:T(8,128)(2,1)S(1)}, u32[]{:S(2)}, u32[]{:S(2)}) collective-permute-start(bf16[896,256]{1,0:T(8,128)(2,1)S(1)} %add.188), channel_id=1, source_target_pairs={{0,16},{1,3},{2,18},{3,1},{4,20},{5,7},{6,22},{7,5},{8,24},{9,11},... | collective-permute-start | bytes 1376264 | tf_op jit(solution)/shard_map/two_second/ppermute | solution.py:90
  37.3 9.6 %collective-permute-start.12 = (bf16[896,256]{1,0:T(8,128)(2,1)S(1)}, bf16[896,256]{1,0:T(8,128)(2,1)S(1)}, u32[]{:S(2)}, u32[]{:S(2)}) collective-permute-start(bf16[896,256]{1,0:T(8,128)(2,1)S(1)} %add.188), channel_id=1, source_target_pairs={{0,2},{1,17},{2,0},{3,19},{4,6},{5,21},{6,4},{7,23},{8,10},{9,25},... | collective-permute-start | bytes 1376264 | tf_op jit(solution)/shard_map/two_first/ppermute | solution.py:90
  39.2 15.4 %collective-permute-start.13 = (bf16[896,256]{1,0:T(8,128)(2,1)S(1)}, bf16[896,256]{1,0:T(8,128)(2,1)S(1)}, u32[]{:S(2)}, u32[]{:S(2)}) collective-permute-start(bf16[896,256]{1,0:T(8,128)(2,1)S(1)} %collective-permute-done.11), channel_id=1, source_target_pairs={{0,16},{1,3},{2,18},{3,1},{4,20},{5,7},{6,22},{7,5},{8,24},{9,11},... | collective-permute-start | bytes 1376264 | tf_op jit(solution)/shard_map/one_both/ppermute | solution.py:90
  44.2 26.3 %collective-permute-start.16 = (bf16[896,256]{1,0:T(8,128)(2,1)S(1)}, bf16[896,256]{1,0:T(8,128)(2,1)S(1)}, u32[]{:S(2)}, u32[]{:S(2)}) collective-permute-start(bf16[896,256]{1,0:T(8,128)(2,1)S(1)} %add.198), channel_id=1, source_target_pairs={{0,16},{1,3},{2,18},{3,1},{4,20},{5,7},{6,22},{7,5},{8,24},{9,11},... | collective-permute-start | bytes 1376264 | tf_op jit(solution)/shard_map/three_second/ppermute | solution.py:90
  44.6 13.0 %collective-permute-start.14 = (bf16[896,256]{1,0:T(8,128)(2,1)S(1)}, bf16[896,256]{1,0:T(8,128)(2,1)S(1)}, u32[]{:S(2)}, u32[]{:S(2)}) collective-permute-start(bf16[896,256]{1,0:T(8,128)(2,1)S(1)} %add.198), channel_id=1, source_target_pairs={{0,2},{1,17},{2,0},{3,19},{4,6},{5,21},{6,4},{7,23},{8,10},{9,25},... | collective-permute-start | bytes 1376264 | tf_op jit(solution)/shard_map/three_first/ppermute | solution.py:90
  46.9 23.0 %collective-permute-start.17 = (bf16[896,256]{1,0:T(8,128)(2,1)S(1)}, bf16[896,256]{1,0:T(8,128)(2,1)S(1)}, u32[]{:S(2)}, u32[]{:S(2)}) collective-permute-start(bf16[896,256]{1,0:T(8,128)(2,1)S(1)} %broadcast_select_fusion), channel_id=1, source_target_pairs={{0,4},{1,5},{2,6},{3,7},{4,0},{5,1},{6,2},{7,3},{8,12},{9,13},{10,... | collective-permute-start | bytes 1376264 | tf_op jit(solution)/shard_map/one_second/ppermute | solution.py:90
  55.3 13.9 %collective-permute-start.18 = (bf16[896,256]{1,0:T(8,128)(2,1)S(1)}, bf16[896,256]{1,0:T(8,128)(2,1)S(1)}, u32[]{:S(2)}, u32[]{:S(2)}) collective-permute-start(bf16[896,256]{1,0:T(8,128)(2,1)S(1)} %collective-permute-done.12), channel_id=1, source_target_pairs={{0,16},{1,3},{2,18},{3,1},{4,20},{5,7},{6,22},{7,5},{8,24},{9,11},... | collective-permute-start | bytes 1376264 | tf_op jit(solution)/shard_map/two_both/ppermute | solution.py:90
  57.6 16.5 %collective-permute-start.19 = (bf16[896,256]{1,0:T(8,128)(2,1)S(1)}, bf16[896,256]{1,0:T(8,128)(2,1)S(1)}, u32[]{:S(2)}, u32[]{:S(2)}) collective-permute-start(bf16[896,256]{1,0:T(8,128)(2,1)S(1)} %collective-permute-done.14), channel_id=1, source_target_pairs={{0,16},{1,3},{2,18},{3,1},{4,20},{5,7},{6,22},{7,5},{8,24},{9,11},... | collective-permute-start | bytes 1376264 | tf_op jit(solution)/shard_map/three_both/ppermute | solution.py:90
  70.6 0.7 copy-start.5
  77.3 12.6 %collective-permute-start.20 = (bf16[2,256,896]{2,1,0:T(8,128)(2,1)S(1)}, bf16[2,256,896]{2,1,0:T(8,128)(2,1)S(1)}, u32[]{:S(2)}, u32[]{:S(2)}) collective-permute-start(bf16[2,256,896]{2,1,0:T(8,128)(2,1)S(1)} %get-tuple-element.442), channel_id=1, source_target_pairs={{0,16},{1,3},{2,18},{3,1},{4,20},{5,7},{6,22},{7,5},{8,24},{9,11},... | collective-permute-start | bytes 2752520 | tf_op jit(solution)/shard_map/seconds_3/ppermute | solution.py:90
  79.6 20.0 %collective-permute-start.21 = (bf16[2,256,896]{2,1,0:T(8,128)(2,1)S(1)}, bf16[2,256,896]{2,1,0:T(8,128)(2,1)S(1)}, u32[]{:S(2)}, u32[]{:S(2)}) collective-permute-start(bf16[2,256,896]{2,1,0:T(8,128)(2,1)S(1)} %contract.7), channel_id=1, source_target_pairs={{0,4},{1,5},{2,6},{3,7},{4,0},{5,1},{6,2},{7,3},{8,12},{9,13},{10,... | collective-permute-start | bytes 2752520 | tf_op jit(solution)/shard_map/raw_1/ppermute | solution.py:90
  81.6 23.1 %collective-permute-start.22 = (bf16[2,256,896]{2,1,0:T(8,128)(2,1)S(1)}, bf16[2,256,896]{2,1,0:T(8,128)(2,1)S(1)}, u32[]{:S(2)}, u32[]{:S(2)}) collective-permute-start(bf16[2,256,896]{2,1,0:T(8,128)(2,1)S(1)} %contract.8), channel_id=1, source_target_pairs={{0,16},{1,3},{2,18},{3,1},{4,20},{5,7},{6,22},{7,5},{8,24},{9,11},... | collective-permute-start | bytes 2752520 | tf_op jit(solution)/shard_map/seconds_2/ppermute | solution.py:90
  90.0 12.7 %collective-permute-start.23 = (bf16[256,896]{1,0:T(8,128)(2,1)S(1)}, bf16[256,896]{1,0:T(8,128)(2,1)S(1)}, u32[]{:S(2)}, u32[]{:S(2)}) collective-permute-start(bf16[256,896]{1,0:T(8,128)(2,1)S(1)} %fusion.66), channel_id=1, source_target_pairs={{0,2},{1,17},{2,0},{3,19},{4,6},{5,21},{6,4},{7,23},{8,10},{9,25},... | collective-permute-start | bytes 1376264 | tf_op jit(solution)/shard_map/first_3/ppermute | solution.py:90
  104.8 7.7 %collective-permute-start.26 = (bf16[256,896]{1,0:T(8,128)(2,1)S(1)}, bf16[256,896]{1,0:T(8,128)(2,1)S(1)}, u32[]{:S(2)}, u32[]{:S(2)}) collective-permute-start(bf16[256,896]{1,0:T(8,128)(2,1)S(1)} %fusion.67), channel_id=1, source_target_pairs={{0,2},{1,17},{2,0},{3,19},{4,6},{5,21},{6,4},{7,23},{8,10},{9,25},... | collective-permute-start | bytes 1376264 | tf_op jit(solution)/shard_map/first_2/ppermute | solution.py:90
  106.1 12.1 %collective-permute-start.27 = (bf16[256,896]{1,0:T(8,128)(2,1)S(1)}, bf16[256,896]{1,0:T(8,128)(2,1)S(1)}, u32[]{:S(2)}, u32[]{:S(2)}) collective-permute-start(bf16[256,896]{1,0:T(8,128)(2,1)S(1)} %fusion.65), channel_id=1, source_target_pairs={{0,4},{1,5},{2,6},{3,7},{12,8},{13,9},{14,10},{15,11},{16,20},{17,... | collective-permute-start | bytes 1376264 | tf_op jit(solution)/shard_map/three_in/ppermute | solution.py:90
  107.4 21.8 %collective-permute-start.24 = (bf16[2,256,896]{2,1,0:T(8,128)(2,1)S(1)}, bf16[2,256,896]{2,1,0:T(8,128)(2,1)S(1)}, u32[]{:S(2)}, u32[]{:S(2)}) collective-permute-start(bf16[2,256,896]{2,1,0:T(8,128)(2,1)S(1)} %add_convert_fusion), channel_id=1, source_target_pairs={{0,16},{1,3},{2,18},{3,1},{4,20},{5,7},{6,22},{7,5},{8,24},{9,11},... | collective-permute-start | bytes 2752520 | tf_op jit(solution)/shard_map/seconds_0/ppermute | solution.py:90
  107.5 15.2 %collective-permute-start.25 = (bf16[256,896]{1,0:T(8,128)(2,1)S(1)}, bf16[256,896]{1,0:T(8,128)(2,1)S(1)}, u32[]{:S(2)}, u32[]{:S(2)}) collective-permute-start(bf16[256,896]{1,0:T(8,128)(2,1)S(1)} %fusion.69), channel_id=1, source_target_pairs={{0,2},{1,17},{2,0},{3,19},{4,6},{5,21},{6,4},{7,23},{8,10},{9,25},... | collective-permute-start | bytes 1376264 | tf_op jit(solution)/shard_map/first_1/ppermute | solution.py:90
  118.3 11.6 %collective-permute-start.29 = (bf16[256,896]{1,0:T(8,128)(2,1)S(1)}, bf16[256,896]{1,0:T(8,128)(2,1)S(1)}, u32[]{:S(2)}, u32[]{:S(2)}) collective-permute-start(bf16[256,896]{1,0:T(8,128)(2,1)S(1)} %fusion.64), channel_id=1, source_target_pairs={{0,4},{1,5},{2,6},{3,7},{12,8},{13,9},{14,10},{15,11},{16,20},{17,... | collective-permute-start | bytes 1376264 | tf_op jit(solution)/shard_map/two_in/ppermute | solution.py:90
  119.6 11.2 %collective-permute-start.28 = (bf16[256,896]{1,0:T(8,128)(2,1)S(1)}, bf16[256,896]{1,0:T(8,128)(2,1)S(1)}, u32[]{:S(2)}, u32[]{:S(2)}) collective-permute-start(bf16[256,896]{1,0:T(8,128)(2,1)S(1)} %fusion.64), channel_id=1, source_target_pairs={{4,8},{5,9},{6,10},{7,11},{8,4},{9,5},{10,6},{11,7},{20,24},{21,25... | collective-permute-start | bytes 1376264 | tf_op jit(solution)/shard_map/two/ppermute | solution.py:90
  129.3 7.7 %collective-permute-start.30 = (bf16[256,896]{1,0:T(8,128)(2,1)S(1)}, bf16[256,896]{1,0:T(8,128)(2,1)S(1)}, u32[]{:S(2)}, u32[]{:S(2)}) collective-permute-start(bf16[256,896]{1,0:T(8,128)(2,1)S(1)} %fusion.68), channel_id=1, source_target_pairs={{0,2},{1,17},{2,0},{3,19},{4,6},{5,21},{6,4},{7,23},{8,10},{9,25},... | collective-permute-start | bytes 1376264 | tf_op jit(solution)/shard_map/first_0/ppermute | solution.py:90
  130.9 17.6 %copy-start.2 = (bf16[448,512]{1,0:T(8,128)(2,1)S(1)}, bf16[448,512]{1,0:T(8,128)(2,1)}, u32[]{:S(2)}) copy-start(bf16[448,512]{1,0:T(8,128)(2,1)} %probe_ref.3) | copy-start | bytes 1376260
  130.9 17.6 %copy-start.3 = (f32[448,256]{1,0:T(8,128)S(1)}, f32[448,256]{1,0:T(8,128)}, u32[]{:S(2)}) copy-start(f32[448,256]{1,0:T(8,128)} %momentum_ref) | copy-start | bytes 1376260
  130.9 17.6 %copy-start.4 = (f32[448,256]{1,0:T(8,128)S(1)}, f32[448,256]{1,0:T(8,128)}, u32[]{:S(2)}) copy-start(f32[448,256]{1,0:T(8,128)} %curvature_ref.1) | copy-start | bytes 1376260
  130.9 8.4 %collective-permute-start.32 = (bf16[256,896]{1,0:T(8,128)(2,1)S(1)}, bf16[256,896]{1,0:T(8,128)(2,1)S(1)}, u32[]{:S(2)}, u32[]{:S(2)}) collective-permute-start(bf16[256,896]{1,0:T(8,128)(2,1)S(1)} %add_convert_fusion.1), channel_id=1, source_target_pairs={{0,4},{1,5},{2,6},{3,7},{4,0},{5,1},{6,2},{7,3},{8,12},{9,13},{10,... | collective-permute-start | bytes 1376264 | tf_op jit(solution)/shard_map/one/ppermute | solution.py:90
  131.0 10.4 %collective-permute-start.31 = (bf16[256,896]{1,0:T(8,128)(2,1)S(1)}, bf16[256,896]{1,0:T(8,128)(2,1)S(1)}, u32[]{:S(2)}, u32[]{:S(2)}) collective-permute-start(bf16[256,896]{1,0:T(8,128)(2,1)S(1)} %add_convert_fusion.2), channel_id=1, source_target_pairs={{4,8},{5,9},{6,10},{7,11},{8,4},{9,5},{10,6},{11,7},{20,24},{21,25... | collective-permute-start | bytes 1376264 | tf_op jit(solution)/shard_map/three/ppermute | solution.py:90
  142.7 5.8 %collective-permute-start.33 = (bf16[448,256]{1,0:T(8,128)(2,1)S(1)}, bf16[448,256]{1,0:T(8,128)(2,1)S(1)}, u32[]{:S(2)}, u32[]{:S(2)}) collective-permute-start(bf16[448,256]{1,0:T(8,128)(2,1)S(1)} %get-tuple-element.545), channel_id=1, source_target_pairs={{0,1},{1,0},{2,3},{3,2},{4,5},{5,4},{6,7},{7,6},{8,9},{9,8},{10,11... | collective-permute-start | bytes 688136 | tf_op jit(solution)/shard_map/taken/ppermute | solution.py:90

commit v7 on v6

--- a/solution.py
+++ b/solution.py
@@ -146,7 +146,7 @@
 SMEM = pl.BlockSpec(memory_space=pltpu.SMEM)
 
 
-def call(kernel, outs, scalars, *operands, name, cost=3 * 10**6, aliases=None):
+def call(kernel, outs, scalars, *operands, name, cost=10**6, aliases=None):
     return pl.pallas_call(
         kernel,
         out_shape=outs,

time: 151 us -> 151 us (level)
  no operation moved by 1% of the time
where the time goes in v7:
time: 151 us; the launch traced here: 150 us
  waiting for transfers between devices  68.1 us (45%)
  starting transfers between devices  38.2 us (25%)
  Pallas kernels  22.1 us (15%)
  matrix products  9.72 us (6%)
  other arithmetic  8.96 us (6%)
  local copies, waits for them, and re-layouts  2.12 us (1%)
    ppermute x34, waiting for transfers between devices, send(): return lax.ppermute(value, AXES, pairs_of(move))  68.1 us
    ppermute x34, starting transfers between devices, send(): return lax.ppermute(value, AXES, pairs_of(move))  38.2 us
    pallas_call x13, Pallas kernels, call(): pl.pallas_call(kernel, out_shape=outs, in_specs=[SMEM] + [VMEM] * len(ope...  22.1 us
    dot_general x15, matrix products, product(): jnp.dot(block_of(held, slot, flip_x), unit, preferred_element_type=jnp.fl...  9.72 us
    concatenate x1, other arithmetic, by_links(): jnp.concatenate([a, b], axis=0)  6.77 us
  transfers between devices with their start and end apart: 34, of which 20 were waited for; matrix products, arithmetic and copies ran while one was open for 12% of the time, Pallas kernels for 10%

profile of v7, /device:TPU:11, one launch (start us, length us, event | category | flops | bytes accessed | tf_op | source)
XLA Modules:
  0.0 150.3 jit_solution(10594373838072163495)
XLA Ops:
  1.5 1.0 copy-done
  5.5 3.2 %collective-permute-start.4 = (bf16[896,256]{1,0:T(8,128)(2,1)S(1)}, bf16[896,256]{1,0:T(8,128)(2,1)S(1)}, u32[]{:S(2)}, u32[]{:S(2)}) collective-permute-start(bf16[896,256]{1,0:T(8,128)(2,1)S(1)} %get-tuple-element.296), channel_id=1, source_target_pairs={{4,8},{5,9},{6,10},{7,11},{8,4},{9,5},{10,6},{11,7},{20,24},{21,25... | collective-permute-start | bytes 1376264 | tf_op jit(solution)/shard_map/near/ppermute | solution.py:90
  9.2 2.6 %collective-permute-done.5.up_b = bf16[448,512]{1,0:T(8,128)(2,1)S(1)} collective-permute-done((bf16[448,512]{1,0:T(8,128)(2,1)S(1)}, bf16[448,512]{1,0:T(8,128)(2,1)S(1)}, u32[]{:S(2)}, u32[]{:S(2)}) %collective-permute-start.5) | collective-permute-done | bytes 458784 | tf_op jit(solution)/shard_map/other_up/ppermute | solution.py:90
  11.8 7.3 %collective-permute-done.4 = bf16[896,256]{1,0:T(8,128)(2,1)S(1)} collective-permute-done((bf16[896,256]{1,0:T(8,128)(2,1)S(1)}, bf16[896,256]{1,0:T(8,128)(2,1)S(1)}, u32[]{:S(2)}, u32[]{:S(2)}) %collective-permute-start.4) | collective-permute-done | bytes 458784 | tf_op jit(solution)/shard_map/near/ppermute | solution.py:90
  19.1 1.1 collective-permute-done.3
  20.1 2.1 %collective-permute-start.8 = (bf16[896,256]{1,0:T(8,128)(2,1)S(1)}, bf16[896,256]{1,0:T(8,128)(2,1)S(1)}, u32[]{:S(2)}, u32[]{:S(2)}) collective-permute-start(bf16[896,256]{1,0:T(8,128)(2,1)S(1)} %collective-permute-done.3), channel_id=1, source_target_pairs={{4,8},{5,9},{6,10},{7,11},{8,4},{9,5},{10,6},{11,7},{20,24},{21,25... | collective-permute-start | bytes 1376264 | tf_op jit(solution)/shard_map/two_in/ppermute | solution.py:90
  22.3 1.3 collective-permute-start.7
  23.7 1.3 collective-permute-start.10
  25.2 6.8 %pad_maximum_fusion.tokens_ref = bf16[896,7168]{1,0:T(8,128)(2,1)S(1)} fusion(bf16[448,7168]{1,0:T(8,128)(2,1)} %collective-permute-done.2, bf16[448,7168]{1,0:T(8,128)(2,1)} %param.7), kind=kLoop, calls=%fused_computation | loop fusion | flops 25690112 | bytes 25690112 | tf_op jit(solution)/shard_map/concatenate | solution.py:361
  34.8 2.2 %collective-permute-start.9 = (bf16[896,256]{1,0:T(8,128)(2,1)S(1)}, bf16[896,256]{1,0:T(8,128)(2,1)S(1)}, u32[]{:S(2)}, u32[]{:S(2)}) collective-permute-start(bf16[896,256]{1,0:T(8,128)(2,1)S(1)} %add.188), channel_id=1, source_target_pairs={{4,0},{5,1},{6,2},{7,3},{8,12},{9,13},{10,14},{11,15},{20,16},{21,... | collective-permute-start | bytes 1376264 | tf_op jit(solution)/shard_map/three_out/ppermute | solution.py:90
  37.3 1.2 collective-permute-start.12
  39.2 1.3 collective-permute-start.13
  41.8 2.3 %collective-permute-done.9 = bf16[896,256]{1,0:T(8,128)(2,1)S(1)} collective-permute-done((bf16[896,256]{1,0:T(8,128)(2,1)S(1)}, bf16[896,256]{1,0:T(8,128)(2,1)S(1)}, u32[]{:S(2)}, u32[]{:S(2)}) %collective-permute-start.9) | collective-permute-done | bytes 458784 | tf_op jit(solution)/shard_map/three_out/ppermute | solution.py:90
  44.6 1.2 collective-permute-start.14
  46.9 1.3 collective-permute-start.17
  48.1 6.5 %collective-permute-done.13 = bf16[896,256]{1,0:T(8,128)(2,1)S(1)} collective-permute-done((bf16[896,256]{1,0:T(8,128)(2,1)S(1)}, bf16[896,256]{1,0:T(8,128)(2,1)S(1)}, u32[]{:S(2)}, u32[]{:S(2)}) %collective-permute-start.13) | collective-permute-done | bytes 458784 | tf_op jit(solution)/shard_map/one_both/ppermute | solution.py:90
  57.6 1.3 collective-permute-start.19
  59.5 9.7 %collective-permute-done.18 = bf16[896,256]{1,0:T(8,128)(2,1)S(1)} collective-permute-done((bf16[896,256]{1,0:T(8,128)(2,1)S(1)}, bf16[896,256]{1,0:T(8,128)(2,1)S(1)}, u32[]{:S(2)}, u32[]{:S(2)}) %collective-permute-start.18) | collective-permute-done | bytes 458784 | tf_op jit(solution)/shard_map/two_both/ppermute | solution.py:90
  71.2 1.5 gradients_here.1
  72.7 1.4 collective-permute-done.19.last_ref
  74.2 3.1 %gradients_there.1 = (bf16[256,448]{1,0:T(8,128)(2,1)S(1)}, bf16[256,448]{1,0:T(8,128)(2,1)S(1)}, bf16[2,256,896]{2,1,0:T(8,128)(2,1)S(1)}) custom-call(s32[4]{0:T(128)S(1)} %pad_add_fusion.3.at_ref, bf16[896,7168]{1,0:T(8,128)(2,1)S(1)} %pad_maximum_fusion.tokens_ref, bf16[256,448]{1,0:T(8,128)(2,1)S(1)} %get-tuple-element.470.here_a, ...), custom_call_target="tpu_custom_call" | custom-call | flops 100000000 | bytes 1000000 | tf_op jit(solution)/shard_map/gradients_there/pallas_call | solution.py:150
  77.7 1.8 %contract.7 = bf16[2,256,896]{2,1,0:T(8,128)(2,1)S(1)} custom-call(s32[3]{0:T(128)S(1)} %get-tuple-element.550.at_ref, bf16[896,7168]{1,0:T(8,128)(2,1)S(1)} %pad_maximum_fusion.tokens_ref, bf16[256,448]{1,0:T(8,128)(2,1)S(1)} %get-tuple-element.470.here_a, bf16[256,448]{1,0:T(8,128)(2,1)S(1)} %get-tuple-element.471.here_b, ...), custom_call_target="tpu_custom_call" | custom-call | flops 100000000 | bytes 1000000 | tf_op jit(solution)/shard_map/contract/pallas_call | solution.py:150
  79.7 1.8 %contract.8 = bf16[2,256,896]{2,1,0:T(8,128)(2,1)S(1)} custom-call(s32[3]{0:T(128)S(1)} %get-tuple-element.551.at_ref, bf16[896,7168]{1,0:T(8,128)(2,1)S(1)} %pad_maximum_fusion.tokens_ref, bf16[256,448]{1,0:T(8,128)(2,1)S(1)} %get-tuple-element.470.here_a, bf16[256,448]{1,0:T(8,128)(2,1)S(1)} %get-tuple-element.471.here_b, ...), custom_call_target="tpu_custom_call" | custom-call | flops 100000000 | bytes 1000000 | tf_op jit(solution)/shard_map/contract/pallas_call | solution.py:150
  81.6 1.3 collective-permute-start.22
  82.8 2.1 %contract.9 = f32[2,256,896]{2,1,0:T(8,128)S(1)} custom-call(s32[3]{0:T(128)S(1)} %get-tuple-element.552.at_ref, bf16[896,7168]{1,0:T(8,128)(2,1)S(1)} %pad_maximum_fusion.tokens_ref, bf16[256,448]{1,0:T(8,128)(2,1)S(1)} %get-tuple-element.470.here_a, bf16[256,448]{1,0:T(8,128)(2,1)S(1)} %get-tuple-element.471.here_b, ...), custom_call_target="tpu_custom_call" | custom-call | flops 100000000 | bytes 1000000 | tf_op jit(solution)/shard_map/contract/pallas_call | solution.py:150
  84.9 5.0 %collective-permute-done.20 = bf16[2,256,896]{2,1,0:T(8,128)(2,1)S(1)} collective-permute-done((bf16[2,256,896]{2,1,0:T(8,128)(2,1)S(1)}, bf16[2,256,896]{2,1,0:T(8,128)(2,1)S(1)}, u32[]{:S(2)}, u32[]{:S(2)}) %collective-permute-start.20) | collective-permute-done | bytes 917536 | tf_op jit(solution)/shard_map/seconds_3/ppermute | solution.py:90
  90.0 1.3 collective-permute-start.23
  91.3 1.8 %contract.10 = bf16[2,256,896]{2,1,0:T(8,128)(2,1)S(1)} custom-call(s32[3]{0:T(128)S(1)} %get-tuple-element.549.at_ref, bf16[896,7168]{1,0:T(8,128)(2,1)S(1)} %pad_maximum_fusion.tokens_ref, bf16[256,448]{1,0:T(8,128)(2,1)S(1)} %get-tuple-element.470.here_a, bf16[256,448]{1,0:T(8,128)(2,1)S(1)} %get-tuple-element.471.here_b, ...), custom_call_target="tpu_custom_call" | custom-call | flops 100000000 | bytes 1000000 | tf_op jit(solution)/shard_map/contract/pallas_call | solution.py:150
  93.1 1.8 %contract.11 = f32[2,256,896]{2,1,0:T(8,128)S(1)} custom-call(s32[3]{0:T(128)S(1)} %get-tuple-element.551.at_ref, bf16[896,7168]{1,0:T(8,128)(2,1)S(1)} %pad_maximum_fusion.tokens_ref, bf16[256,448]{1,0:T(8,128)(2,1)S(1)} %get-tuple-element.470.here_a, bf16[256,448]{1,0:T(8,128)(2,1)S(1)} %get-tuple-element.471.here_b, ...), custom_call_target="tpu_custom_call" | custom-call | flops 100000000 | bytes 1000000 | tf_op jit(solution)/shard_map/contract/pallas_call | solution.py:150
  95.0 1.8 %contract.12 = f32[2,256,896]{2,1,0:T(8,128)S(1)} custom-call(s32[3]{0:T(128)S(1)} %get-tuple-element.550.at_ref, bf16[896,7168]{1,0:T(8,128)(2,1)S(1)} %pad_maximum_fusion.tokens_ref, bf16[256,448]{1,0:T(8,128)(2,1)S(1)} %get-tuple-element.470.here_a, bf16[256,448]{1,0:T(8,128)(2,1)S(1)} %get-tuple-element.471.here_b, ...), custom_call_target="tpu_custom_call" | custom-call | flops 100000000 | bytes 1000000 | tf_op jit(solution)/shard_map/contract/pallas_call | solution.py:150
  96.8 1.8 %contract.13 = f32[2,256,896]{2,1,0:T(8,128)S(1)} custom-call(s32[3]{0:T(128)S(1)} %get-tuple-element.549.at_ref, bf16[896,7168]{1,0:T(8,128)(2,1)S(1)} %pad_maximum_fusion.tokens_ref, bf16[256,448]{1,0:T(8,128)(2,1)S(1)} %get-tuple-element.470.here_a, bf16[256,448]{1,0:T(8,128)(2,1)S(1)} %get-tuple-element.471.here_b, ...), custom_call_target="tpu_custom_call" | custom-call | flops 100000000 | bytes 1000000 | tf_op jit(solution)/shard_map/contract/pallas_call | solution.py:150
  99.8 2.9 %collective-permute-done.23 = bf16[256,896]{1,0:T(8,128)(2,1)S(1)} collective-permute-done((bf16[256,896]{1,0:T(8,128)(2,1)S(1)}, bf16[256,896]{1,0:T(8,128)(2,1)S(1)}, u32[]{:S(2)}, u32[]{:S(2)}) %collective-permute-start.23) | collective-permute-done | bytes 458784 | tf_op jit(solution)/shard_map/first_3/ppermute | solution.py:90
  102.9 1.8 %collective-permute-done.22 = bf16[2,256,896]{2,1,0:T(8,128)(2,1)S(1)} collective-permute-done((bf16[2,256,896]{2,1,0:T(8,128)(2,1)S(1)}, bf16[2,256,896]{2,1,0:T(8,128)(2,1)S(1)}, u32[]{:S(2)}, u32[]{:S(2)}) %collective-permute-start.22) | collective-permute-done | bytes 917536 | tf_op jit(solution)/shard_map/seconds_2/ppermute | solution.py:90
  104.8 1.3 collective-permute-start.26
  106.0 1.3 collective-permute-start.27
  107.8 4.7 %collective-permute-done.26 = bf16[256,896]{1,0:T(8,128)(2,1)S(1)} collective-permute-done((bf16[256,896]{1,0:T(8,128)(2,1)S(1)}, bf16[256,896]{1,0:T(8,128)(2,1)S(1)}, u32[]{:S(2)}, u32[]{:S(2)}) %collective-permute-start.26) | collective-permute-done | bytes 458784 | tf_op jit(solution)/shard_map/first_2/ppermute | solution.py:90
  112.4 5.7 %collective-permute-done.27 = bf16[256,896]{1,0:T(8,128)(2,1)S(1)} collective-permute-done((bf16[256,896]{1,0:T(8,128)(2,1)S(1)}, bf16[256,896]{1,0:T(8,128)(2,1)S(1)}, u32[]{:S(2)}, u32[]{:S(2)}) %collective-permute-start.27) | collective-permute-done | bytes 458784 | tf_op jit(solution)/shard_map/three_in/ppermute | solution.py:90
  118.3 1.3 collective-permute-start.29
  119.6 3.1 %collective-permute-start.28 = (bf16[256,896]{1,0:T(8,128)(2,1)S(1)}, bf16[256,896]{1,0:T(8,128)(2,1)S(1)}, u32[]{:S(2)}, u32[]{:S(2)}) collective-permute-start(bf16[256,896]{1,0:T(8,128)(2,1)S(1)} %fusion.64), channel_id=1, source_target_pairs={{4,8},{5,9},{6,10},{7,11},{8,4},{9,5},{10,6},{11,7},{20,24},{21,25... | collective-permute-start | bytes 1376264 | tf_op jit(solution)/shard_map/two/ppermute | solution.py:90
  122.8 6.4 %collective-permute-done.24 = bf16[2,256,896]{2,1,0:T(8,128)(2,1)S(1)} collective-permute-done((bf16[2,256,896]{2,1,0:T(8,128)(2,1)S(1)}, bf16[2,256,896]{2,1,0:T(8,128)(2,1)S(1)}, u32[]{:S(2)}, u32[]{:S(2)}) %collective-permute-start.24) | collective-permute-done | bytes 917536 | tf_op jit(solution)/shard_map/seconds_0/ppermute | solution.py:90
  131.0 3.2 %collective-permute-start.31 = (bf16[256,896]{1,0:T(8,128)(2,1)S(1)}, bf16[256,896]{1,0:T(8,128)(2,1)S(1)}, u32[]{:S(2)}, u32[]{:S(2)}) collective-permute-start(bf16[256,896]{1,0:T(8,128)(2,1)S(1)} %add_convert_fusion.2), channel_id=1, source_target_pairs={{4,8},{5,9},{6,10},{7,11},{8,4},{9,5},{10,6},{11,7},{20,24},{21,25... | collective-permute-start | bytes 1376264 | tf_op jit(solution)/shard_map/three/ppermute | solution.py:90
  134.3 2.7 %collective-permute-done.30.refs_1_ = bf16[256,896]{1,0:T(8,128)(2,1)S(1)} collective-permute-done((bf16[256,896]{1,0:T(8,128)(2,1)S(1)}, bf16[256,896]{1,0:T(8,128)(2,1)S(1)}, u32[]{:S(2)}, u32[]{:S(2)}) %collective-permute-start.30) | collective-permute-done | bytes 458784 | tf_op jit(solution)/shard_map/first_0/ppermute | solution.py:90
  137.0 2.4 %collective-permute-done.32.refs_3_ = bf16[256,896]{1,0:T(8,128)(2,1)S(1)} collective-permute-done((bf16[256,896]{1,0:T(8,128)(2,1)S(1)}, bf16[256,896]{1,0:T(8,128)(2,1)S(1)}, u32[]{:S(2)}, u32[]{:S(2)}) %collective-permute-start.32) | collective-permute-done | bytes 458784 | tf_op jit(solution)/shard_map/one/ppermute | solution.py:90
  139.3 2.0 %collective-permute-done.31.refs_2_ = bf16[256,896]{1,0:T(8,128)(2,1)S(1)} collective-permute-done((bf16[256,896]{1,0:T(8,128)(2,1)S(1)}, bf16[256,896]{1,0:T(8,128)(2,1)S(1)}, u32[]{:S(2)}, u32[]{:S(2)}) %collective-permute-start.31) | collective-permute-done | bytes 458784 | tf_op jit(solution)/shard_map/three/ppermute | solution.py:90
  141.4 1.3 by_rows.1
  142.7 4.7 %collective-permute-start.33 = (bf16[448,256]{1,0:T(8,128)(2,1)S(1)}, bf16[448,256]{1,0:T(8,128)(2,1)S(1)}, u32[]{:S(2)}, u32[]{:S(2)}) collective-permute-start(bf16[448,256]{1,0:T(8,128)(2,1)S(1)} %get-tuple-element.545), channel_id=1, source_target_pairs={{0,1},{1,0},{2,3},{3,2},{4,5},{5,4},{6,7},{7,6},{8,9},{9,8},{10,11... | collective-permute-start | bytes 688136 | tf_op jit(solution)/shard_map/taken/ppermute | solution.py:90
  147.4 1.0 collective-permute-done.33.taken_ref
  148.5 1.8 %finish.1 = (f32[448,256]{1,0:T(8,128)}, f32[448,256]{1,0:T(8,128)}, f32[448,256]{1,0:T(8,128)}) custom-call(s32[2]{0:T(128)S(1)} %pad_add_fusion.at_ref, f32[448,256]{1,0:T(8,128)S(1)} %get-tuple-element.544.kept_ref, bf16[448,256]{1,0:T(8,128)(2,1)S(1)} %collective-permute-done.33.taken_ref, bf16[448,512]{1,0:T(8,128)(2,1)S(1)} %copy-done.1, ...), custom_call_target="tpu_custom_call" | custom-call | flops 100000000 | bytes 1000000 | tf_op jit(solution)/shard_map/finish/pallas_call | solution.py:150
  (84 shorter events, 21.5 us)
Async XLA Ops:
  0.6 3.7 %collective-permute-start = (bf16[448,512]{1,0:T(8,128)(2,1)}, bf16[448,512]{1,0:T(8,128)(2,1)S(1)}, u32[]{:S(2)}, u32[]{:S(2)}) collective-permute-start(bf16[448,512]{1,0:T(8,128)(2,1)} %weight_ref.1), channel_id=1, source_target_pairs={{0,1},{1,0},{2,3},{3,2},{4,5},{5,4},{6,7},{7,6},{8,9},{9,8},{10,11... | collective-permute-start | bytes 1376264 | tf_op jit(solution)/shard_map/other_weight/ppermute | solution.py:90
  1.4 2.9 %collective-permute-start.1 = (bf16[448,512]{1,0:T(8,128)(2,1)}, bf16[448,512]{1,0:T(8,128)(2,1)S(1)}, u32[]{:S(2)}, u32[]{:S(2)}) collective-permute-start(bf16[448,512]{1,0:T(8,128)(2,1)} %probe_ref.3), channel_id=1, source_target_pairs={{0,1},{1,0},{2,3},{3,2},{4,5},{5,4},{6,7},{7,6},{8,9},{9,8},{10,11... | collective-permute-start | bytes 1376264 | tf_op jit(solution)/shard_map/other_probe/ppermute | solution.py:90
  1.5 1.0 copy-start
  2.5 1.0 copy-start.3
  3.6 1.9 %copy-start.2 = (bf16[448,512]{1,0:T(8,128)(2,1)S(1)}, bf16[448,512]{1,0:T(8,128)(2,1)}, u32[]{:S(2)}) copy-start(bf16[448,512]{1,0:T(8,128)(2,1)} %up_a.3) | copy-start | bytes 1376260
  4.9 18.7 %collective-permute-start.2 = (bf16[448,7168]{1,0:T(8,128)(2,1)}, bf16[448,7168]{1,0:T(8,128)(2,1)}, u32[]{:S(2)}, u32[]{:S(2)}) collective-permute-start(bf16[448,7168]{1,0:T(8,128)(2,1)} %param.7), channel_id=1, source_target_pairs={{0,1},{1,0},{2,3},{3,2},{4,5},{5,4},{6,7},{7,6},{8,9},{9,8},{10,11... | collective-permute-start | bytes 19267592 | tf_op jit(solution)/shard_map/other_acts/ppermute | solution.py:90
  5.4 6.4 %collective-permute-start.5 = (bf16[448,512]{1,0:T(8,128)(2,1)S(1)}, bf16[448,512]{1,0:T(8,128)(2,1)S(1)}, u32[]{:S(2)}, u32[]{:S(2)}) collective-permute-start(bf16[448,512]{1,0:T(8,128)(2,1)S(1)} %copy-done.2), channel_id=1, source_target_pairs={{0,1},{1,0},{2,3},{3,2},{4,5},{5,4},{6,7},{7,6},{8,9},{9,8},{10,11... | collective-permute-start | bytes 1376264 | tf_op jit(solution)/shard_map/other_up/ppermute | solution.py:90
  5.5 13.6 %collective-permute-start.4 = (bf16[896,256]{1,0:T(8,128)(2,1)S(1)}, bf16[896,256]{1,0:T(8,128)(2,1)S(1)}, u32[]{:S(2)}, u32[]{:S(2)}) collective-permute-start(bf16[896,256]{1,0:T(8,128)(2,1)S(1)} %get-tuple-element.296), channel_id=1, source_target_pairs={{4,8},{5,9},{6,10},{7,11},{8,4},{9,5},{10,6},{11,7},{20,24},{21,25... | collective-permute-start | bytes 1376264 | tf_op jit(solution)/shard_map/near/ppermute | solution.py:90
  8.7 11.4 %collective-permute-start.3 = (bf16[896,256]{1,0:T(8,128)(2,1)S(1)}, bf16[896,256]{1,0:T(8,128)(2,1)S(1)}, u32[]{:S(2)}, u32[]{:S(2)}) collective-permute-start(bf16[896,256]{1,0:T(8,128)(2,1)S(1)} %get-tuple-element.296), channel_id=1, source_target_pairs={{0,4},{1,5},{2,6},{3,7},{4,0},{5,1},{6,2},{7,3},{8,12},{9,13},{10,... | collective-permute-start | bytes 1376264 | tf_op jit(solution)/shard_map/one/ppermute | solution.py:90
  8.8 14.8 %collective-permute-start.6 = (bf16[896,256]{1,0:T(8,128)(2,1)S(1)}, bf16[896,256]{1,0:T(8,128)(2,1)S(1)}, u32[]{:S(2)}, u32[]{:S(2)}) collective-permute-start(bf16[896,256]{1,0:T(8,128)(2,1)S(1)} %get-tuple-element.296), channel_id=1, source_target_pairs={{0,2},{1,3},{2,0},{3,1},{4,6},{5,7},{6,4},{7,5},{8,10},{9,11},{10,... | collective-permute-start | bytes 1376264 | tf_op jit(solution)/shard_map/across/ppermute | solution.py:90
  20.1 13.8 %collective-permute-start.8 = (bf16[896,256]{1,0:T(8,128)(2,1)S(1)}, bf16[896,256]{1,0:T(8,128)(2,1)S(1)}, u32[]{:S(2)}, u32[]{:S(2)}) collective-permute-start(bf16[896,256]{1,0:T(8,128)(2,1)S(1)} %collective-permute-done.3), channel_id=1, source_target_pairs={{4,8},{5,9},{6,10},{7,11},{8,4},{9,5},{10,6},{11,7},{20,24},{21,25... | collective-permute-start | bytes 1376264 | tf_op jit(solution)/shard_map/two_in/ppermute | solution.py:90
  22.3 11.7 %collective-permute-start.7 = (bf16[896,256]{1,0:T(8,128)(2,1)S(1)}, bf16[896,256]{1,0:T(8,128)(2,1)S(1)}, u32[]{:S(2)}, u32[]{:S(2)}) collective-permute-start(bf16[896,256]{1,0:T(8,128)(2,1)S(1)} %collective-permute-done.4), channel_id=1, source_target_pairs={{4,0},{5,1},{6,2},{7,3},{8,12},{9,13},{10,14},{11,15},{20,16},{21,... | collective-permute-start | bytes 1376264 | tf_op jit(solution)/shard_map/two_out/ppermute | solution.py:90
  23.7 13.3 %collective-permute-start.10 = (bf16[896,256]{1,0:T(8,128)(2,1)S(1)}, bf16[896,256]{1,0:T(8,128)(2,1)S(1)}, u32[]{:S(2)}, u32[]{:S(2)}) collective-permute-start(bf16[896,256]{1,0:T(8,128)(2,1)S(1)} %broadcast_select_fusion.1), channel_id=1, source_target_pairs={{0,2},{1,17},{2,0},{3,19},{4,6},{5,21},{6,4},{7,23},{8,10},{9,25},... | collective-permute-start | bytes 1376264 | tf_op jit(solution)/shard_map/corner/ppermute | solution.py:90
  25.0 12.0 %collective-permute-start.11 = (bf16[896,256]{1,0:T(8,128)(2,1)S(1)}, bf16[896,256]{1,0:T(8,128)(2,1)S(1)}, u32[]{:S(2)}, u32[]{:S(2)}) collective-permute-start(bf16[896,256]{1,0:T(8,128)(2,1)S(1)} %collective-permute-done.3), channel_id=1, source_target_pairs={{0,2},{1,17},{2,0},{3,19},{4,6},{5,21},{6,4},{7,23},{8,10},{9,25},... | collective-permute-start | bytes 1376264 | tf_op jit(solution)/shard_map/one_first/ppermute | solution.py:90
  34.8 9.3 %collective-permute-start.9 = (bf16[896,256]{1,0:T(8,128)(2,1)S(1)}, bf16[896,256]{1,0:T(8,128)(2,1)S(1)}, u32[]{:S(2)}, u32[]{:S(2)}) collective-permute-start(bf16[896,256]{1,0:T(8,128)(2,1)S(1)} %add.188), channel_id=1, source_target_pairs={{4,0},{5,1},{6,2},{7,3},{8,12},{9,13},{10,14},{11,15},{20,16},{21,... | collective-permute-start | bytes 1376264 | tf_op jit(solution)/shard_map/three_out/ppermute | solution.py:90
  37.0 20.0 %collective-permute-start.15 = (bf16[896,256]{1,0:T(8,128)(2,1)S(1)}, bf16[896,256]{1,0:T(8,128)(2,1)S(1)}, u32[]{:S(2)}, u32[]{:S(2)}) collective-permute-start(bf16[896,256]{1,0:T(8,128)(2,1)S(1)} %add.188), channel_id=1, source_target_pairs={{0,16},{1,3},{2,18},{3,1},{4,20},{5,7},{6,22},{7,5},{8,24},{9,11},... | collective-permute-start | bytes 1376264 | tf_op jit(solution)/shard_map/two_second/ppermute | solution.py:90
  37.3 9.6 %collective-permute-start.12 = (bf16[896,256]{1,0:T(8,128)(2,1)S(1)}, bf16[896,256]{1,0:T(8,128)(2,1)S(1)}, u32[]{:S(2)}, u32[]{:S(2)}) collective-permute-start(bf16[896,256]{1,0:T(8,128)(2,1)S(1)} %add.188), channel_id=1, source_target_pairs={{0,2},{1,17},{2,0},{3,19},{4,6},{5,21},{6,4},{7,23},{8,10},{9,25},... | collective-permute-start | bytes 1376264 | tf_op jit(solution)/shard_map/two_first/ppermute | solution.py:90
  39.2 15.4 %collective-permute-start.13 = (bf16[896,256]{1,0:T(8,128)(2,1)S(1)}, bf16[896,256]{1,0:T(8,128)(2,1)S(1)}, u32[]{:S(2)}, u32[]{:S(2)}) collective-permute-start(bf16[896,256]{1,0:T(8,128)(2,1)S(1)} %collective-permute-done.11), channel_id=1, source_target_pairs={{0,16},{1,3},{2,18},{3,1},{4,20},{5,7},{6,22},{7,5},{8,24},{9,11},... | collective-permute-start | bytes 1376264 | tf_op jit(solution)/shard_map/one_both/ppermute | solution.py:90
  44.2 26.3 %collective-permute-start.16 = (bf16[896,256]{1,0:T(8,128)(2,1)S(1)}, bf16[896,256]{1,0:T(8,128)(2,1)S(1)}, u32[]{:S(2)}, u32[]{:S(2)}) collective-permute-start(bf16[896,256]{1,0:T(8,128)(2,1)S(1)} %add.198), channel_id=1, source_target_pairs={{0,16},{1,3},{2,18},{3,1},{4,20},{5,7},{6,22},{7,5},{8,24},{9,11},... | collective-permute-start | bytes 1376264 | tf_op jit(solution)/shard_map/three_second/ppermute | solution.py:90
  44.6 13.0 %collective-permute-start.14 = (bf16[896,256]{1,0:T(8,128)(2,1)S(1)}, bf16[896,256]{1,0:T(8,128)(2,1)S(1)}, u32[]{:S(2)}, u32[]{:S(2)}) collective-permute-start(bf16[896,256]{1,0:T(8,128)(2,1)S(1)} %add.198), channel_id=1, source_target_pairs={{0,2},{1,17},{2,0},{3,19},{4,6},{5,21},{6,4},{7,23},{8,10},{9,25},... | collective-permute-start | bytes 1376264 | tf_op jit(solution)/shard_map/three_first/ppermute | solution.py:90
  46.9 23.0 %collective-permute-start.17 = (bf16[896,256]{1,0:T(8,128)(2,1)S(1)}, bf16[896,256]{1,0:T(8,128)(2,1)S(1)}, u32[]{:S(2)}, u32[]{:S(2)}) collective-permute-start(bf16[896,256]{1,0:T(8,128)(2,1)S(1)} %broadcast_select_fusion), channel_id=1, source_target_pairs={{0,4},{1,5},{2,6},{3,7},{4,0},{5,1},{6,2},{7,3},{8,12},{9,13},{10,... | collective-permute-start | bytes 1376264 | tf_op jit(solution)/shard_map/one_second/ppermute | solution.py:90
  55.3 13.9 %collective-permute-start.18 = (bf16[896,256]{1,0:T(8,128)(2,1)S(1)}, bf16[896,256]{1,0:T(8,128)(2,1)S(1)}, u32[]{:S(2)}, u32[]{:S(2)}) collective-permute-start(bf16[896,256]{1,0:T(8,128)(2,1)S(1)} %collective-permute-done.12), channel_id=1, source_target_pairs={{0,16},{1,3},{2,18},{3,1},{4,20},{5,7},{6,22},{7,5},{8,24},{9,11},... | collective-permute-start | bytes 1376264 | tf_op jit(solution)/shard_map/two_both/ppermute | solution.py:90
  57.6 16.5 %collective-permute-start.19 = (bf16[896,256]{1,0:T(8,128)(2,1)S(1)}, bf16[896,256]{1,0:T(8,128)(2,1)S(1)}, u32[]{:S(2)}, u32[]{:S(2)}) collective-permute-start(bf16[896,256]{1,0:T(8,128)(2,1)S(1)} %collective-permute-done.14), channel_id=1, source_target_pairs={{0,16},{1,3},{2,18},{3,1},{4,20},{5,7},{6,22},{7,5},{8,24},{9,11},... | collective-permute-start | bytes 1376264 | tf_op jit(solution)/shard_map/three_both/ppermute | solution.py:90
  70.6 0.7 copy-start.6
  77.3 12.6 %collective-permute-start.20 = (bf16[2,256,896]{2,1,0:T(8,128)(2,1)S(1)}, bf16[2,256,896]{2,1,0:T(8,128)(2,1)S(1)}, u32[]{:S(2)}, u32[]{:S(2)}) collective-permute-start(bf16[2,256,896]{2,1,0:T(8,128)(2,1)S(1)} %get-tuple-element.442), channel_id=1, source_target_pairs={{0,16},{1,3},{2,18},{3,1},{4,20},{5,7},{6,22},{7,5},{8,24},{9,11},... | collective-permute-start | bytes 2752520 | tf_op jit(solution)/shard_map/seconds_3/ppermute | solution.py:90
  79.6 20.0 %collective-permute-start.21 = (bf16[2,256,896]{2,1,0:T(8,128)(2,1)S(1)}, bf16[2,256,896]{2,1,0:T(8,128)(2,1)S(1)}, u32[]{:S(2)}, u32[]{:S(2)}) collective-permute-start(bf16[2,256,896]{2,1,0:T(8,128)(2,1)S(1)} %contract.7), channel_id=1, source_target_pairs={{0,4},{1,5},{2,6},{3,7},{4,0},{5,1},{6,2},{7,3},{8,12},{9,13},{10,... | collective-permute-start | bytes 2752520 | tf_op jit(solution)/shard_map/raw_1/ppermute | solution.py:90
  81.6 23.1 %collective-permute-start.22 = (bf16[2,256,896]{2,1,0:T(8,128)(2,1)S(1)}, bf16[2,256,896]{2,1,0:T(8,128)(2,1)S(1)}, u32[]{:S(2)}, u32[]{:S(2)}) collective-permute-start(bf16[2,256,896]{2,1,0:T(8,128)(2,1)S(1)} %contract.8), channel_id=1, source_target_pairs={{0,16},{1,3},{2,18},{3,1},{4,20},{5,7},{6,22},{7,5},{8,24},{9,11},... | collective-permute-start | bytes 2752520 | tf_op jit(solution)/shard_map/seconds_2/ppermute | solution.py:90
  90.0 12.7 %collective-permute-start.23 = (bf16[256,896]{1,0:T(8,128)(2,1)S(1)}, bf16[256,896]{1,0:T(8,128)(2,1)S(1)}, u32[]{:S(2)}, u32[]{:S(2)}) collective-permute-start(bf16[256,896]{1,0:T(8,128)(2,1)S(1)} %fusion.66), channel_id=1, source_target_pairs={{0,2},{1,17},{2,0},{3,19},{4,6},{5,21},{6,4},{7,23},{8,10},{9,25},... | collective-permute-start | bytes 1376264 | tf_op jit(solution)/shard_map/first_3/ppermute | solution.py:90
  104.8 7.7 %collective-permute-start.26 = (bf16[256,896]{1,0:T(8,128)(2,1)S(1)}, bf16[256,896]{1,0:T(8,128)(2,1)S(1)}, u32[]{:S(2)}, u32[]{:S(2)}) collective-permute-start(bf16[256,896]{1,0:T(8,128)(2,1)S(1)} %fusion.67), channel_id=1, source_target_pairs={{0,2},{1,17},{2,0},{3,19},{4,6},{5,21},{6,4},{7,23},{8,10},{9,25},... | collective-permute-start | bytes 1376264 | tf_op jit(solution)/shard_map/first_2/ppermute | solution.py:90
  106.0 12.1 %collective-permute-start.27 = (bf16[256,896]{1,0:T(8,128)(2,1)S(1)}, bf16[256,896]{1,0:T(8,128)(2,1)S(1)}, u32[]{:S(2)}, u32[]{:S(2)}) collective-permute-start(bf16[256,896]{1,0:T(8,128)(2,1)S(1)} %fusion.65), channel_id=1, source_target_pairs={{0,4},{1,5},{2,6},{3,7},{12,8},{13,9},{14,10},{15,11},{16,20},{17,... | collective-permute-start | bytes 1376264 | tf_op jit(solution)/shard_map/three_in/ppermute | solution.py:90
  107.4 21.8 %collective-permute-start.24 = (bf16[2,256,896]{2,1,0:T(8,128)(2,1)S(1)}, bf16[2,256,896]{2,1,0:T(8,128)(2,1)S(1)}, u32[]{:S(2)}, u32[]{:S(2)}) collective-permute-start(bf16[2,256,896]{2,1,0:T(8,128)(2,1)S(1)} %add_convert_fusion), channel_id=1, source_target_pairs={{0,16},{1,3},{2,18},{3,1},{4,20},{5,7},{6,22},{7,5},{8,24},{9,11},... | collective-permute-start | bytes 2752520 | tf_op jit(solution)/shard_map/seconds_0/ppermute | solution.py:90
  107.5 15.2 %collective-permute-start.25 = (bf16[256,896]{1,0:T(8,128)(2,1)S(1)}, bf16[256,896]{1,0:T(8,128)(2,1)S(1)}, u32[]{:S(2)}, u32[]{:S(2)}) collective-permute-start(bf16[256,896]{1,0:T(8,128)(2,1)S(1)} %fusion.69), channel_id=1, source_target_pairs={{0,2},{1,17},{2,0},{3,19},{4,6},{5,21},{6,4},{7,23},{8,10},{9,25},... | collective-permute-start | bytes 1376264 | tf_op jit(solution)/shard_map/first_1/ppermute | solution.py:90
  118.3 11.6 %collective-permute-start.29 = (bf16[256,896]{1,0:T(8,128)(2,1)S(1)}, bf16[256,896]{1,0:T(8,128)(2,1)S(1)}, u32[]{:S(2)}, u32[]{:S(2)}) collective-permute-start(bf16[256,896]{1,0:T(8,128)(2,1)S(1)} %fusion.64), channel_id=1, source_target_pairs={{0,4},{1,5},{2,6},{3,7},{12,8},{13,9},{14,10},{15,11},{16,20},{17,... | collective-permute-start | bytes 1376264 | tf_op jit(solution)/shard_map/two_in/ppermute | solution.py:90
  119.6 11.2 %collective-permute-start.28 = (bf16[256,896]{1,0:T(8,128)(2,1)S(1)}, bf16[256,896]{1,0:T(8,128)(2,1)S(1)}, u32[]{:S(2)}, u32[]{:S(2)}) collective-permute-start(bf16[256,896]{1,0:T(8,128)(2,1)S(1)} %fusion.64), channel_id=1, source_target_pairs={{4,8},{5,9},{6,10},{7,11},{8,4},{9,5},{10,6},{11,7},{20,24},{21,25... | collective-permute-start | bytes 1376264 | tf_op jit(solution)/shard_map/two/ppermute | solution.py:90
  129.3 7.7 %collective-permute-start.30 = (bf16[256,896]{1,0:T(8,128)(2,1)S(1)}, bf16[256,896]{1,0:T(8,128)(2,1)S(1)}, u32[]{:S(2)}, u32[]{:S(2)}) collective-permute-start(bf16[256,896]{1,0:T(8,128)(2,1)S(1)} %fusion.68), channel_id=1, source_target_pairs={{0,2},{1,17},{2,0},{3,19},{4,6},{5,21},{6,4},{7,23},{8,10},{9,25},... | collective-permute-start | bytes 1376264 | tf_op jit(solution)/shard_map/first_0/ppermute | solution.py:90
  130.9 17.6 %copy-start.1 = (bf16[448,512]{1,0:T(8,128)(2,1)S(1)}, bf16[448,512]{1,0:T(8,128)(2,1)}, u32[]{:S(2)}) copy-start(bf16[448,512]{1,0:T(8,128)(2,1)} %probe_ref.3) | copy-start | bytes 1376260
  130.9 17.6 %copy-start.4 = (f32[448,256]{1,0:T(8,128)S(1)}, f32[448,256]{1,0:T(8,128)}, u32[]{:S(2)}) copy-start(f32[448,256]{1,0:T(8,128)} %momentum_ref) | copy-start | bytes 1376260
  130.9 17.6 %copy-start.5 = (f32[448,256]{1,0:T(8,128)S(1)}, f32[448,256]{1,0:T(8,128)}, u32[]{:S(2)}) copy-start(f32[448,256]{1,0:T(8,128)} %curvature_ref.1) | copy-start | bytes 1376260
  130.9 8.4 %collective-permute-start.32 = (bf16[256,896]{1,0:T(8,128)(2,1)S(1)}, bf16[256,896]{1,0:T(8,128)(2,1)S(1)}, u32[]{:S(2)}, u32[]{:S(2)}) collective-permute-start(bf16[256,896]{1,0:T(8,128)(2,1)S(1)} %add_convert_fusion.1), channel_id=1, source_target_pairs={{0,4},{1,5},{2,6},{3,7},{4,0},{5,1},{6,2},{7,3},{8,12},{9,13},{10,... | collective-permute-start | bytes 1376264 | tf_op jit(solution)/shard_map/one/ppermute | solution.py:90
  131.0 10.4 %collective-permute-start.31 = (bf16[256,896]{1,0:T(8,128)(2,1)S(1)}, bf16[256,896]{1,0:T(8,128)(2,1)S(1)}, u32[]{:S(2)}, u32[]{:S(2)}) collective-permute-start(bf16[256,896]{1,0:T(8,128)(2,1)S(1)} %add_convert_fusion.2), channel_id=1, source_target_pairs={{4,8},{5,9},{6,10},{7,11},{8,4},{9,5},{10,6},{11,7},{20,24},{21,25... | collective-permute-start | bytes 1376264 | tf_op jit(solution)/shard_map/three/ppermute | solution.py:90
  142.7 5.8 %collective-permute-start.33 = (bf16[448,256]{1,0:T(8,128)(2,1)S(1)}, bf16[448,256]{1,0:T(8,128)(2,1)S(1)}, u32[]{:S(2)}, u32[]{:S(2)}) collective-permute-start(bf16[448,256]{1,0:T(8,128)(2,1)S(1)} %get-tuple-element.545), channel_id=1, source_target_pairs={{0,1},{1,0},{2,3},{3,2},{4,5},{5,4},{6,7},{7,6},{8,9},{9,8},{10,11... | collective-permute-start | bytes 688136 | tf_op jit(solution)/shard_map/taken/ppermute | solution.py:90
